TPU v7x, 512 devices: a whole 4x8x8 slice. The times are simulated.
512 devices in a mesh: row: 32 (over x_hi, y, core), col: 16 (over z, x_lo).
Axes of the slice: x: 4 (x_hi: 2, x_lo: 2; x = x_hi * 2 + x_lo), y: 8, z: 8, core: 2. Of those that a mesh axis runs over, the one named last changes fastest.
Arguments:
- amplitudes: float32 [8, 8192, 6144], P(None, 'row', 'col'), may hold values from -6 to 6
- integrals: float32 [8, 512, 6144], P(None, 'row', 'col'), may hold values from -0.078125 to 0.078125
- residual_in: float32 [8, 8192, 512], P(None, ('row', 'col')), may hold values from -3 to 3
- cd_count: int32 [8], replicated, may hold values from 3072 to 6144, as said below
Outputs:
- residual: float32 [8, 8192, 512], P(None, ('row', 'col'))
Inputs may be any that keep to these rules, and one draw needn't show every extreme that they name: Live contracted pairs of an irrep are the first cd_count of its 6144 slots; some irrep has all 6144 slots live in every draw.
All inputs are finite; a program needn't handle non-finite values.
Results may differ from a plain program's by a relative error of at most 0.0003.
Values sent between devices are 32-bit elements; how exact they have to be, the bound alone decides.
No kernel may reach another device: no remote copies, remote signals or barrier semaphores. Data moves between devices by JAX's collectives and lax.ppermute only.
A program may use at most 64 MiB of HBM per device.

v0:
```python
import jax
import jax.numpy as jnp
from jax import lax
from jax.sharding import PartitionSpec as P


def body(amplitudes, integrals, residual_in, cd_count):
    width = amplitudes.shape[2]
    offset = lax.axis_index("col") * width
    slots = lax.broadcasted_iota(jnp.int32, (1, 1, width), 2) + offset
    t_live = jnp.where(slots < cd_count[:, None, None], amplitudes, jnp.zeros_like(amplitudes))
    partial_sums = jnp.einsum(
        "hic,hac->hia",
        t_live,
        lax.all_gather(integrals, "row", axis=1, tiled=True),
        precision=lax.Precision.HIGHEST,
    )
    ladder = lax.psum_scatter(partial_sums, "col", scatter_dimension=1, tiled=True)
    return residual_in + ladder


def solution(mesh):
    in_specs = (P(None, "row", "col"), P(None, "row", "col"), P(None, ("row", "col"), None), P())
    out_specs = P(None, ("row", "col"), None)
    return jax.shard_map(body, mesh=mesh, in_specs=in_specs, out_specs=out_specs, check_vma=False)
```

profile of v0, /device:TPU:6, one launch (start us, length us, event | category | flops | bytes accessed | tf_op | source)
XLA Modules:
  0.0 234.0 jit_solution(12535401563487160352)
XLA Ops:
  6.5 0.0 all-gather.2.cloned.1.call-start
  6.5 0.7 all-gather.2.cloned.1.call-update
  7.3 0.0 reduce-scatter.2.cloned.1.call-start
  7.3 0.7 broadcast_compare_fusion
  8.0 105.4 %all-gather.2.cloned.1.call-done = f32[8,512,384]{2,1,0:T(8,128)} async-done(((f32[8,16,384]{2,1,0:T(8,128)}), f32[8,512,384]{2,1,0:T(8,128)}) %all-gather.2.cloned.1.call-update) | async-done | bytes 6291472 | tf_op jit(solution)/shard_map/all_gather | solution.py:15
  113.4 11.9 %fusion = f32[8,256,512]{2,1,0:T(8,128)} fusion(f32[8,512,384]{2,1,0:T(8,128)} %all-gather.2.cloned.1.call-done, f32[8,256,384]{2,1,0:T(8,128)} %param.4, pred[8,384]{1,0:T(8,128)(4,1)S(1)} %broadcast_compare_fusion), kind=kOutput, calls=%fused_computation | convolution fusion | flops 4832624640 | bytes 13634560 | tf_op jit(solution)/shard_map/hic,hac->hia/dot_general | solution.py:12
  125.3 0.0 copy-start
  125.3 0.0 reduce-scatter.2.cloned.1.call-update
  125.4 100.1 %reduce-scatter.2.cloned.1.call-done = f32[8,16,512]{2,1,0:T(8,128)} async-done(((f32[8,256,512]{2,1,0:T(8,128)}), f32[8,16,512]{2,1,0:T(8,128)}) %reduce-scatter.2.cloned.1.call-update) | async-done | bytes 262160 | tf_op jit(solution)/shard_map/reduce_scatter | solution.py:18
  225.5 0.0 copy-done
  225.5 1.7 add.18
  (1 shorter events, 0.0 us)
Async XLA Ops:
  6.5 106.9 %all-gather.2.cloned.1.call-start = ((), (), s32[]{:S(2)}) async-start(), calls=%async_computation.1 | async-start | bytes 6488064 | tf_op jit(solution)/shard_map/all_gather | solution.py:15
  7.3 218.2 %reduce-scatter.2.cloned.1.call-start = ((), (), s32[]{:S(2)}) async-start(), calls=%async_computation.2 | async-start | bytes 4456448 | tf_op jit(solution)/shard_map/reduce_scatter | solution.py:18
  125.3 100.2 %copy-start = (f32[8,16,512]{2,1,0:T(8,128)S(1)}, f32[8,16,512]{2,1,0:T(8,128)}, u32[]{:S(2)}) copy-start(f32[8,16,512]{2,1,0:T(8,128)} %param.6) | copy-start | bytes 786436
Sparse Core Ops, SparseCore 0:
  10.6 102.7 all-gather.1
  125.5 99.9 reduce-scatter.1
where the time goes:
time: 236 us; the launch traced here: 234 us
  waiting for transfers between devices  206 us (87%)
  between operations  13.4 us (6%)
  matrix products  11.9 us (5%)
  other arithmetic  2.42 us (1%)
    all_gather x1, waiting for transfers between devices, body(): lax.all_gather(integrals, 'row', axis=1, tiled=True)  105 us
    reduce_scatter x1, waiting for transfers between devices, body(): lax.psum_scatter(partial_sums, 'col', scatter_dimension=1, tiled=True)  100 us
    dot_general x1, matrix products, body(): jnp.einsum('hic,hac->hia', t_live, lax.all_gather(integrals, 'row', axis=...  11.9 us
  transfers between devices with their start and end apart: 2, of which 2 were waited for; matrix products, arithmetic and copies ran while one was open for 0% of the time, Pallas kernels for 0%

commit v1 on v0

v1 whole, which is shorter than its diff:
```python
import jax
import jax.numpy as jnp
from jax import lax
from jax.sharding import Mesh, PartitionSpec as P

LINE = ("xh", "core", "xl")


def body(amplitudes, integrals, residual_in, cd_count):
    width = amplitudes.shape[2]
    v = lax.all_to_all(integrals, LINE, 0, 0, tiled=True)
    v = lax.all_gather(v, "y", axis=0)
    t = lax.all_to_all(amplitudes, LINE, 0, 0, tiled=True)

    count = cd_count[lax.axis_index(LINE)]
    v = v.reshape(8, 2, 2, 2, 16, width)
    t = t.reshape(2, 2, 2, 256, width)
    slots = lax.broadcasted_iota(jnp.int32, (2, 1, width), 0) * width + lax.broadcasted_iota(jnp.int32, (2, 1, width), 2)
    slots = slots + lax.axis_index("z") * (2 * width)
    v = v.transpose(3, 1, 0, 2, 4, 5).reshape(2, 512, width)
    v = jnp.where(slots < count, v, jnp.zeros_like(v))
    t = t.transpose(2, 0, 1, 3, 4).reshape(2, 1024, width)
    sums = jnp.einsum("xic,xac->ia", t, v, precision=lax.Precision.HIGH)
    sums = sums.reshape(2, 2, 8, 2, 16, 512).transpose(2, 0, 1, 3, 4, 5).reshape(8, 8, 16, 512)
    mine = lax.psum_scatter(sums, "z", scatter_dimension=0)
    ladder = lax.all_to_all(mine, LINE, 0, 0, tiled=True)
    return residual_in + ladder


def solution(mesh):
    mesh = Mesh(mesh.devices.reshape(2, 8, 2, 8, 2), ("xh", "y", "core", "z", "xl"))
    row, col = ("xh", "y", "core"), ("z", "xl")
    in_specs = (P(None, row, col), P(None, row, col), P(None, row + col, None), P())
    return jax.shard_map(body, mesh=mesh, in_specs=in_specs, out_specs=P(None, row + col, None), check_vma=False)
```

time: 236 us -> 148 us (0.63)
  waiting for transfers between devices: 206 us -> 86.4 us
  blocking collectives: 0 us -> 25 us
  local copies, waits for them, and re-layouts: 0.01 us -> 10.9 us
  matrix products: 11.9 us -> 2.79 us
  starting transfers between devices: 0.04 us -> 5.83 us
    all_gather x1, waiting for transfers between devices: 105 us -> 6.81 us  [body(): v = lax.all_gather(v, 'y', axis=0)]
    reduce_scatter x1, waiting for transfers between devices: 100 us -> 44.6 us  [body(): mine = lax.psum_scatter(sums, 'z', scatter_dimension=0)]
    all_to_all x0 -> x1, waiting for transfers between devices: none -> 34.3 us  [body(): t = lax.all_to_all(amplitudes, LINE, 0, 0, tiled=True)]
    all_to_all x0 -> x2, blocking collectives: none -> 25 us  [the longest x1 14.6 us: body(): v = lax.all_to_all(integrals, LINE, 0, 0, tiled=True)]
    dot_general x1, matrix products: 11.9 us -> 2.79 us  [body(): sums = jnp.einsum('xic,xac->ia', t, v, precision=lax.Precision.HIGH)]
    all_to_all x0 -> x1, starting transfers between devices: none -> 5.79 us  [body(): t = lax.all_to_all(amplitudes, LINE, 0, 0, tiled=True)]
    transpose x0 -> x2, local copies, waits for them, and re-layouts: none -> 4.86 us  [the longest x1 3.25 us: body(): sums.reshape(2, 2, 8, 2, 16, 512).transpose(2, 0, 1, 3, 4, 5)]
  transfers between devices with their start and end apart: 2 -> 3, of which waited for: 2 -> 3; matrix products, arithmetic and copies ran while one was open for 0% -> 2% of each run, Pallas kernels for 0% -> 0%
where the time goes in v1:
time: 148 us; the launch traced here: 146 us
  waiting for transfers between devices  86.4 us (58%)
  blocking collectives  25 us (17%)
  between operations  13.5 us (9%)
  local copies, waits for them, and re-layouts  10.9 us (7%)
  starting transfers between devices  5.83 us (4%)
  matrix products  2.79 us (2%)
  other arithmetic  1.57 us (1%)
    reduce_scatter x1, waiting for transfers between devices, body(): mine = lax.psum_scatter(sums, 'z', scatter_dimension=0)  44.6 us
    all_to_all x1, waiting for transfers between devices, body(): t = lax.all_to_all(amplitudes, LINE, 0, 0, tiled=True)  34.3 us
    all_to_all x1, blocking collectives, body(): v = lax.all_to_all(integrals, LINE, 0, 0, tiled=True)  14.6 us
    all_to_all x1, blocking collectives, body(): ladder = lax.all_to_all(mine, LINE, 0, 0, tiled=True)  10.4 us
    all_gather x1, waiting for transfers between devices, body(): v = lax.all_gather(v, 'y', axis=0)  6.81 us
    all_to_all x1, starting transfers between devices, body(): t = lax.all_to_all(amplitudes, LINE, 0, 0, tiled=True)  5.79 us
    transpose x1, local copies, waits for them, and re-layouts, body(): sums.reshape(2, 2, 8, 2, 16, 512).transpose(2, 0, 1, 3, 4, 5)  3.25 us
  transfers between devices with their start and end apart: 3, of which 3 were waited for; matrix products, arithmetic and copies ran while one was open for 2% of the time, Pallas kernels for 0%

profile of v1, /device:TPU:6, one launch (start us, length us, event | category | flops | bytes accessed | tf_op | source)
XLA Modules:
  0.0 146.0 jit_solution(5319308882261863689)
XLA Ops:
  6.5 14.6 %all_to_all.15 = f32[8,16,384]{2,1,0:T(8,128)} all-to-all(f32[8,16,384]{2,1,0:T(8,128)} %param.5), channel_id=1, replica_groups=mesh['xh'=2,'y'=8,'core'=2,'z'=8,'xl'=2] {'xh','core','xl'}, dimensions={0} | all-to-all | bytes 393216 | tf_op jit(solution)/shard_map/all_to_all | solution.py:11
  21.1 0.0 copy-start.2
  21.2 5.8 %all-to-all-start.1 = ((f32[8,256,384]{2,1,0:T(8,128)}), f32[8,256,384]{2,1,0:T(8,128)S(1)}, u32[]{:S(2)}, u32[]{:S(2)}) async-start(f32[8,256,384]{2,1,0:T(8,128)} %param.4), calls=%async_computation.1 | async-start | bytes 6291456 | tf_op jit(solution)/shard_map/all_to_all | solution.py:13
  26.9 0.0 all-gather.3.cloned.1.call-start
  26.9 0.7 all-gather.3.cloned.1.call-update
  27.7 0.0 reduce-scatter.2.cloned.1.call-start
  27.7 0.0 copy-done.2
  27.7 0.6 dynamic_slice.3
  28.3 0.7 add_compare_fusion
  29.0 34.3 %all-to-all-done.1 = f32[8,256,384]{2,1,0:T(8,128)S(1)} async-done(((f32[8,256,384]{2,1,0:T(8,128)}), f32[8,256,384]{2,1,0:T(8,128)S(1)}, u32[]{:S(2)}, u32[]{:S(2)}) %all-to-all-start.1) | async-done | bytes 3145760 | tf_op jit(solution)/shard_map/all_to_all | solution.py:13
  63.3 1.9 %copy.16 = f32[2,2,2,256,384]{4,3,1,0,2:T(8,128)} copy(f32[2,2,2,256,384]{4,3,2,1,0:T(8,128)S(1)} %bitcast.21) | data formatting | bytes 6291456 | tf_op jit(solution)/shard_map/reshape | solution.py:17
  65.2 6.8 %all-gather.3.cloned.1.call-done = f32[64,16,384]{2,1,0:T(8,128)} async-done(((f32[8,16,384]{2,1,0:T(8,128)}), f32[64,16,384]{2,1,0:T(8,128)}) %all-gather.3.cloned.1.call-update) | async-done | bytes 1572880 | tf_op jit(solution)/shard_map/all_gather | solution.py:12
  72.0 1.6 %copy.15 = f32[2,2,8,2,16,384]{5,4,3,2,1,0:T(8,128)S(1)} copy(f32[2,2,8,2,16,384]{5,4,0,3,1,2:T(8,128)} %bitcast.25) | data formatting | bytes 3145728 | tf_op jit(solution)/shard_map/transpose | solution.py:20
  73.6 0.0 copy-start
  73.6 0.1 bitcast_select_fusion
  73.8 1.8 %copy-done = f32[2,2,2,256,384]{4,3,1,0,2:T(8,128)S(1)} copy-done((f32[2,2,2,256,384]{4,3,1,0,2:T(8,128)S(1)}, f32[2,2,2,256,384]{4,3,1,0,2:T(8,128)}, u32[]{:S(2)}) %copy-start) | copy-done | bytes 3145752
  75.5 2.8 %convolution_bitcast_fusion = f32[1024,512]{0,1:T(8,128)S(1)} fusion(f32[2,512,384]{2,1,0:T(8,128)S(1)} %bitcast_select_fusion, f32[2,1024,384]{2,1,0:T(8,128)S(1)} %bitcast.22), kind=kOutput, calls=%fused_computation | convolution fusion | flops 2415919104 | bytes 6815744 | tf_op jit(solution)/shard_map/xic,xac->ia/dot_general | solution.py:23
  78.3 1.8 %copy.17 = f32[1024,512]{1,0:T(8,128)} copy(f32[1024,512]{0,1:T(8,128)S(1)} %convolution_bitcast_fusion) | data formatting | bytes 4194304 | tf_op jit(solution)/shard_map/xic,xac->ia/dot_general | solution.py:23
  80.1 3.2 %copy.18 = f32[8,2,2,2,16,512]{5,4,3,2,1,0:T(8,128)} copy(f32[8,2,2,2,16,512]{5,4,3,0,2,1:T(8,128)} %bitcast.24) | data formatting | bytes 4194304 | tf_op jit(solution)/shard_map/transpose | solution.py:24
  83.4 0.0 copy-start.1
  83.4 0.0 reduce-scatter.2.cloned.1.call-update
  83.4 44.6 %reduce-scatter.2.cloned.1.call-done = f32[1,8,16,512]{3,2,1,0:T(8,128)} async-done(((f32[8,8,16,512]{3,2,1,0:T(8,128)}), f32[1,8,16,512]{3,2,1,0:T(8,128)}) %reduce-scatter.2.cloned.1.call-update) | async-done | bytes 262160 | tf_op jit(solution)/shard_map/reduce_scatter | solution.py:25
  128.0 10.4 %all_to_all.16 = f32[8,16,512]{2,1,0:T(8,128)S(1)} all-to-all(f32[8,16,512]{2,1,0:T(8,128)} %bitcast.26), channel_id=1, replica_groups=mesh['xh'=2,'y'=8,'core'=2,'z'=8,'xl'=2] {'xh','core','xl'}, dimensions={0} | all-to-all | bytes 524288 | tf_op jit(solution)/shard_map/all_to_all | solution.py:26
  138.4 0.0 copy-done.1
  138.4 0.7 add.39
  (1 shorter events, 0.0 us)
Async XLA Ops:
  21.1 6.6 %copy-start.2 = (s32[8]{0:T(128)S(1)}, s32[8]{0:T(128)}, u32[]{:S(2)}) copy-start(s32[8]{0:T(128)} %param.7) | copy-start | bytes 100
  21.2 42.2 %all-to-all-start.1 = ((f32[8,256,384]{2,1,0:T(8,128)}), f32[8,256,384]{2,1,0:T(8,128)S(1)}, u32[]{:S(2)}, u32[]{:S(2)}) async-start(f32[8,256,384]{2,1,0:T(8,128)} %param.4), calls=%async_computation.1 | async-start | bytes 6291456 | tf_op jit(solution)/shard_map/all_to_all | solution.py:13
  26.9 45.1 %all-gather.3.cloned.1.call-start = ((), (), s32[]{:S(2)}) async-start(), calls=%async_computation.5 | async-start | bytes 1769472 | tf_op jit(solution)/shard_map/all_gather | solution.py:12
  27.7 100.3 %reduce-scatter.2.cloned.1.call-start = ((), (), s32[]{:S(2)}) async-start(), calls=%async_computation.4 | async-start | bytes 2359296 | tf_op jit(solution)/shard_map/reduce_scatter | solution.py:25
  73.6 1.9 %copy-start = (f32[2,2,2,256,384]{4,3,1,0,2:T(8,128)S(1)}, f32[2,2,2,256,384]{4,3,1,0,2:T(8,128)}, u32[]{:S(2)}) copy-start(f32[2,2,2,256,384]{4,3,1,0,2:T(8,128)} %copy.16) | copy-start | bytes 9437188
  83.4 55.0 %copy-start.1 = (f32[8,16,512]{2,1,0:T(8,128)S(1)}, f32[8,16,512]{2,1,0:T(8,128)}, u32[]{:S(2)}) copy-start(f32[8,16,512]{2,1,0:T(8,128)} %param.6) | copy-start | bytes 786436
Sparse Core Ops, SparseCore 0:
  29.8 42.1 all-gather.2
  83.5 44.4 reduce-scatter.1

commit v2 on v1

v2 whole, which is shorter than its diff:
```python
import functools

import jax
import jax.numpy as jnp
from jax import lax
from jax.experimental import pallas as pl
from jax.experimental.pallas import tpu as pltpu
from jax.sharding import Mesh, PartitionSpec as P

LINE = ("xh", "core", "xl")
N_Z = N_Y = 8
N_LINE = 8
EARLY = (3, 4, 5)
LATE = (2, 6, 1, 7, 0)


def shift(x, axis, by, size):
    return lax.ppermute(x, axis, [(i, (i + by) % size) for i in range(size)])


def split(x):
    high = x.astype(jnp.bfloat16)
    return high, (x - high.astype(jnp.float32)).astype(jnp.bfloat16)


def product(t_high, t_low, v_high, v_low):
    dot = functools.partial(
        lax.dot_general, dimension_numbers=(((1,), (1,)), ((), ())), preferred_element_type=jnp.float32
    )
    return dot(t_high, v_high) + (dot(t_low, v_high) + dot(t_high, v_low))


def fill_t(t_refs, th, tl):
    rows, width = t_refs[0].shape[1:]
    for k, t_ref in enumerate(t_refs):
        for g in range(N_LINE):
            part, x = divmod(g, 2)
            high, low = split(t_ref[g])
            at = (slice((4 * k + part) * rows, (4 * k + part + 1) * rows), slice(x * width, (x + 1) * width))
            th[at] = high
            tl[at] = low


def early_kernel(meta, v_ref, t3, t4, t5, p3, p4a, p4b, p5, vh, vl, th, tl):
    rows, width = v_ref.shape[2:]
    slots = lax.broadcasted_iota(jnp.int32, (rows, width), 1)
    for y in range(N_Y):
        for g in range(N_LINE):
            part, x = divmod(g, 2)
            xh, core = divmod(part, 2)
            high, low = split(jnp.where(slots + x * width < meta[16], v_ref[y, g], 0.0))
            at = (slice(((xh * N_Y + y) * 2 + core) * rows, ((xh * N_Y + y) * 2 + core + 1) * rows), slice(x * width, (x + 1) * width))
            vh[at] = high
            vl[at] = low
    fill_t((t3, t4, t5), th, tl)
    sums = product(th[...], tl[...], vh[...], vl[...])
    chunk = p3.shape[0]
    p3[...] = sums[:chunk]
    p4a[...] = sums[chunk : chunk + chunk // 2]
    p4b[...] = sums[chunk + chunk // 2 : 2 * chunk]
    p5[...] = sums[2 * chunk :]


def late_kernel(meta, vh, vl, *refs):
    n = len(LATE)
    t_refs, p_refs, (th, tl) = refs[:n], refs[n : 2 * n], refs[2 * n :]
    fill_t(t_refs, th, tl)
    sums = product(th[...], tl[...], vh[...], vl[...])
    chunk = p_refs[0].shape[0]
    for k, p_ref in enumerate(p_refs):
        p_ref[...] = sums[k * chunk : (k + 1) * chunk]


def relay_kernel(first, own, came, half, out):
    out[...] = own[...] + came[...]
    rows = half.shape[0]
    at = slice(0, rows) if first else slice(rows, 2 * rows)
    out[at] += half[...]


def call(kernel, meta, arrays, specs, outs, scratch, flops):
    whole = lambda shape: pl.BlockSpec(shape, lambda i, m, n=len(shape): (0,) * n)
    return pl.pallas_call(
        kernel,
        out_shape=[jax.ShapeDtypeStruct(*o) for o in outs],
        grid_spec=pltpu.PrefetchScalarGridSpec(
            num_scalar_prefetch=1,
            grid=(1,),
            in_specs=[whole(a.shape) if s is None else s for a, s in zip(arrays, specs)],
            out_specs=[whole(o[0]) for o in outs],
            scratch_shapes=scratch,
        ),
        compiler_params=pltpu.CompilerParams(vmem_limit_bytes=32 << 20),
        cost_estimate=pl.CostEstimate(flops=flops, bytes_accessed=4 << 20, transcendentals=0),
    )(meta, *arrays)


def relay(first, own, came, half):
    return pl.pallas_call(
        functools.partial(relay_kernel, first),
        out_shape=jax.ShapeDtypeStruct(own.shape, own.dtype),
        cost_estimate=pl.CostEstimate(flops=own.size, bytes_accessed=own.size * 12, transcendentals=0),
    )(own, came, half)


def body(amplitudes, integrals, residual_in, cd_count):
    width = amplitudes.shape[2]
    y, z = lax.axis_index("y"), lax.axis_index("z")
    steps = jnp.arange(8, dtype=jnp.int32)
    live = cd_count[lax.axis_index(LINE)] - z * (2 * width)
    meta = jnp.concatenate([(z + steps) % N_Z, (y + steps) % N_Y, live[None]]).astype(jnp.int32)

    v = lax.all_to_all(integrals, LINE, 0, 0, tiled=True)
    v = lax.all_gather(v, "y", axis=0)
    t = lax.all_to_all(amplitudes, LINE, 0, 0, tiled=True)

    rows, outer = 32, 512
    chunk = 4 * rows
    f32, bf16 = jnp.float32, jnp.bfloat16
    t_spec = lambda k: pl.BlockSpec((N_LINE, rows, width), lambda i, m, k=k: (0, m[k], 0))
    t_halves = lambda n: [pltpu.VMEM((n * chunk, 2 * width), bf16)] * 2
    flops = 6 * chunk * 2 * width * outer
    p3, p4a, p4b, p5, vh, vl = call(
        early_kernel, meta, [v, t, t, t], [None] + [t_spec(k) for k in EARLY],
        [((chunk, outer), f32), ((chunk // 2, outer), f32), ((chunk // 2, outer), f32), ((chunk, outer), f32)]
        + [((outer, 2 * width), bf16)] * 2,
        t_halves(len(EARLY)), flops * len(EARLY),
    )
    r3 = shift(p3, "z", 1, N_Z)
    r5 = shift(p5, "z", -1, N_Z)
    r4a = shift(p4a, "z", 2, N_Z)
    r4b = shift(p4b, "z", -2, N_Z)
    p2, p6, p1, p7, p0 = call(
        late_kernel, meta, [vh, vl] + [t] * len(LATE), [None, None] + [t_spec(k) for k in LATE],
        [((chunk, outer), f32)] * len(LATE), t_halves(len(LATE)), flops * len(LATE),
    )
    d1 = shift(p1, "z", 1, N_Z)
    d7 = shift(p7, "z", -1, N_Z)
    d2 = shift(relay(True, p2, r3, r4a), "z", 2, N_Z)
    d6 = shift(relay(False, p6, r5, r4b), "z", -2, N_Z)
    mine = p0 + d1 + d7 + d2 + d6
    ladder = lax.all_to_all(mine.reshape(N_LINE, 16, outer), LINE, 0, 0, tiled=True)
    return residual_in + ladder


def solution(mesh):
    mesh = Mesh(mesh.devices.reshape(2, 8, 2, 8, 2), ("xh", "y", "core", "z", "xl"))
    row, col = ("xh", "y", "core"), ("z", "xl")
    in_specs = (P(None, row, col), P(None, row, col), P(None, row + col, None), P())
    return jax.shard_map(body, mesh=mesh, in_specs=in_specs, out_specs=P(None, row + col, None), check_vma=False)
```

time: 148 us -> 145 us (0.980)
  waiting for transfers between devices: 86.4 us -> 52.5 us
  starting transfers between devices: 5.83 us -> 36.6 us
  Pallas kernels: 0 us -> 9.05 us
  local copies, waits for them, and re-layouts: 10.9 us -> 4.1 us
  matrix products: 2.79 us -> 0 us
    reduce_scatter x1 -> x0, waiting for transfers between devices: 44.6 us -> none  [body(): mine = lax.psum_scatter(sums, 'z', scatter_dimension=0)]
    ppermute x0 -> x8, starting transfers between devices: none -> 30.8 us  [shift(): return lax.ppermute(x, axis, [(i, (i + by) % size) for i in range(size)])]
    pallas_call x0 -> x4, Pallas kernels: none -> 9.05 us  [the longest x2 5.46 us: call(): pl.pallas_call(kernel, out_shape=[jax.ShapeDtypeStruct(*o) for o in outs]...]
    ppermute x0 -> x8, waiting for transfers between devices: none -> 8.85 us  [shift(): return lax.ppermute(x, axis, [(i, (i + by) % size) for i in range(size)])]
    transpose x2 -> x0, local copies, waits for them, and re-layouts: 4.86 us -> none  [the longest x1 3.25 us: body(): sums.reshape(2, 2, 8, 2, 16, 512).transpose(2, 0, 1, 3, 4, 5)]
    dot_general x1 -> x0, matrix products: 2.79 us -> none  [body(): sums = jnp.einsum('xic,xac->ia', t, v, precision=lax.Precision.HIGH)]
    reshape x1 -> x0, local copies, waits for them, and re-layouts: 1.86 us -> none  [body(): t = t.reshape(2, 2, 2, 256, width)]
    all_gather x1, waiting for transfers between devices: 6.81 us -> 8.67 us  [body(): v = lax.all_gather(v, 'y', axis=0)]
  transfers between devices with their start and end apart: 3 -> 10, of which waited for: 3 -> 4; matrix products, arithmetic and copies ran while one was open for 2% -> 0% of each run, Pallas kernels for 0% -> 5%
where the time goes in v2:
time: 145 us; the launch traced here: 142 us
  waiting for transfers between devices  52.5 us (36%)
  starting transfers between devices  36.6 us (25%)
  blocking collectives  24.7 us (17%)
  between operations  14.2 us (10%)
  Pallas kernels  9.05 us (6%)
  local copies, waits for them, and re-layouts  4.1 us (3%)
    all_to_all x1, waiting for transfers between devices, body(): t = lax.all_to_all(amplitudes, LINE, 0, 0, tiled=True)  34.3 us
    ppermute x8, starting transfers between devices, shift(): return lax.ppermute(x, axis, [(i, (i + by) % size) for i in range(size)])  30.8 us
    all_to_all x1, blocking collectives, body(): v = lax.all_to_all(integrals, LINE, 0, 0, tiled=True)  14.6 us
    all_to_all x1, blocking collectives, body(): lax.all_to_all(mine.reshape(N_LINE, 16, outer), LINE, 0, 0, tiled=True)  10.1 us
    ppermute x8, waiting for transfers between devices, shift(): return lax.ppermute(x, axis, [(i, (i + by) % size) for i in range(size)])  8.85 us
    all_gather x1, waiting for transfers between devices, body(): v = lax.all_gather(v, 'y', axis=0)  8.67 us
    all_to_all x1, starting transfers between devices, body(): t = lax.all_to_all(amplitudes, LINE, 0, 0, tiled=True)  5.79 us
    pallas_call x2, Pallas kernels, call(): pl.pallas_call(kernel, out_shape=[jax.ShapeDtypeStruct(*o) for o in outs]...  5.46 us
  transfers between devices with their start and end apart: 10, of which 4 were waited for; matrix products, arithmetic and copies ran while one was open for 0% of the time, Pallas kernels for 5%

profile of v2, /device:TPU:6, one launch (start us, length us, event | category | flops | bytes accessed | tf_op | source)
XLA Modules:
  0.0 142.1 jit_solution(3697441312783513194)
XLA Ops:
  6.5 14.6 %all_to_all.15 = f32[8,16,384]{2,1,0:T(8,128)} all-to-all(f32[8,16,384]{2,1,0:T(8,128)} %param.5), channel_id=1, replica_groups=mesh['xh'=2,'y'=8,'core'=2,'z'=8,'xl'=2] {'xh','core','xl'}, dimensions={0} | all-to-all | bytes 393216 | tf_op jit(solution)/shard_map/all_to_all | solution.py:113
  21.2 5.8 %all-to-all-start.1 = ((f32[8,256,384]{2,1,0:T(8,128)}), f32[8,256,384]{2,1,0:T(8,128)S(1)}, u32[]{:S(2)}, u32[]{:S(2)}) async-start(f32[8,256,384]{2,1,0:T(8,128)} %param.4), calls=%async_computation.1 | async-start | bytes 6291456 | tf_op jit(solution)/shard_map/all_to_all | solution.py:115
  26.9 0.7 all-gather.3.cloned.1.call-update
  27.7 0.6 dynamic_slice.3
  29.0 0.1 pad_add_fusion.meta
  29.0 34.3 %all-to-all-done.1.t3.t4.t5.refs_0_.refs_1_.refs_2_.refs_3_.refs_4_ = f32[8,256,384]{2,1,0:T(8,128)S(1)} async-done(((f32[8,256,384]{2,1,0:T(8,128)}), f32[8,256,384]{2,1,0:T(8,128)S(1)}, u32[]{:S(2)}, u32[]{:S(2)}) %all-to-all-start.1) | async-done | bytes 3145760 | tf_op jit(solution)/shard_map/all_to_all | solution.py:115
  63.3 8.7 %all-gather.3.cloned.1.call-done = f32[64,16,384]{2,1,0:T(8,128)} async-done(((f32[8,16,384]{2,1,0:T(8,128)}), f32[64,16,384]{2,1,0:T(8,128)}) %all-gather.3.cloned.1.call-update) | async-done | bytes 1572880 | tf_op jit(solution)/shard_map/all_gather | solution.py:114
  72.0 1.4 copy-done
  73.4 2.4 %shard_map.46 = (f32[128,512]{1,0:T(8,128)S(1)}, f32[64,512]{1,0:T(8,128)S(1)}, f32[64,512]{1,0:T(8,128)S(1)}, f32[128,512]{1,0:T(8,128)}, bf16[512,768]{1,0:T(8,128)(2,1)S(1)}, /*index=5*/bf16[512,768]{1,0:T(8,128)(2,1)S(1)}) custom-call(s32[17]{0:T(128)S(1)} %pad_add_fusion.meta, f32[8,8,16,384]{3,2,1,0:T(8,128)S(1)} %bitcast.4, ...), custom_call_target="tpu_custom_call" | custom-call | flops 905969664 | bytes 4194304 | tf_op jit(solution)/shard_map/pallas_call | solution.py:83
  75.9 3.5 %collective-permute-start.2 = (f32[128,512]{1,0:T(8,128)S(1)}, f32[128,512]{1,0:T(8,128)S(1)}, u32[]{:S(2)}, u32[]{:S(2)}) collective-permute-start(f32[128,512]{1,0:T(8,128)S(1)} %get-tuple-element.22), channel_id=1, source_target_pairs={{0,2},{2,4},{4,6},{6,8},{8,10},{10,12},{12,14},{14,0},{1,3},{3,5},... | collective-permute-start | bytes 786440 | tf_op jit(solution)/shard_map/ppermute | solution.py:18
  79.4 4.2 %collective-permute-start.5 = (f32[128,512]{1,0:T(8,128)}, f32[128,512]{1,0:T(8,128)}, u32[]{:S(2)}, u32[]{:S(2)}) collective-permute-start(f32[128,512]{1,0:T(8,128)} %get-tuple-element.25), channel_id=1, source_target_pairs={{0,14},{2,0},{4,2},{6,4},{8,6},{10,8},{12,10},{14,12},{1,15},{3,1}... | collective-permute-start | bytes 786440 | tf_op jit(solution)/shard_map/ppermute | solution.py:18
  83.6 2.7 %collective-permute-start.3 = (f32[64,512]{1,0:T(8,128)S(1)}, f32[64,512]{1,0:T(8,128)S(1)}, u32[]{:S(2)}, u32[]{:S(2)}) collective-permute-start(f32[64,512]{1,0:T(8,128)S(1)} %get-tuple-element.23), channel_id=1, source_target_pairs={{0,4},{2,6},{4,8},{6,10},{8,12},{10,14},{12,0},{14,2},{1,5},{3,7},... | collective-permute-start | bytes 393224 | tf_op jit(solution)/shard_map/ppermute | solution.py:18
  86.4 5.3 %collective-permute-start.6 = (f32[64,512]{1,0:T(8,128)S(1)}, f32[64,512]{1,0:T(8,128)}, u32[]{:S(2)}, u32[]{:S(2)}) collective-permute-start(f32[64,512]{1,0:T(8,128)S(1)} %get-tuple-element.26), channel_id=1, source_target_pairs={{0,12},{2,14},{4,0},{6,2},{8,4},{10,6},{12,8},{14,10},{1,13},{3,15... | collective-permute-start | bytes 393224 | tf_op jit(solution)/shard_map/ppermute | solution.py:18
  91.6 3.0 %shard_map.47 = (f32[128,512]{1,0:T(8,128)S(1)}, f32[128,512]{1,0:T(8,128)S(1)}, f32[128,512]{1,0:T(8,128)}, f32[128,512]{1,0:T(8,128)}, f32[128,512]{1,0:T(8,128)S(1)}) custom-call(s32[17]{0:T(128)S(1)} %pad_add_fusion.meta, bf16[512,768]{1,0:T(8,128)(2,1)S(1)} %get-tuple-element.16.vh, bf16[512,768]{1,0:T(8,128)(2,1)S(1)} %get-tuple-element.17.vl, ...), custom_call_target="tpu_custom_call" | custom-call | flops 1509949440 | bytes 4194304 | tf_op jit(solution)/shard_map/pallas_call | solution.py:83
  94.6 0.7 copy-done.1
  95.3 0.7 copy-done.2
  96.0 2.0 %collective-permute-start = (f32[128,512]{1,0:T(8,128)}, f32[128,512]{1,0:T(8,128)S(1)}, u32[]{:S(2)}, u32[]{:S(2)}) collective-permute-start(f32[128,512]{1,0:T(8,128)} %get-tuple-element.19), channel_id=1, source_target_pairs={{0,2},{2,4},{4,6},{6,8},{8,10},{10,12},{12,14},{14,0},{1,3},{3,5},... | collective-permute-start | bytes 786440 | tf_op jit(solution)/shard_map/ppermute | solution.py:18
  98.1 5.1 %collective-permute-start.1 = (f32[128,512]{1,0:T(8,128)}, f32[128,512]{1,0:T(8,128)S(1)}, u32[]{:S(2)}, u32[]{:S(2)}) collective-permute-start(f32[128,512]{1,0:T(8,128)} %get-tuple-element.20), channel_id=1, source_target_pairs={{0,14},{2,0},{4,2},{6,4},{8,6},{10,8},{12,10},{14,12},{1,15},{3,1}... | collective-permute-start | bytes 786440 | tf_op jit(solution)/shard_map/ppermute | solution.py:18
  103.2 0.0 collective-permute-done.2.came
  103.3 0.7 copy-done.4
  104.0 1.8 %shard_map.48 = f32[128,512]{1,0:T(8,128)} custom-call(f32[128,512]{1,0:T(8,128)} %copy-done.2, f32[128,512]{1,0:T(8,128)} %copy-done.4, f32[64,512]{1,0:T(8,128)} %copy-done.5), custom_call_target="tpu_custom_call" | custom-call | flops 65536 | bytes 786432 | tf_op jit(solution)/shard_map/pallas_call | solution.py:99
  105.8 2.5 %collective-permute-start.4 = (f32[128,512]{1,0:T(8,128)}, f32[128,512]{1,0:T(8,128)S(1)}, u32[]{:S(2)}, u32[]{:S(2)}) collective-permute-start(f32[128,512]{1,0:T(8,128)} %shard_map.48), channel_id=1, source_target_pairs={{0,4},{2,6},{4,8},{6,10},{8,12},{10,14},{12,0},{14,2},{1,5},{3,7},... | collective-permute-start | bytes 786440 | tf_op jit(solution)/shard_map/ppermute | solution.py:18
  108.3 0.0 collective-permute-done.6.half
  108.3 0.0 collective-permute-done.5.came
  108.3 1.8 %shard_map.49 = f32[128,512]{1,0:T(8,128)} custom-call(f32[128,512]{1,0:T(8,128)} %copy-done.1, f32[128,512]{1,0:T(8,128)} %collective-permute-done.5.came, f32[64,512]{1,0:T(8,128)} %collective-permute-done.6.half), custom_call_target="tpu_custom_call" | custom-call | flops 65536 | bytes 786432 | tf_op jit(solution)/shard_map/pallas_call | solution.py:99
  110.1 5.4 %collective-permute-start.7 = (f32[128,512]{1,0:T(8,128)}, f32[128,512]{1,0:T(8,128)S(1)}, u32[]{:S(2)}, u32[]{:S(2)}) collective-permute-start(f32[128,512]{1,0:T(8,128)} %shard_map.49), channel_id=1, source_target_pairs={{0,12},{2,14},{4,0},{6,2},{8,4},{10,6},{12,8},{14,10},{1,13},{3,15... | collective-permute-start | bytes 786440 | tf_op jit(solution)/shard_map/ppermute | solution.py:18
  115.5 0.0 collective-permute-done
  115.5 2.5 %collective-permute-done.4 = f32[128,512]{1,0:T(8,128)S(1)} collective-permute-done((f32[128,512]{1,0:T(8,128)}, f32[128,512]{1,0:T(8,128)S(1)}, u32[]{:S(2)}, u32[]{:S(2)}) %collective-permute-start.4) | collective-permute-done | bytes 262176 | tf_op jit(solution)/shard_map/ppermute | solution.py:18
  118.0 6.3 %collective-permute-done.7 = f32[128,512]{1,0:T(8,128)S(1)} collective-permute-done((f32[128,512]{1,0:T(8,128)}, f32[128,512]{1,0:T(8,128)S(1)}, u32[]{:S(2)}, u32[]{:S(2)}) %collective-permute-start.7) | collective-permute-done | bytes 262176 | tf_op jit(solution)/shard_map/ppermute | solution.py:18
  124.4 0.1 add_add_fusion
  124.5 10.1 %all_to_all.16 = f32[8,16,512]{2,1,0:T(8,128)S(1)} all-to-all(f32[8,16,512]{2,1,0:T(8,128)S(1)} %bitcast.5), channel_id=1, replica_groups=mesh['xh'=2,'y'=8,'core'=2,'z'=8,'xl'=2] {'xh','core','xl'}, dimensions={0} | all-to-all | bytes 524288 | tf_op jit(solution)/shard_map/all_to_all | solution.py:142
  134.6 0.7 add.59
  (14 shorter events, 0.0 us)
Async XLA Ops:
  21.2 6.5 %copy-start.6 = (s32[8]{0:T(128)S(1)}, s32[8]{0:T(128)}, u32[]{:S(2)}) copy-start(s32[8]{0:T(128)} %param.7) | copy-start | bytes 100
  21.2 42.2 %all-to-all-start.1 = ((f32[8,256,384]{2,1,0:T(8,128)}), f32[8,256,384]{2,1,0:T(8,128)S(1)}, u32[]{:S(2)}, u32[]{:S(2)}) async-start(f32[8,256,384]{2,1,0:T(8,128)} %param.4), calls=%async_computation.1 | async-start | bytes 6291456 | tf_op jit(solution)/shard_map/all_to_all | solution.py:115
  26.9 45.1 %all-gather.3.cloned.1.call-start = ((), (), s32[]{:S(2)}) async-start(), calls=%async_computation.3 | async-start | bytes 1769472 | tf_op jit(solution)/shard_map/all_gather | solution.py:114
  72.0 1.4 copy-start
  75.9 27.4 %collective-permute-start.2 = (f32[128,512]{1,0:T(8,128)S(1)}, f32[128,512]{1,0:T(8,128)S(1)}, u32[]{:S(2)}, u32[]{:S(2)}) collective-permute-start(f32[128,512]{1,0:T(8,128)S(1)} %get-tuple-element.22), channel_id=1, source_target_pairs={{0,2},{2,4},{4,6},{6,8},{8,10},{10,12},{12,14},{14,0},{1,3},{3,5},... | collective-permute-start | bytes 786440 | tf_op jit(solution)/shard_map/ppermute | solution.py:18
  79.4 28.9 %collective-permute-start.5 = (f32[128,512]{1,0:T(8,128)}, f32[128,512]{1,0:T(8,128)}, u32[]{:S(2)}, u32[]{:S(2)}) collective-permute-start(f32[128,512]{1,0:T(8,128)} %get-tuple-element.25), channel_id=1, source_target_pairs={{0,14},{2,0},{4,2},{6,4},{8,6},{10,8},{12,10},{14,12},{1,15},{3,1}... | collective-permute-start | bytes 786440 | tf_op jit(solution)/shard_map/ppermute | solution.py:18
  83.6 14.4 %collective-permute-start.3 = (f32[64,512]{1,0:T(8,128)S(1)}, f32[64,512]{1,0:T(8,128)S(1)}, u32[]{:S(2)}, u32[]{:S(2)}) collective-permute-start(f32[64,512]{1,0:T(8,128)S(1)} %get-tuple-element.23), channel_id=1, source_target_pairs={{0,4},{2,6},{4,8},{6,10},{8,12},{10,14},{12,0},{14,2},{1,5},{3,7},... | collective-permute-start | bytes 393224 | tf_op jit(solution)/shard_map/ppermute | solution.py:18
  86.4 21.9 %collective-permute-start.6 = (f32[64,512]{1,0:T(8,128)S(1)}, f32[64,512]{1,0:T(8,128)}, u32[]{:S(2)}, u32[]{:S(2)}) collective-permute-start(f32[64,512]{1,0:T(8,128)S(1)} %get-tuple-element.26), channel_id=1, source_target_pairs={{0,12},{2,14},{4,0},{6,2},{8,4},{10,6},{12,8},{14,10},{1,13},{3,15... | collective-permute-start | bytes 393224 | tf_op jit(solution)/shard_map/ppermute | solution.py:18
  94.6 0.7 copy-start.1
  95.3 0.7 copy-start.2
  96.0 38.5 %copy-start.3 = (f32[8,16,512]{2,1,0:T(8,128)S(1)}, f32[8,16,512]{2,1,0:T(8,128)}, u32[]{:S(2)}) copy-start(f32[8,16,512]{2,1,0:T(8,128)} %param.6) | copy-start | bytes 786436
  96.0 19.5 %collective-permute-start = (f32[128,512]{1,0:T(8,128)}, f32[128,512]{1,0:T(8,128)S(1)}, u32[]{:S(2)}, u32[]{:S(2)}) collective-permute-start(f32[128,512]{1,0:T(8,128)} %get-tuple-element.19), channel_id=1, source_target_pairs={{0,2},{2,4},{4,6},{6,8},{8,10},{10,12},{12,14},{14,0},{1,3},{3,5},... | collective-permute-start | bytes 786440 | tf_op jit(solution)/shard_map/ppermute | solution.py:18
  98.1 5.2 %copy-start.5 = (f32[64,512]{1,0:T(8,128)}, f32[64,512]{1,0:T(8,128)S(1)}, u32[]{:S(2)}) copy-start(f32[64,512]{1,0:T(8,128)S(1)} %collective-permute-done.3.half) | copy-start | bytes 393220
  98.1 17.4 %collective-permute-start.1 = (f32[128,512]{1,0:T(8,128)}, f32[128,512]{1,0:T(8,128)S(1)}, u32[]{:S(2)}, u32[]{:S(2)}) collective-permute-start(f32[128,512]{1,0:T(8,128)} %get-tuple-element.20), channel_id=1, source_target_pairs={{0,14},{2,0},{4,2},{6,4},{8,6},{10,8},{12,10},{14,12},{1,15},{3,1}... | collective-permute-start | bytes 786440 | tf_op jit(solution)/shard_map/ppermute | solution.py:18
  103.3 0.7 copy-start.4
  105.8 12.3 %collective-permute-start.4 = (f32[128,512]{1,0:T(8,128)}, f32[128,512]{1,0:T(8,128)S(1)}, u32[]{:S(2)}, u32[]{:S(2)}) collective-permute-start(f32[128,512]{1,0:T(8,128)} %shard_map.48), channel_id=1, source_target_pairs={{0,4},{2,6},{4,8},{6,10},{8,12},{10,14},{12,0},{14,2},{1,5},{3,7},... | collective-permute-start | bytes 786440 | tf_op jit(solution)/shard_map/ppermute | solution.py:18
  110.1 14.3 %collective-permute-start.7 = (f32[128,512]{1,0:T(8,128)}, f32[128,512]{1,0:T(8,128)S(1)}, u32[]{:S(2)}, u32[]{:S(2)}) collective-permute-start(f32[128,512]{1,0:T(8,128)} %shard_map.49), channel_id=1, source_target_pairs={{0,12},{2,14},{4,0},{6,2},{8,4},{10,6},{12,8},{14,10},{1,13},{3,15... | collective-permute-start | bytes 786440 | tf_op jit(solution)/shard_map/ppermute | solution.py:18
Sparse Core Ops, SparseCore 0:
  29.8 42.1 all-gather.2

commit v3 on v1

v3 whole, which is shorter than its diff:
```python
import functools

import jax
import jax.numpy as jnp
from jax import lax
from jax.experimental import pallas as pl
from jax.experimental.pallas import tpu as pltpu
from jax.sharding import Mesh, PartitionSpec as P

LINE = ("xh", "core", "xl")
N_Y = N_Z = N_LINE = 8
ROWS = 16
OUTER = 512
STEPS = 2


def split(x):
    high = x.astype(jnp.bfloat16)
    return high, (x - high.astype(jnp.float32)).astype(jnp.bfloat16)


def sums_kernel(live, v0, v1, t_ref, out, th, tl, vh, vl):
    width = t_ref.shape[2]

    @pl.when(pl.program_id(0) == 0)
    def _():
        slots = lax.broadcasted_iota(jnp.int32, (ROWS, width), 1)
        for xh, v_ref in enumerate((v0, v1)):
            for core in range(2):
                for y in range(N_Y):
                    for x in range(2):
                        block = v_ref[core, (y * 2 + x) * ROWS : (y * 2 + x + 1) * ROWS]
                        high, low = split(jnp.where(slots + x * width < live[0], block, 0.0))
                        row = ((xh * N_Y + y) * 2 + core) * ROWS
                        at = (slice(row, row + ROWS), slice(x * width, (x + 1) * width))
                        vh[at] = high
                        vl[at] = low

    for z in range(N_Z // STEPS):
        for g in range(N_LINE):
            part, x = divmod(g, 2)
            high, low = split(t_ref[g, z * 32 : (z + 1) * 32])
            at = (slice((z * 4 + part) * 32, (z * 4 + part + 1) * 32), slice(x * width, (x + 1) * width))
            th[at] = high
            tl[at] = low
    dot = functools.partial(
        lax.dot_general, dimension_numbers=(((1,), (1,)), ((), ())), preferred_element_type=jnp.float32
    )
    out[...] = dot(th[...], vh[...]) + (dot(tl[...], vh[...]) + dot(th[...], vl[...]))


def partial_sums(live, v0, v1, t):
    rows, width = t.shape[1] // STEPS, t.shape[2]
    total = 4 * t.shape[1]
    half = total // STEPS
    v_spec = pl.BlockSpec(v0.shape, lambda i, m: (0, 0, 0))
    return pl.pallas_call(
        sums_kernel,
        out_shape=jax.ShapeDtypeStruct((total, OUTER), jnp.float32),
        grid_spec=pltpu.PrefetchScalarGridSpec(
            num_scalar_prefetch=1,
            grid=(STEPS,),
            in_specs=[v_spec, v_spec, pl.BlockSpec((N_LINE, rows, width), lambda i, m: (0, i, 0))],
            out_specs=pl.BlockSpec((half, OUTER), lambda i, m: (i, 0)),
            scratch_shapes=[pltpu.VMEM((half, 2 * width), jnp.bfloat16)] * 2
            + [pltpu.VMEM((OUTER, 2 * width), jnp.bfloat16)] * 2,
        ),
        compiler_params=pltpu.CompilerParams(vmem_limit_bytes=32 << 20),
        cost_estimate=pl.CostEstimate(flops=12 * total * width * OUTER, bytes_accessed=8 << 20, transcendentals=0),
    )(live, v0, v1, t)


def body(amplitudes, integrals, residual_in, cd_count):
    width = amplitudes.shape[2]
    live = cd_count[lax.axis_index(LINE)] - lax.axis_index("z") * (2 * width)

    v = lax.all_to_all(integrals, LINE, 0, 0, tiled=True)
    t = lax.all_to_all(amplitudes, LINE, 0, 0, tiled=True)
    v = v.reshape(2, 2, 2 * ROWS, width)
    v0, v1 = (lax.all_gather(v[xh], "y", axis=1, tiled=True) for xh in range(2))

    sums = partial_sums(live[None].astype(jnp.int32), v0, v1, t)
    mine = lax.psum_scatter(sums.reshape(N_Z, N_LINE * ROWS, OUTER), "z", scatter_dimension=0)
    ladder = lax.all_to_all(mine.reshape(N_LINE, ROWS, OUTER), LINE, 0, 0, tiled=True)
    return residual_in + ladder


def solution(mesh):
    mesh = Mesh(mesh.devices.reshape(2, 8, 2, 8, 2), ("xh", "y", "core", "z", "xl"))
    row, col = ("xh", "y", "core"), ("z", "xl")
    in_specs = (P(None, row, col), P(None, row, col), P(None, row + col, None), P())
    return jax.shard_map(body, mesh=mesh, in_specs=in_specs, out_specs=P(None, row + col, None), check_vma=False)
```

time: 148 us -> 157 us (1.061)
  blocking collectives: 25 us -> 80.8 us
  waiting for transfers between devices: 86.4 us -> 46 us
  local copies, waits for them, and re-layouts: 10.9 us -> 4.21 us
  Pallas kernels: 0 us -> 3.39 us
  matrix products: 2.79 us -> 0 us
    all_gather x0 -> x2, blocking collectives: none -> 56.7 us  [body(): v0, v1 = (lax.all_gather(v[xh], 'y', axis=1, tiled=True) for xh in range(2))]
    all_to_all x1, waiting for transfers between devices: 34.3 us -> 0.01 us  [body(): t = lax.all_to_all(amplitudes, LINE, 0, 0, tiled=True)]
    all_gather x1 -> x0, waiting for transfers between devices: 6.81 us -> none  [body(): v = lax.all_gather(v, 'y', axis=0)]
    transpose x2 -> x0, local copies, waits for them, and re-layouts: 4.86 us -> none  [the longest x1 3.25 us: body(): sums.reshape(2, 2, 8, 2, 16, 512).transpose(2, 0, 1, 3, 4, 5)]
    pallas_call x0 -> x1, Pallas kernels: none -> 3.39 us  [partial_sums(): pl.pallas_call(sums_kernel, out_shape=jax.ShapeDtypeStruct((total, OUTER)...]
    dot_general x1 -> x0, matrix products: 2.79 us -> none  [body(): sums = jnp.einsum('xic,xac->ia', t, v, precision=lax.Precision.HIGH)]
    reshape x1 -> x0, local copies, waits for them, and re-layouts: 1.86 us -> none  [body(): t = t.reshape(2, 2, 2, 256, width)]
    unnamed x6 -> x10, local copies, waits for them, and re-layouts: 1.78 us -> 3.61 us
  transfers between devices with their start and end apart: 3 -> 2, of which waited for: 3 -> 1; matrix products, arithmetic and copies ran while one was open for 2% -> 0% of each run, Pallas kernels for 0% -> 0%
where the time goes in v3:
time: 157 us; the launch traced here: 155 us
  blocking collectives  80.8 us (51%)
  waiting for transfers between devices  46 us (29%)
  between operations  14.1 us (9%)
  starting transfers between devices  5.79 us (4%)
  local copies, waits for them, and re-layouts  4.21 us (3%)
  Pallas kernels  3.39 us (2%)
    all_gather x2, blocking collectives, body(): v0, v1 = (lax.all_gather(v[xh], 'y', axis=1, tiled=True) for xh in range(2))  56.7 us
    reduce_scatter x1, waiting for transfers between devices, body(): lax.psum_scatter(sums.reshape(N_Z, N_LINE * ROWS, OUTER), 'z', scatter_di...  46 us
    all_to_all x1, blocking collectives, body(): v = lax.all_to_all(integrals, LINE, 0, 0, tiled=True)  13.9 us
    all_to_all x1, blocking collectives, body(): lax.all_to_all(mine.reshape(N_LINE, ROWS, OUTER), LINE, 0, 0, tiled=True)  10.2 us
    all_to_all x1, starting transfers between devices, body(): t = lax.all_to_all(amplitudes, LINE, 0, 0, tiled=True)  5.79 us
    unnamed x10, local copies, waits for them, and re-layouts  3.61 us
    pallas_call x1, Pallas kernels, partial_sums(): pl.pallas_call(sums_kernel, out_shape=jax.ShapeDtypeStruct((total, OUTER)...  3.39 us
  transfers between devices with their start and end apart: 2, of which 1 were waited for; matrix products, arithmetic and copies ran while one was open for 0% of the time, Pallas kernels for 0%

profile of v3, /device:TPU:6, one launch (start us, length us, event | category | flops | bytes accessed | tf_op | source)
XLA Modules:
  0.0 155.0 jit_solution(975513465512447291)
XLA Ops:
  6.5 13.9 %all_to_all.15 = f32[8,16,384]{2,1,0:T(8,128)S(1)} all-to-all(f32[8,16,384]{2,1,0:T(8,128)} %param.5), channel_id=1, replica_groups=mesh['xh'=2,'y'=8,'core'=2,'z'=8,'xl'=2] {'xh','core','xl'}, dimensions={0} | all-to-all | bytes 393216 | tf_op jit(solution)/shard_map/all_to_all | solution.py:77
  20.4 0.0 copy-start.4
  20.4 5.8 %all-to-all-start.1 = ((f32[8,256,384]{2,1,0:T(8,128)}), f32[8,256,384]{2,1,0:T(8,128)S(1)}, u32[]{:S(2)}, u32[]{:S(2)}) async-start(f32[8,256,384]{2,1,0:T(8,128)} %param.4), calls=%async_computation.1 | async-start | bytes 6291456 | tf_op jit(solution)/shard_map/all_to_all | solution.py:78
  26.2 0.0 reduce-scatter.2.cloned.1.call-start
  26.2 0.0 copy-done.4
  26.2 0.6 dynamic_slice.3
  27.5 28.3 %all_gather.6.v0 = f32[2,256,384]{2,1,0:T(8,128)} all-gather(f32[2,32,384]{2,1,0:T(8,128)S(1)} %bitcast.8), channel_id=1, replica_groups=mesh['xh'=2,'y'=8,'core'=2,'z'=8,'xl'=2] {'y'}, dimensions={1}, use_global_device_ids=true | all-gather | bytes 884736 | tf_op jit(solution)/shard_map/all_gather | solution.py:80
  55.8 28.4 %all_gather.7.v1 = f32[2,256,384]{2,1,0:T(8,128)} all-gather(f32[2,32,384]{2,1,0:T(8,128)S(1)} %bitcast.7), channel_id=1, replica_groups=mesh['xh'=2,'y'=8,'core'=2,'z'=8,'xl'=2] {'y'}, dimensions={1}, use_global_device_ids=true | all-gather | bytes 884736 | tf_op jit(solution)/shard_map/all_gather | solution.py:80
  84.2 0.0 all-to-all-done.1.t_ref
  84.2 0.0 copy-start.1
  84.2 1.1 copy-done.1
  85.4 0.0 copy-start.2
  85.4 1.1 copy-done.2
  86.5 0.0 copy-start.3
  86.5 3.4 %shard_map.46 = f32[1024,512]{1,0:T(8,128)S(1)} custom-call(s32[1]{0:T(128)} %bitcast.1.live, f32[2,256,384]{2,1,0:T(8,128)S(1)} %copy-done.1, f32[2,256,384]{2,1,0:T(8,128)S(1)} %copy-done.2, f32[8,256,384]{2,1,0:T(8,128)S(1)} %all-to-all-done.1.t_ref), custom_call_target="tpu_custom_call" | custom-call | flops 2415919104 | bytes 8388608 | tf_op jit(solution)/shard_map/pallas_call | solution.py:57
  89.9 0.0 copy-start
  89.9 1.3 copy-done
  91.2 0.0 reduce-scatter.2.cloned.1.call-update
  91.2 46.0 %reduce-scatter.2.cloned.1.call-done = f32[1,128,512]{2,1,0:T(8,128)} async-done(((f32[8,128,512]{2,1,0:T(8,128)}), f32[1,128,512]{2,1,0:T(8,128)}) %reduce-scatter.2.cloned.1.call-update) | async-done | bytes 262160 | tf_op jit(solution)/shard_map/reduce_scatter | solution.py:83
  137.2 10.2 %all_to_all.16 = f32[8,16,512]{2,1,0:T(8,128)S(1)} all-to-all(f32[8,16,512]{2,1,0:T(8,128)} %bitcast.9), channel_id=1, replica_groups=mesh['xh'=2,'y'=8,'core'=2,'z'=8,'xl'=2] {'xh','core','xl'}, dimensions={0} | all-to-all | bytes 524288 | tf_op jit(solution)/shard_map/all_to_all | solution.py:84
  147.4 0.0 copy-done.3
  147.4 0.7 add.17
  (1 shorter events, 0.0 us)
Async XLA Ops:
  20.4 5.8 %copy-start.4 = (s32[8]{0:T(128)S(1)}, s32[8]{0:T(128)}, u32[]{:S(2)}) copy-start(s32[8]{0:T(128)} %param.7) | copy-start | bytes 100
  20.4 63.8 %all-to-all-start.1 = ((f32[8,256,384]{2,1,0:T(8,128)}), f32[8,256,384]{2,1,0:T(8,128)S(1)}, u32[]{:S(2)}, u32[]{:S(2)}) async-start(f32[8,256,384]{2,1,0:T(8,128)} %param.4), calls=%async_computation.1 | async-start | bytes 6291456 | tf_op jit(solution)/shard_map/all_to_all | solution.py:78
  26.2 111.0 %reduce-scatter.2.cloned.1.call-start = ((), (), s32[]{:S(2)}) async-start(), calls=%async_computation.4 | async-start | bytes 2359296 | tf_op jit(solution)/shard_map/reduce_scatter | solution.py:83
  84.2 1.1 copy-start.1
  85.4 1.1 copy-start.2
  86.5 61.0 %copy-start.3 = (f32[8,16,512]{2,1,0:T(8,128)S(1)}, f32[8,16,512]{2,1,0:T(8,128)}, u32[]{:S(2)}) copy-start(f32[8,16,512]{2,1,0:T(8,128)} %param.6) | copy-start | bytes 786436
  89.9 1.3 copy-start
Sparse Core Ops, SparseCore 0:
  91.4 45.8 reduce-scatter.1

commit v4 on v3

v4 whole, which is shorter than its diff:
```python
import functools

import jax
import jax.numpy as jnp
from jax import lax
from jax.experimental import pallas as pl
from jax.experimental.pallas import tpu as pltpu
from jax.sharding import Mesh, PartitionSpec as P

GROUP = ("core", "z0", "xl")
N_Y, N_ZQ, N_GROUP = 8, 4, 8
ROWS = 16
OUTER = 512
STEPS = 2


def split(x):
    high = x.astype(jnp.bfloat16)
    return high, (x - high.astype(jnp.float32)).astype(jnp.bfloat16)


def sums_kernel(live, v_ref, t_ref, out, th, tl, vh, vl):
    width = t_ref.shape[2]

    @pl.when(pl.program_id(0) == 0)
    def _():
        slots = lax.broadcasted_iota(jnp.int32, (ROWS, width), 1)
        for y in range(N_Y):
            for xh in range(2):
                for g in range(N_GROUP):
                    core, c = divmod(g, 4)
                    block = jnp.where(slots + c * width < live[0], v_ref[y, xh * N_GROUP + g], 0.0)
                    high, low = split(block)
                    row = ((xh * N_Y + y) * 2 + core) * ROWS
                    at = (slice(row, row + ROWS), slice(c * width, (c + 1) * width))
                    vh[at] = high
                    vl[at] = low

    for zq in range(N_ZQ // STEPS):
        for g in range(N_GROUP):
            core, c = divmod(g, 4)
            high, low = split(t_ref[g, zq * 64 : (zq + 1) * 64])
            at = (slice((zq * 2 + core) * 64, (zq * 2 + core + 1) * 64), slice(c * width, (c + 1) * width))
            th[at] = high
            tl[at] = low
    dot = functools.partial(
        lax.dot_general, dimension_numbers=(((1,), (1,)), ((), ())), preferred_element_type=jnp.float32
    )
    out[...] = dot(th[...], vh[...]) + (dot(tl[...], vh[...]) + dot(th[...], vl[...]))


def partial_sums(live, v, t):
    rows, width = t.shape[1] // STEPS, t.shape[2]
    total = 2 * t.shape[1]
    part = total // STEPS
    return pl.pallas_call(
        sums_kernel,
        out_shape=jax.ShapeDtypeStruct((total, OUTER), jnp.float32),
        grid_spec=pltpu.PrefetchScalarGridSpec(
            num_scalar_prefetch=1,
            grid=(STEPS,),
            in_specs=[
                pl.BlockSpec(v.shape, lambda i, m: (0, 0, 0, 0)),
                pl.BlockSpec((N_GROUP, rows, width), lambda i, m: (0, i, 0)),
            ],
            out_specs=pl.BlockSpec((part, OUTER), lambda i, m: (i, 0)),
            scratch_shapes=[pltpu.VMEM((part, 4 * width), jnp.bfloat16)] * 2
            + [pltpu.VMEM((OUTER, 4 * width), jnp.bfloat16)] * 2,
        ),
        compiler_params=pltpu.CompilerParams(vmem_limit_bytes=56 << 20),
        cost_estimate=pl.CostEstimate(flops=24 * total * width * OUTER, bytes_accessed=8 << 20, transcendentals=0),
    )(live, v, t)


def body(amplitudes, integrals, residual_in, cd_count):
    width = amplitudes.shape[2]
    live = cd_count[lax.axis_index(GROUP)] - lax.axis_index("zq") * (4 * width)

    v = lax.all_to_all(jnp.concatenate([integrals, integrals]), ("xh",) + GROUP, 0, 0, tiled=True)
    v = lax.all_gather(v, "y", axis=0)
    t = lax.all_to_all(amplitudes, GROUP, 0, 0, tiled=True)

    sums = partial_sums(live[None].astype(jnp.int32), v, t)
    mine = lax.psum_scatter(sums.reshape(N_ZQ, N_GROUP * ROWS, OUTER), "zq", scatter_dimension=0)
    ladder = lax.all_to_all(mine.reshape(N_GROUP, ROWS, OUTER), GROUP, 0, 0, tiled=True)
    return residual_in + ladder


def solution(mesh):
    mesh = Mesh(mesh.devices.reshape(2, 8, 2, 4, 2, 2), ("xh", "y", "core", "zq", "z0", "xl"))
    row, col = ("xh", "y", "core"), ("zq", "z0", "xl")
    in_specs = (P(None, row, col), P(None, row, col), P(None, row + col, None), P())
    return jax.shard_map(body, mesh=mesh, in_specs=in_specs, out_specs=P(None, row + col, None), check_vma=False)
```

time: 157 us -> 142 us (0.904)
  the two profiles are of different devices: /device:TPU:6 before, /device:TPU:1 now
where the time goes in v4:
time: 142 us; the launch traced here: 141 us
  waiting for transfers between devices  83.5 us (59%)
  blocking collectives  30.1 us (21%)
  between operations  14.1 us (10%)
  Pallas kernels  6.59 us (5%)
  starting transfers between devices  4.54 us (3%)
  other arithmetic  1.83 us (1%)
    all_to_all x1, waiting for transfers between devices, body(): t = lax.all_to_all(amplitudes, GROUP, 0, 0, tiled=True)  35.5 us
    reduce_scatter x1, waiting for transfers between devices, body(): lax.psum_scatter(sums.reshape(N_ZQ, N_GROUP * ROWS, OUTER), 'zq', scatter...  35.5 us
    all_to_all x1, blocking collectives, body(): lax.all_to_all(jnp.concatenate([integrals, integrals]), ('xh',) + GROUP,...  18.6 us
    all_gather x1, waiting for transfers between devices, body(): v = lax.all_gather(v, 'y', axis=0)  11.8 us
    all_to_all x1, blocking collectives, body(): lax.all_to_all(mine.reshape(N_GROUP, ROWS, OUTER), GROUP, 0, 0, tiled=True)  11.4 us
    pallas_call x1, Pallas kernels, partial_sums(): pl.pallas_call(sums_kernel, out_shape=jax.ShapeDtypeStruct((total, OUTER)...  6.59 us
    all_to_all x1, starting transfers between devices, body(): t = lax.all_to_all(amplitudes, GROUP, 0, 0, tiled=True)  4.5 us
  transfers between devices with their start and end apart: 3, of which 3 were waited for; matrix products, arithmetic and copies ran while one was open for 0% of the time, Pallas kernels for 0%

profile of v4, /device:TPU:1, one launch (start us, length us, event | category | flops | bytes accessed | tf_op | source)
XLA Modules:
  0.0 141.2 jit_solution(8498007551904036000)
XLA Ops:
  6.5 1.1 pad_maximum_fusion
  7.6 18.6 %all_to_all.15 = f32[16,16,384]{2,1,0:T(8,128)} all-to-all(f32[16,16,384]{2,1,0:T(8,128)S(1)} %pad_maximum_fusion), channel_id=1, replica_groups=mesh['xh'=2,'y'=8,'core'=2,'zq'=4,'z0'=2,'xl'=2] {'xh','core','z0','xl'}, dimensions={0} | all-to-all | bytes 786432 | tf_op jit(solution)/shard_map/all_to_all | solution.py:79
  26.2 0.0 copy-start.2
  26.2 4.5 %all-to-all-start.1 = ((f32[8,256,384]{2,1,0:T(8,128)}), f32[8,256,384]{2,1,0:T(8,128)S(1)}, u32[]{:S(2)}, u32[]{:S(2)}) async-start(f32[8,256,384]{2,1,0:T(8,128)} %param.4), calls=%async_computation.1 | async-start | bytes 6291456 | tf_op jit(solution)/shard_map/all_to_all | solution.py:81
  30.7 0.0 all-gather.3.cloned.1.call-start
  30.8 0.7 all-gather.3.cloned.1.call-update
  31.5 0.0 reduce-scatter.2.cloned.1.call-start
  31.5 0.0 copy-done.2
  31.5 0.6 dynamic_slice.3
  32.8 35.5 %all-to-all-done.1.t_ref = f32[8,256,384]{2,1,0:T(8,128)S(1)} async-done(((f32[8,256,384]{2,1,0:T(8,128)}), f32[8,256,384]{2,1,0:T(8,128)S(1)}, u32[]{:S(2)}, u32[]{:S(2)}) %all-to-all-start.1) | async-done | bytes 3145760 | tf_op jit(solution)/shard_map/all_to_all | solution.py:81
  68.3 0.0 copy-start
  68.3 11.8 %all-gather.3.cloned.1.call-done = f32[128,16,384]{2,1,0:T(8,128)} async-done(((f32[16,16,384]{2,1,0:T(8,128)}), f32[128,16,384]{2,1,0:T(8,128)}) %all-gather.3.cloned.1.call-update) | async-done | bytes 3145744 | tf_op jit(solution)/shard_map/all_gather | solution.py:80
  80.1 0.0 copy-done
  80.1 0.0 copy-start.1
  80.1 6.6 %shard_map.46 = f32[512,512]{1,0:T(8,128)} custom-call(s32[1]{0:T(128)} %bitcast.1.live, f32[8,16,16,384]{3,2,1,0:T(8,128)} %bitcast.7, f32[8,256,384]{2,1,0:T(8,128)} %copy-done), custom_call_target="tpu_custom_call" | custom-call | flops 2415919104 | bytes 8388608 | tf_op jit(solution)/shard_map/pallas_call | solution.py:56
  86.7 0.0 reduce-scatter.2.cloned.1.call-update
  86.7 35.5 %reduce-scatter.2.cloned.1.call-done = f32[1,128,512]{2,1,0:T(8,128)} async-done(((f32[4,128,512]{2,1,0:T(8,128)}), f32[1,128,512]{2,1,0:T(8,128)}) %reduce-scatter.2.cloned.1.call-update) | async-done | bytes 262160 | tf_op jit(solution)/shard_map/reduce_scatter | solution.py:84
  122.2 11.4 %all_to_all.16 = f32[8,16,512]{2,1,0:T(8,128)S(1)} all-to-all(f32[8,16,512]{2,1,0:T(8,128)} %bitcast.6), channel_id=1, replica_groups=mesh['xh'=2,'y'=8,'core'=2,'zq'=4,'z0'=2,'xl'=2] {'core','z0','xl'}, dimensions={0} | all-to-all | bytes 524288 | tf_op jit(solution)/shard_map/all_to_all | solution.py:85
  133.7 0.0 copy-done.1
  133.7 0.7 add.17
Async XLA Ops:
  26.2 5.3 %copy-start.2 = (s32[8]{0:T(128)S(1)}, s32[8]{0:T(128)}, u32[]{:S(2)}) copy-start(s32[8]{0:T(128)} %param.7) | copy-start | bytes 100
  26.2 42.0 %all-to-all-start.1 = ((f32[8,256,384]{2,1,0:T(8,128)}), f32[8,256,384]{2,1,0:T(8,128)S(1)}, u32[]{:S(2)}, u32[]{:S(2)}) async-start(f32[8,256,384]{2,1,0:T(8,128)} %param.4), calls=%async_computation.1 | async-start | bytes 6291456 | tf_op jit(solution)/shard_map/all_to_all | solution.py:81
  30.7 49.3 %all-gather.3.cloned.1.call-start = ((), (), s32[]{:S(2)}) async-start(), calls=%async_computation.5 | async-start | bytes 3538944 | tf_op jit(solution)/shard_map/all_gather | solution.py:80
  31.5 90.7 %reduce-scatter.2.cloned.1.call-start = ((), (), s32[]{:S(2)}) async-start(), calls=%async_computation.4 | async-start | bytes 1310720 | tf_op jit(solution)/shard_map/reduce_scatter | solution.py:84
  68.3 11.8 %copy-start = (f32[8,256,384]{2,1,0:T(8,128)}, f32[8,256,384]{2,1,0:T(8,128)S(1)}, u32[]{:S(2)}) copy-start(f32[8,256,384]{2,1,0:T(8,128)S(1)} %all-to-all-done.1.t_ref) | copy-start | bytes 9437188
  80.1 53.6 %copy-start.1 = (f32[8,16,512]{2,1,0:T(8,128)S(1)}, f32[8,16,512]{2,1,0:T(8,128)}, u32[]{:S(2)}) copy-start(f32[8,16,512]{2,1,0:T(8,128)} %param.6) | copy-start | bytes 786436
Sparse Core Ops, SparseCore 0:
  33.6 46.3 all-gather.2
  86.8 35.3 reduce-scatter.1

commit v5 on v1

v5 whole, which is shorter than its diff:
```python
import functools

import jax
import jax.numpy as jnp
from jax import lax
from jax.experimental import pallas as pl
from jax.experimental.pallas import tpu as pltpu
from jax.sharding import Mesh, PartitionSpec as P

GROUP = ("core", "z0", "xl")
N_Y, N_ZQ, N_GROUP = 8, 4, 8
ROWS = 16
OUTER = 512


def split(x):
    high = x.astype(jnp.bfloat16)
    return high, (x - high.astype(jnp.float32)).astype(jnp.bfloat16)


def pair_kernel(t_ref, th, tl):
    rows, width = t_ref.shape[1:]
    for c in range(4):
        th[:, c * width : (c + 1) * width], tl[:, c * width : (c + 1) * width] = split(t_ref[c])


def pairs(t):
    rows, width = t.shape[1] // N_ZQ, t.shape[2]
    total = 2 * t.shape[1]
    out_spec = pl.BlockSpec((rows, 4 * width), lambda zq, core: (2 * zq + core, 0))
    return pl.pallas_call(
        pair_kernel,
        out_shape=[jax.ShapeDtypeStruct((total, 4 * width), jnp.bfloat16)] * 2,
        grid=(N_ZQ, 2),
        in_specs=[pl.BlockSpec((4, rows, width), lambda zq, core: (core, zq, 0))],
        out_specs=[out_spec] * 2,
        compiler_params=pltpu.CompilerParams(vmem_limit_bytes=60 << 20),
        cost_estimate=pl.CostEstimate(flops=3 * t.size, bytes_accessed=8 * t.size, transcendentals=0),
    )(t)


def sums_kernel(live, v_ref, th, tl, out, vh, vl):
    width = v_ref.shape[3]
    slots = lax.broadcasted_iota(jnp.int32, (ROWS, width), 1)
    for y in range(N_Y):
        for xh in range(2):
            for g in range(N_GROUP):
                core, c = divmod(g, 4)
                block = jnp.where(slots + c * width < live[0], v_ref[y, xh * N_GROUP + g], 0.0)
                high, low = split(block)
                row = ((xh * N_Y + y) * 2 + core) * ROWS
                at = (slice(row, row + ROWS), slice(c * width, (c + 1) * width))
                vh[at] = high
                vl[at] = low
    dot = functools.partial(
        lax.dot_general, dimension_numbers=(((1,), (1,)), ((), ())), preferred_element_type=jnp.float32
    )
    out[...] = dot(th[...], vh[...]) + (dot(tl[...], vh[...]) + dot(th[...], vl[...]))


def partial_sums(live, v, th, tl):
    whole = lambda a: pl.BlockSpec(a.shape, lambda i, m: (0,) * a.ndim)
    out = jax.ShapeDtypeStruct((th.shape[0], OUTER), jnp.float32)
    return pl.pallas_call(
        sums_kernel,
        out_shape=out,
        grid_spec=pltpu.PrefetchScalarGridSpec(
            num_scalar_prefetch=1,
            grid=(1,),
            in_specs=[whole(v), whole(th), whole(tl)],
            out_specs=whole(out),
            scratch_shapes=[pltpu.VMEM((OUTER, th.shape[1]), jnp.bfloat16)] * 2,
        ),
        compiler_params=pltpu.CompilerParams(vmem_limit_bytes=60 << 20),
        cost_estimate=pl.CostEstimate(flops=6 * th.size * OUTER, bytes_accessed=8 << 20, transcendentals=0),
    )(live, v, th, tl)


def body(amplitudes, integrals, residual_in, cd_count):
    width = amplitudes.shape[2]
    live = cd_count[lax.axis_index(GROUP)] - lax.axis_index("zq") * (4 * width)

    v = lax.all_to_all(jnp.concatenate([integrals, integrals]), ("xh",) + GROUP, 0, 0, tiled=True)
    v = lax.all_gather(v, "y", axis=0)
    th, tl = pairs(lax.all_to_all(amplitudes, GROUP, 0, 0, tiled=True))

    sums = partial_sums(live[None].astype(jnp.int32), v, th, tl)
    parts = lax.all_to_all(sums.reshape(N_ZQ * N_GROUP, ROWS, OUTER), ("zq",) + GROUP, 0, 0, tiled=True)
    return residual_in + jnp.sum(parts.reshape(N_ZQ, N_GROUP, ROWS, OUTER), axis=0)


def solution(mesh):
    mesh = Mesh(mesh.devices.reshape(2, 8, 2, 4, 2, 2), ("xh", "y", "core", "zq", "z0", "xl"))
    row, col = ("xh", "y", "core"), ("zq", "z0", "xl")
    in_specs = (P(None, row, col), P(None, row, col), P(None, row + col, None), P())
    return jax.shard_map(body, mesh=mesh, in_specs=in_specs, out_specs=P(None, row + col, None), check_vma=False)
```

time: 148 us -> 132 us (0.89); the launches traced: 146 us -> 132 us
  waiting for transfers between devices: 86.4 us -> 42.1 us
  blocking collectives: 25 us -> 54 us
  Pallas kernels: 0 us -> 12.8 us
  local copies, waits for them, and re-layouts: 10.9 us -> 2.28 us
  matrix products: 2.79 us -> 0 us
    reduce_scatter x1 -> x0, waiting for transfers between devices: 44.6 us -> none  [body(): mine = lax.psum_scatter(sums, 'z', scatter_dimension=0)]
    all_to_all x2, blocking collectives: 25 us -> 54 us  [the longest x1 37.7 us: body(): lax.all_to_all(sums.reshape(N_ZQ * N_GROUP, ROWS, OUTER), ('zq',) + GROUP...]
    pallas_call x0 -> x2, Pallas kernels: none -> 12.8 us  [the longest x1 6.55 us: partial_sums(): pl.pallas_call(sums_kernel, out_shape=out, grid_spec=pltpu.PrefetchScalar...]
    transpose x2 -> x0, local copies, waits for them, and re-layouts: 4.86 us -> none  [the longest x1 3.25 us: body(): sums.reshape(2, 2, 8, 2, 16, 512).transpose(2, 0, 1, 3, 4, 5)]
    dot_general x1 -> x0, matrix products: 2.79 us -> none  [body(): sums = jnp.einsum('xic,xac->ia', t, v, precision=lax.Precision.HIGH)]
    reshape x1 -> x0, local copies, waits for them, and re-layouts: 1.86 us -> none  [body(): t = t.reshape(2, 2, 2, 256, width)]
    dot_general x1 -> x0, local copies, waits for them, and re-layouts: 1.83 us -> none  [body(): sums = jnp.einsum('xic,xac->ia', t, v, precision=lax.Precision.HIGH)]
  transfers between devices with their start and end apart: 3 -> 2, of which waited for: 3 -> 2; matrix products, arithmetic and copies ran while one was open for 2% -> 0% of each run, Pallas kernels for 0% -> 5%
where the time goes in v5:
time: 132 us
  blocking collectives  54 us (41%)
  waiting for transfers between devices  42.1 us (32%)
  between operations  14.1 us (11%)
  Pallas kernels  12.8 us (10%)
  starting transfers between devices  4.51 us (3%)
  local copies, waits for them, and re-layouts  2.28 us (2%)
  other arithmetic  1.87 us (1%)
    all_to_all x1, blocking collectives, body(): lax.all_to_all(sums.reshape(N_ZQ * N_GROUP, ROWS, OUTER), ('zq',) + GROUP...  37.7 us
    all_to_all x1, waiting for transfers between devices, body(): th, tl = pairs(lax.all_to_all(amplitudes, GROUP, 0, 0, tiled=True))  33.3 us
    all_to_all x1, blocking collectives, body(): lax.all_to_all(jnp.concatenate([integrals, integrals]), ('xh',) + GROUP,...  16.3 us
    all_gather x1, waiting for transfers between devices, body(): v = lax.all_gather(v, 'y', axis=0)  8.12 us
    pallas_call x1, Pallas kernels, partial_sums(): pl.pallas_call(sums_kernel, out_shape=out, grid_spec=pltpu.PrefetchScalar...  6.55 us
    pallas_call x1, Pallas kernels, pairs(): pl.pallas_call(pair_kernel, out_shape=[jax.ShapeDtypeStruct((total, 4 * w...  6.27 us
    all_to_all x1, starting transfers between devices, body(): th, tl = pairs(lax.all_to_all(amplitudes, GROUP, 0, 0, tiled=True))  4.51 us
  transfers between devices with their start and end apart: 2, of which 2 were waited for; matrix products, arithmetic and copies ran while one was open for 0% of the time, Pallas kernels for 5%

profile of v5, /device:TPU:6, one launch (start us, length us, event | category | flops | bytes accessed | tf_op | source)
XLA Modules:
  0.0 131.7 jit_solution(2486210212594658211)
XLA Ops:
  6.5 1.0 pad_maximum_fusion
  7.6 16.3 %all_to_all.15 = f32[16,16,384]{2,1,0:T(8,128)} all-to-all(f32[16,16,384]{2,1,0:T(8,128)S(1)} %pad_maximum_fusion), channel_id=1, replica_groups=mesh['xh'=2,'y'=8,'core'=2,'zq'=4,'z0'=2,'xl'=2] {'xh','core','z0','xl'}, dimensions={0} | all-to-all | bytes 786432 | tf_op jit(solution)/shard_map/all_to_all | solution.py:83
  23.9 0.0 copy-start.2
  23.9 4.5 %all-to-all-start.1 = ((f32[8,256,384]{2,1,0:T(8,128)}), f32[8,256,384]{2,1,0:T(8,128)S(1)}, u32[]{:S(2)}, u32[]{:S(2)}) async-start(f32[8,256,384]{2,1,0:T(8,128)} %param.4), calls=%async_computation.1 | async-start | bytes 6291456 | tf_op jit(solution)/shard_map/all_to_all | solution.py:85
  28.4 0.0 all-gather.3.cloned.1.call-start
  28.4 0.7 all-gather.3.cloned.1.call-update
  29.1 0.0 copy-done.2
  29.1 0.6 dynamic_slice.3
  30.4 33.3 %all-to-all-done.1.t_ref = f32[8,256,384]{2,1,0:T(8,128)S(1)} async-done(((f32[8,256,384]{2,1,0:T(8,128)}), f32[8,256,384]{2,1,0:T(8,128)S(1)}, u32[]{:S(2)}, u32[]{:S(2)}) %all-to-all-start.1) | async-done | bytes 3145760 | tf_op jit(solution)/shard_map/all_to_all | solution.py:85
  63.7 0.0 copy-start
  63.7 1.7 %copy-done = f32[8,256,384]{2,1,0:T(8,128)} copy-done((f32[8,256,384]{2,1,0:T(8,128)}, f32[8,256,384]{2,1,0:T(8,128)S(1)}, u32[]{:S(2)}) %copy-start) | copy-done | bytes 3145752
  65.4 6.3 %shard_map.46 = (bf16[512,1536]{1,0:T(8,128)(2,1)}, bf16[512,1536]{1,0:T(8,128)(2,1)}) custom-call(f32[8,256,384]{2,1,0:T(8,128)} %copy-done), custom_call_target="tpu_custom_call" | custom-call | flops 2359296 | bytes 6291456 | tf_op jit(solution)/shard_map/pallas_call | solution.py:31
  71.6 8.1 %all-gather.3.cloned.1.call-done = f32[128,16,384]{2,1,0:T(8,128)} async-done(((f32[16,16,384]{2,1,0:T(8,128)}), f32[128,16,384]{2,1,0:T(8,128)}) %all-gather.3.cloned.1.call-update) | async-done | bytes 3145744 | tf_op jit(solution)/shard_map/all_gather | solution.py:84
  79.7 6.5 %shard_map.47 = f32[512,512]{1,0:T(8,128)} custom-call(s32[1]{0:T(128)} %bitcast.1.live, f32[8,16,16,384]{3,2,1,0:T(8,128)} %bitcast.7, bf16[512,1536]{1,0:T(8,128)(2,1)} %get-tuple-element.7.th, bf16[512,1536]{1,0:T(8,128)(2,1)} %get-tuple-element.8.tl), custom_call_target="tpu_custom_call" | custom-call | flops 2415919104 | bytes 8388608 | tf_op jit(solution)/shard_map/pallas_call | solution.py:64
  86.3 0.0 copy-start.1
  86.3 37.7 %all_to_all.16 = f32[32,16,512]{2,1,0:T(8,128)S(1)} all-to-all(f32[32,16,512]{2,1,0:T(8,128)} %bitcast.6), channel_id=1, replica_groups=mesh['xh'=2,'y'=8,'core'=2,'zq'=4,'z0'=2,'xl'=2] {'zq','core','z0','xl'}, dimensions={0} | all-to-all | bytes 2097152 | tf_op jit(solution)/shard_map/all_to_all | solution.py:88
  124.0 0.1 reduce_sum.9
  124.1 0.0 copy-done.1
  124.1 0.7 add.15
Async XLA Ops:
  23.9 5.2 %copy-start.2 = (s32[8]{0:T(128)S(1)}, s32[8]{0:T(128)}, u32[]{:S(2)}) copy-start(s32[8]{0:T(128)} %param.7) | copy-start | bytes 100
  23.9 39.8 %all-to-all-start.1 = ((f32[8,256,384]{2,1,0:T(8,128)}), f32[8,256,384]{2,1,0:T(8,128)S(1)}, u32[]{:S(2)}, u32[]{:S(2)}) async-start(f32[8,256,384]{2,1,0:T(8,128)} %param.4), calls=%async_computation.1 | async-start | bytes 6291456 | tf_op jit(solution)/shard_map/all_to_all | solution.py:85
  28.4 51.4 %all-gather.3.cloned.1.call-start = ((), (), s32[]{:S(2)}) async-start(), calls=%async_computation.3 | async-start | bytes 3538944 | tf_op jit(solution)/shard_map/all_gather | solution.py:84
  63.7 1.7 %copy-start = (f32[8,256,384]{2,1,0:T(8,128)}, f32[8,256,384]{2,1,0:T(8,128)S(1)}, u32[]{:S(2)}) copy-start(f32[8,256,384]{2,1,0:T(8,128)S(1)} %all-to-all-done.1.t_ref) | copy-start | bytes 9437188
  86.3 37.8 %copy-start.1 = (f32[8,16,512]{2,1,0:T(8,128)S(1)}, f32[8,16,512]{2,1,0:T(8,128)}, u32[]{:S(2)}) copy-start(f32[8,16,512]{2,1,0:T(8,128)} %param.6) | copy-start | bytes 786436
Sparse Core Ops, SparseCore 0:
  31.3 48.4 all-gather.2

commit v6 on v5

v6 whole, which is shorter than its diff:
```python
import functools

import jax
import jax.numpy as jnp
from jax import lax
from jax.experimental import pallas as pl
from jax.experimental.pallas import tpu as pltpu
from jax.sharding import Mesh, PartitionSpec as P

GROUP = ("xh", "z0", "xl")
N_Y, N_ZQ, N_GROUP = 8, 4, 8
ROWS = 16
OUTER = 512
HALF = OUTER // 2
STEPS = 2

DOT = functools.partial(
    lax.dot_general, dimension_numbers=(((1,), (1,)), ((), ())), preferred_element_type=jnp.float32
)


def split(x):
    high = x.astype(jnp.bfloat16)
    return high, (x - high.astype(jnp.float32)).astype(jnp.bfloat16)


def pair_kernel(live, t_ref, th, tl):
    rows, width = t_ref.shape[1:]
    slots = lax.broadcasted_iota(jnp.int32, (rows, width), 1)
    for g in range(N_GROUP):
        xh, c = divmod(g, 4)
        at = (slice(xh * rows, (xh + 1) * rows), slice(c * width, (c + 1) * width))
        th[at], tl[at] = split(jnp.where(slots + c * width < live[0], t_ref[g], 0.0))


def pairs(live, t):
    rows, width = t.shape[1] // N_ZQ, t.shape[2]
    total = 2 * t.shape[1]
    return pl.pallas_call(
        pair_kernel,
        out_shape=[pltpu.HBM((total, 4 * width), jnp.bfloat16)] * 2,
        grid_spec=pltpu.PrefetchScalarGridSpec(
            num_scalar_prefetch=1,
            grid=(N_ZQ,),
            in_specs=[pl.BlockSpec((N_GROUP, rows, width), lambda zq, m: (0, zq, 0))],
            out_specs=[pl.BlockSpec((2 * rows, 4 * width), lambda zq, m: (zq, 0))] * 2,
        ),
        compiler_params=pltpu.CompilerParams(vmem_limit_bytes=16 << 20),
        cost_estimate=pl.CostEstimate(flops=3 * t.size, bytes_accessed=8 * t.size, transcendentals=0),
    )(live, t)


def sums_kernel(core, v_ref, th, tl, *rest):
    out, vh, vl = rest[-3:]
    width = v_ref.shape[4]
    for c in range(v_ref.shape[2]):
        for y in range(N_Y):
            for xh in range(2):
                row = (xh * N_Y + y) * ROWS
                at = (slice(row, row + ROWS), slice(c * width, (c + 1) * width))
                vh[at], vl[at] = split(v_ref[y, xh, c])
    sums = DOT(th[...], vh[...]) + (DOT(tl[...], vh[...]) + DOT(th[...], vl[...]))

    @pl.when(pl.program_id(0) == 0)
    def _():
        out[...] = sums

    @pl.when(pl.program_id(0) > 0)
    def _():
        out[...] += sums


def partial_sums(core, v, th, tl, into=None):
    width = v.shape[3]
    depth = 4 // STEPS
    v = v.reshape(N_Y, 2, 4, ROWS, width)
    total = th.shape[0]
    t_spec = pl.BlockSpec((total, depth * width), lambda k, m: (0, k))
    arrays = [core, v, th, tl] + ([] if into is None else [into])
    return pl.pallas_call(
        sums_kernel,
        out_shape=jax.ShapeDtypeStruct((total, OUTER), jnp.float32),
        grid_spec=pltpu.PrefetchScalarGridSpec(
            num_scalar_prefetch=1,
            grid=(STEPS,),
            in_specs=[pl.BlockSpec((N_Y, 2, depth, ROWS, width), lambda k, m: (0, 0, k, 0, 0)), t_spec, t_spec]
            + [pl.BlockSpec(memory_space=pl.ANY)] * (len(arrays) - 4),
            out_specs=pl.BlockSpec((total, HALF), lambda k, m: (0, m[0])),
            scratch_shapes=[pltpu.VMEM((HALF, depth * width), jnp.bfloat16)] * 2,
        ),
        input_output_aliases={} if into is None else {4: 0},
        compiler_params=pltpu.CompilerParams(vmem_limit_bytes=60 << 20),
        cost_estimate=pl.CostEstimate(flops=6 * th.size * HALF, bytes_accessed=8 << 20, transcendentals=0),
    )(*arrays)


def finish_kernel(parts, residual, out):
    ladder = (parts[0] + parts[1]) + (parts[2] + parts[3])
    to = lax.broadcasted_iota(jnp.int32, (OUTER, OUTER), 0)
    source = lax.broadcasted_iota(jnp.int32, (OUTER, OUTER), 1)
    wanted = ((to >> 4) & 1) * HALF + (to >> 5) * ROWS + (to & (ROWS - 1))
    order = jnp.where(source == wanted, 1.0, 0.0).astype(jnp.bfloat16)
    first, _ = split(ladder)
    rest = ladder - first.astype(jnp.float32)
    second, third = split(rest)
    out[...] = residual[...] + (DOT(first, order) + (DOT(second, order) + DOT(third, order)))


def finish(parts, residual):
    shape = residual.shape
    parts = parts.reshape(N_ZQ, N_GROUP * ROWS, OUTER)
    residual = residual.reshape(N_GROUP * ROWS, OUTER)
    out = pl.pallas_call(
        finish_kernel,
        out_shape=jax.ShapeDtypeStruct(residual.shape, residual.dtype),
        compiler_params=pltpu.CompilerParams(vmem_limit_bytes=32 << 20),
        cost_estimate=pl.CostEstimate(flops=6 * residual.size * OUTER, bytes_accessed=24 * residual.size, transcendentals=0),
    )(parts, residual)
    return out.reshape(shape)


def body(amplitudes, integrals, residual_in, cd_count):
    width = amplitudes.shape[2]
    live = cd_count[lax.axis_index(GROUP)] - lax.axis_index("zq") * (4 * width)
    core = lax.axis_index("core").astype(jnp.int32)

    v = lax.all_to_all(integrals, GROUP, 0, 0, tiled=True)
    v = lax.all_gather(v, "y", axis=0)
    t = lax.all_to_all(amplitudes, GROUP, 0, 0, tiled=True)
    th, tl = pairs(live[None].astype(jnp.int32), t)
    v, th, tl = lax.optimization_barrier((v, th, tl))
    other = lax.ppermute(v, "core", [(0, 1), (1, 0)])

    sums = partial_sums(core[None], v, th, tl)
    sums = partial_sums(1 - core[None], other, th, tl, sums)
    parts = lax.all_to_all(sums.reshape(N_ZQ * N_GROUP, ROWS, OUTER), ("zq",) + GROUP, 0, 0, tiled=True)
    return finish(parts, residual_in)


def solution(mesh):
    mesh = Mesh(mesh.devices.reshape(2, 8, 2, 4, 2, 2), ("xh", "y", "core", "zq", "z0", "xl"))
    row, col = ("xh", "y", "core"), ("zq", "z0", "xl")
    in_specs = (P(None, row, col), P(None, row, col), P(None, row + col, None), P())
    return jax.shard_map(body, mesh=mesh, in_specs=in_specs, out_specs=P(None, row + col, None), check_vma=False)
```

time: 132 us -> 133 us (level)
  starting transfers between devices: 4.51 us -> 8.22 us
  other arithmetic: 1.87 us -> 0 us
    ppermute x0 -> x1, starting transfers between devices: none -> 1.91 us  [body(): other = lax.ppermute(v, 'core', [(0, 1), (1, 0)])]
    all_to_all x1, starting transfers between devices: 4.51 us -> 6.31 us  [body(): t = lax.all_to_all(amplitudes, GROUP, 0, 0, tiled=True)]
    all_to_all x1, blocking collectives: 16.3 us -> 14.5 us  [body(): v = lax.all_to_all(integrals, GROUP, 0, 0, tiled=True)]
    all_to_all x1, blocking collectives: 37.7 us -> 39.4 us  [body(): lax.all_to_all(sums.reshape(N_ZQ * N_GROUP, ROWS, OUTER), ('zq',) + GROUP...]
    pallas_call x2 -> x4, Pallas kernels: 12.8 us -> 12.3 us  [the longest x2 8.46 us: partial_sums(): pl.pallas_call(sums_kernel, out_shape=jax.ShapeDtypeStruct((total, OUTER)...]
  transfers between devices with their start and end apart: 2 -> 3, of which waited for: 2 -> 2; matrix products, arithmetic and copies ran while one was open for 0% -> 0% of each run, Pallas kernels for 5% -> 5%
where the time goes in v6:
time: 133 us; the launch traced here: 132 us
  blocking collectives  53.8 us (40%)
  waiting for transfers between devices  42.3 us (32%)
  between operations  14.1 us (11%)
  Pallas kernels  12.3 us (9%)
  starting transfers between devices  8.22 us (6%)
  local copies, waits for them, and re-layouts  1.75 us (1%)
    all_to_all x1, blocking collectives, body(): lax.all_to_all(sums.reshape(N_ZQ * N_GROUP, ROWS, OUTER), ('zq',) + GROUP...  39.4 us
    all_to_all x1, waiting for transfers between devices, body(): t = lax.all_to_all(amplitudes, GROUP, 0, 0, tiled=True)  32.8 us
    all_to_all x1, blocking collectives, body(): v = lax.all_to_all(integrals, GROUP, 0, 0, tiled=True)  14.5 us
    all_gather x1, waiting for transfers between devices, body(): v = lax.all_gather(v, 'y', axis=0)  8.72 us
    pallas_call x2, Pallas kernels, partial_sums(): pl.pallas_call(sums_kernel, out_shape=jax.ShapeDtypeStruct((total, OUTER)...  8.46 us
    all_to_all x1, starting transfers between devices, body(): t = lax.all_to_all(amplitudes, GROUP, 0, 0, tiled=True)  6.31 us
  transfers between devices with their start and end apart: 3, of which 2 were waited for; matrix products, arithmetic and copies ran while one was open for 0% of the time, Pallas kernels for 5%

profile of v6, /device:TPU:6, one launch (start us, length us, event | category | flops | bytes accessed | tf_op | source)
XLA Modules:
  0.0 132.5 jit_solution(13895850465390722472)
XLA Ops:
  6.5 14.5 %all_to_all.15 = f32[8,16,384]{2,1,0:T(8,128)} all-to-all(f32[8,16,384]{2,1,0:T(8,128)} %param.5), channel_id=1, replica_groups=mesh['xh'=2,'y'=8,'core'=2,'zq'=4,'z0'=2,'xl'=2] {'xh','z0','xl'}, dimensions={0} | all-to-all | bytes 393216 | tf_op jit(solution)/shard_map/all_to_all | solution.py:127
  21.0 0.0 copy-start.2
  21.0 6.3 %all-to-all-start.1 = ((f32[8,256,384]{2,1,0:T(8,128)}), f32[8,256,384]{2,1,0:T(8,128)S(1)}, u32[]{:S(2)}, u32[]{:S(2)}) async-start(f32[8,256,384]{2,1,0:T(8,128)} %param.4), calls=%async_computation.1 | async-start | bytes 6291456 | tf_op jit(solution)/shard_map/all_to_all | solution.py:129
  27.3 0.0 all-gather.3.cloned.1.call-start
  27.3 0.7 all-gather.3.cloned.1.call-update
  28.1 0.0 copy-done.2
  28.1 0.6 dynamic_slice.3
  29.3 32.8 %all-to-all-done.1.t_ref = f32[8,256,384]{2,1,0:T(8,128)S(1)} async-done(((f32[8,256,384]{2,1,0:T(8,128)}), f32[8,256,384]{2,1,0:T(8,128)S(1)}, u32[]{:S(2)}, u32[]{:S(2)}) %all-to-all-start.1) | async-done | bytes 3145760 | tf_op jit(solution)/shard_map/all_to_all | solution.py:129
  62.1 2.4 %shard_map.46 = (bf16[512,1536]{1,0:T(8,128)(2,1)}, bf16[512,1536]{1,0:T(8,128)(2,1)}) custom-call(s32[1]{0:T(128)} %bitcast.3.live, f32[8,256,384]{2,1,0:T(8,128)S(1)} %all-to-all-done.1.t_ref), custom_call_target="tpu_custom_call" | custom-call | flops 2359296 | bytes 6291456 | tf_op jit(solution)/shard_map/pallas_call | solution.py:39
  64.6 8.7 %all-gather.3.cloned.1.call-done = f32[64,16,384]{2,1,0:T(8,128)} async-done(((f32[8,16,384]{2,1,0:T(8,128)}), f32[64,16,384]{2,1,0:T(8,128)}) %all-gather.3.cloned.1.call-update) | async-done | bytes 1572880 | tf_op jit(solution)/shard_map/all_gather | solution.py:128
  73.3 1.9 %collective-permute-start = (f32[8,8,16,384]{3,2,1,0:T(8,128)}, f32[8,8,16,384]{3,2,1,0:T(8,128)S(1)}, u32[]{:S(2)}, u32[]{:S(2)}) collective-permute-start(f32[8,8,16,384]{3,2,1,0:T(8,128)} %bitcast.13), channel_id=1, source_target_pairs={{0,16},{16,0},{1,17},{17,1},{2,18},{18,2},{3,19},{19,3},{4,20},{20... | collective-permute-start | bytes 4718600 | tf_op jit(solution)/shard_map/ppermute | solution.py:132
  75.2 4.2 %shard_map.47.rest_0_ = f32[512,512]{1,0:T(8,128)} custom-call(s32[1]{0:T(128)} %bitcast.core, f32[8,2,4,16,384]{4,3,2,1,0:T(8,128)} %bitcast.14, bf16[512,1536]{1,0:T(8,128)(2,1)} %get-tuple-element.13.th, bf16[512,1536]{1,0:T(8,128)(2,1)} %get-tuple-element.14.tl), custom_call_target="tpu_custom_call" | custom-call | flops 1207959552 | bytes 8388608 | tf_op jit(solution)/shard_map/pallas_call | solution.py:80
  79.5 0.0 collective-permute-done
  79.5 0.0 copy-start.1
  79.5 1.2 copy-done.1
  80.6 4.2 %shard_map.48 = f32[512,512]{1,0:T(8,128)} custom-call(s32[1]{0:T(128)S(6)} %sub.6.core, f32[8,2,4,16,384]{4,3,2,1,0:T(8,128)} %bitcast.15, bf16[512,1536]{1,0:T(8,128)(2,1)} %get-tuple-element.13.th, bf16[512,1536]{1,0:T(8,128)(2,1)} %get-tuple-element.14.tl, f32[512,512]{1,0:T(8,128)} %shard_map.47.rest_0_), custom_call_target="tpu_custom_call", output_to_operand_aliasing={{}: (4, {})} | custom-call | flops 1207959552 | bytes 8388608 | tf_op jit(solution)/shard_map/pallas_call | solution.py:80
  84.8 0.0 copy-start
  84.8 39.4 %all_to_all.16 = f32[32,16,512]{2,1,0:T(8,128)S(1)} all-to-all(f32[32,16,512]{2,1,0:T(8,128)} %bitcast.12), channel_id=1, replica_groups=mesh['xh'=2,'y'=8,'core'=2,'zq'=4,'z0'=2,'xl'=2] {'zq','xh','z0','xl'}, dimensions={0} | all-to-all | bytes 2097152 | tf_op jit(solution)/shard_map/all_to_all | solution.py:136
  124.2 0.0 copy-done
  124.2 1.4 %shard_map.49 = f32[128,512]{1,0:T(8,128)} custom-call(f32[4,128,512]{2,1,0:T(8,128)S(1)} %bitcast.10, f32[128,512]{1,0:T(8,128)S(1)} %bitcast.11), custom_call_target="tpu_custom_call" | custom-call | flops 201326592 | bytes 1572864 | tf_op jit(solution)/shard_map/pallas_call | solution.py:113
Async XLA Ops:
  21.0 7.1 %copy-start.2 = (s32[8]{0:T(128)S(1)}, s32[8]{0:T(128)}, u32[]{:S(2)}) copy-start(s32[8]{0:T(128)} %param.7) | copy-start | bytes 100
  21.0 41.1 %all-to-all-start.1 = ((f32[8,256,384]{2,1,0:T(8,128)}), f32[8,256,384]{2,1,0:T(8,128)S(1)}, u32[]{:S(2)}, u32[]{:S(2)}) async-start(f32[8,256,384]{2,1,0:T(8,128)} %param.4), calls=%async_computation.1 | async-start | bytes 6291456 | tf_op jit(solution)/shard_map/all_to_all | solution.py:129
  27.3 46.0 %all-gather.3.cloned.1.call-start = ((), (), s32[]{:S(2)}) async-start(), calls=%async_computation.3 | async-start | bytes 1769472 | tf_op jit(solution)/shard_map/all_gather | solution.py:128
  73.3 6.2 %collective-permute-start = (f32[8,8,16,384]{3,2,1,0:T(8,128)}, f32[8,8,16,384]{3,2,1,0:T(8,128)S(1)}, u32[]{:S(2)}, u32[]{:S(2)}) collective-permute-start(f32[8,8,16,384]{3,2,1,0:T(8,128)} %bitcast.13), channel_id=1, source_target_pairs={{0,16},{16,0},{1,17},{17,1},{2,18},{18,2},{3,19},{19,3},{4,20},{20... | collective-permute-start | bytes 4718600 | tf_op jit(solution)/shard_map/ppermute | solution.py:132
  79.5 1.2 copy-start.1
  84.8 39.4 %copy-start = (f32[8,16,512]{2,1,0:T(8,128)S(1)}, f32[8,16,512]{2,1,0:T(8,128)}, u32[]{:S(2)}) copy-start(f32[8,16,512]{2,1,0:T(8,128)} %param.6) | copy-start | bytes 786436
Sparse Core Ops, SparseCore 0:
  30.2 43.0 all-gather.2

commit v7 on v6

v7 whole, which is shorter than its diff:
```python
import functools

import jax
import jax.numpy as jnp
from jax import lax
from jax.experimental import pallas as pl
from jax.experimental.pallas import tpu as pltpu
from jax.sharding import Mesh, PartitionSpec as P

GROUP = ("core", "z0", "xl")
N_Y, N_ZQ, N_GROUP = 8, 4, 8
ROWS = 16
OUTER = 512
STEPS = 2


def split(x):
    high = x.astype(jnp.bfloat16)
    return high, (x - high.astype(jnp.float32)).astype(jnp.bfloat16)


def pair_kernel(live, t_ref, th, tl):
    rows, width = t_ref.shape[1:]
    slots = lax.broadcasted_iota(jnp.int32, (rows, width), 1)
    for g in range(N_GROUP):
        core, c = divmod(g, 4)
        at = (slice(core * rows, (core + 1) * rows), slice(c * width, (c + 1) * width))
        th[at], tl[at] = split(jnp.where(slots + c * width < live[0], t_ref[g], 0.0))


def pairs(live, t):
    rows, width = t.shape[1] // N_ZQ, t.shape[2]
    total = 2 * t.shape[1]
    return pl.pallas_call(
        pair_kernel,
        out_shape=[pltpu.HBM((total, 4 * width), jnp.bfloat16)] * 2,
        grid_spec=pltpu.PrefetchScalarGridSpec(
            num_scalar_prefetch=1,
            grid=(N_ZQ,),
            in_specs=[pl.BlockSpec((N_GROUP, rows, width), lambda zq, m: (0, zq, 0))],
            out_specs=[pl.BlockSpec((2 * rows, 4 * width), lambda zq, m: (zq, 0))] * 2,
        ),
        compiler_params=pltpu.CompilerParams(vmem_limit_bytes=16 << 20),
        cost_estimate=pl.CostEstimate(flops=3 * t.size, bytes_accessed=8 * t.size, transcendentals=0),
    )(live, t)


NEAR = ((0, (0, 1)), (-1, (0, 1)), (1, (0, 1)), (-2, (0, 1)), (2, (0, 1)), (-3, (0, 1)), (3, (0, 1)), (4, (0,)), (4, (1,)))


def sums_kernel(ys, v_ref, *rest):
    near_refs, (th, tl, out, vh, vl) = rest[: len(NEAR)], rest[len(NEAR) :]
    depth, width = v_ref.shape[2], v_ref.shape[4]
    for c in range(depth):
        columns = slice(c * width, (c + 1) * width)
        for y in range(N_Y):
            for core in range(2):
                rows = slice((y * 2 + core) * ROWS, (y * 2 + core + 1) * ROWS)
                vh[rows, columns], vl[rows, columns] = split(v_ref[y, core, c])
        for i, (near_ref, (_, cores)) in enumerate(zip(near_refs, NEAR)):
            for j, core in enumerate(cores):
                start = pl.multiple_of(OUTER // 2 + ys[i] * (2 * ROWS) + core * ROWS, ROWS)
                rows = pl.ds(start, ROWS)
                vh[rows, columns], vl[rows, columns] = split(near_ref[j, c])
    dot = functools.partial(
        lax.dot_general, dimension_numbers=(((1,), (1,)), ((), ())), preferred_element_type=jnp.float32
    )
    sums = dot(th[...], vh[...]) + (dot(tl[...], vh[...]) + dot(th[...], vl[...]))

    @pl.when(pl.program_id(0) == 0)
    def _():
        out[...] = sums

    @pl.when(pl.program_id(0) > 0)
    def _():
        out[...] += sums


def partial_sums(ys, v, near, th, tl):
    width = v.shape[3]
    depth = 4 // STEPS
    v = v.reshape(N_Y, 2, 4, ROWS, width)
    near = [x.reshape(-1, 4, ROWS, width) for x in near]
    total = th.shape[0]
    t_spec = pl.BlockSpec((total, depth * width), lambda k, m: (0, k))
    return pl.pallas_call(
        sums_kernel,
        out_shape=jax.ShapeDtypeStruct((total, OUTER), jnp.float32),
        grid_spec=pltpu.PrefetchScalarGridSpec(
            num_scalar_prefetch=1,
            grid=(STEPS,),
            in_specs=[pl.BlockSpec((N_Y, 2, depth, ROWS, width), lambda k, m: (0, 0, k, 0, 0))]
            + [pl.BlockSpec((x.shape[0], depth, ROWS, width), lambda k, m: (0, k, 0, 0)) for x in near]
            + [t_spec, t_spec],
            out_specs=pl.BlockSpec((total, OUTER), lambda k, m: (0, 0)),
            scratch_shapes=[pltpu.VMEM((OUTER, depth * width), jnp.bfloat16)] * 2,
        ),
        compiler_params=pltpu.CompilerParams(vmem_limit_bytes=60 << 20),
        cost_estimate=pl.CostEstimate(flops=6 * th.size * OUTER, bytes_accessed=8 << 20, transcendentals=0),
    )(ys, v, *near, th, tl)


def along_y(x, by):
    return lax.ppermute(x, "y", [(i, (i + by) % N_Y) for i in range(N_Y)])


def gather_by_steps(own):
    down2, up2 = along_y(own, 2), along_y(own, -2)
    down1, up1 = along_y(own, 1), along_y(own, -1)
    down3, up3 = along_y(down2, 1), along_y(up2, -1)
    half = N_GROUP // 2
    down4, up4 = along_y(down2[:half], 2), along_y(up2[half:], -2)
    return [own, down1, up1, down2, up2, down3, up3, down4, up4]


def body(amplitudes, integrals, residual_in, cd_count):
    width = amplitudes.shape[2]
    live = cd_count[lax.axis_index(GROUP)] - lax.axis_index("zq") * (4 * width)

    both = jnp.broadcast_to(integrals[None], (2,) + integrals.shape).reshape(2 * N_GROUP, ROWS, width)
    v = lax.all_to_all(both, ("xh",) + GROUP, 0, 0, tiled=True)
    t = lax.all_to_all(amplitudes, GROUP, 0, 0, tiled=True)
    near = gather_by_steps(v[N_GROUP:])
    v = lax.all_gather(v[:N_GROUP], "y", axis=0)
    th, tl = pairs(live[None].astype(jnp.int32), t)

    offsets = jnp.array([near_y for near_y, _ in NEAR], jnp.int32)
    ys = (lax.axis_index("y").astype(jnp.int32) + N_Y + offsets) % N_Y
    sums = partial_sums(ys, v, near, th, tl)
    parts = lax.all_to_all(sums.reshape(N_ZQ * N_GROUP, ROWS, OUTER), ("zq",) + GROUP, 0, 0, tiled=True)
    return residual_in + jnp.sum(parts.reshape(N_ZQ, N_GROUP, ROWS, OUTER), axis=0)


def solution(mesh):
    mesh = Mesh(mesh.devices.reshape(2, 8, 2, 4, 2, 2), ("xh", "y", "core", "zq", "z0", "xl"))
    row, col = ("xh", "y", "core"), ("zq", "z0", "xl")
    in_specs = (P(None, row, col), P(None, row, col), P(None, row + col, None), P())
    return jax.shard_map(body, mesh=mesh, in_specs=in_specs, out_specs=P(None, row + col, None), check_vma=False)
```

time: 133 us -> 133 us (level)
  waiting for transfers between devices: 42.3 us -> 15.4 us
  starting transfers between devices: 8.22 us -> 33.5 us
  Pallas kernels: 12.3 us -> 9.44 us
  local copies, waits for them, and re-layouts: 1.75 us -> 3.29 us
  other arithmetic: 0 us -> 1.38 us
    all_to_all x1, waiting for transfers between devices: 32.8 us -> 2.13 us  [body(): t = lax.all_to_all(amplitudes, GROUP, 0, 0, tiled=True)]
    ppermute x1 -> x8, starting transfers between devices: 1.91 us -> 29 us  [along_y(): return lax.ppermute(x, 'y', [(i, (i + by) % N_Y) for i in range(N_Y)])]
    ppermute x1 -> x8, waiting for transfers between devices: 0.01 us -> 5.3 us  [along_y(): return lax.ppermute(x, 'y', [(i, (i + by) % N_Y) for i in range(N_Y)])]
    all_to_all x1, starting transfers between devices: 6.31 us -> 4.51 us  [body(): t = lax.all_to_all(amplitudes, GROUP, 0, 0, tiled=True)]
    slice x0 -> x3, local copies, waits for them, and re-layouts: none -> 1.69 us  [the longest x2 0.91 us: gather_by_steps(): down4, up4 = (along_y(down2[:half], 2), along_y(up2[half:], -2))]
    pallas_call x2 -> x1, Pallas kernels: 8.46 us -> 6.94 us  [partial_sums(): pl.pallas_call(sums_kernel, out_shape=jax.ShapeDtypeStruct((total, OUTER)...]
    pallas_call x1 -> x0, Pallas kernels: 1.41 us -> none  [finish(): pl.pallas_call(finish_kernel, out_shape=jax.ShapeDtypeStruct(residual.sha...]
  transfers between devices with their start and end apart: 3 -> 10, of which waited for: 2 -> 5; matrix products, arithmetic and copies ran while one was open for 0% -> 2% of each run, Pallas kernels for 5% -> 2%
where the time goes in v7:
time: 133 us; the launch traced here: 132 us
  blocking collectives  54.7 us (41%)
  starting transfers between devices  33.5 us (25%)
  waiting for transfers between devices  15.4 us (12%)
  between operations  14.2 us (11%)
  Pallas kernels  9.44 us (7%)
  local copies, waits for them, and re-layouts  3.29 us (2%)
  other arithmetic  1.38 us (1%)
    all_to_all x1, blocking collectives, body(): lax.all_to_all(sums.reshape(N_ZQ * N_GROUP, ROWS, OUTER), ('zq',) + GROUP...  39.1 us
    ppermute x8, starting transfers between devices, along_y(): return lax.ppermute(x, 'y', [(i, (i + by) % N_Y) for i in range(N_Y)])  29 us
    all_to_all x1, blocking collectives, body(): v = lax.all_to_all(both, ('xh',) + GROUP, 0, 0, tiled=True)  15.6 us
    all_gather x1, waiting for transfers between devices, body(): v = lax.all_gather(v[:N_GROUP], 'y', axis=0)  7.98 us
    pallas_call x1, Pallas kernels, partial_sums(): pl.pallas_call(sums_kernel, out_shape=jax.ShapeDtypeStruct((total, OUTER)...  6.94 us
    ppermute x8, waiting for transfers between devices, along_y(): return lax.ppermute(x, 'y', [(i, (i + by) % N_Y) for i in range(N_Y)])  5.3 us
    all_to_all x1, starting transfers between devices, body(): t = lax.all_to_all(amplitudes, GROUP, 0, 0, tiled=True)  4.51 us
  transfers between devices with their start and end apart: 10, of which 5 were waited for; matrix products, arithmetic and copies ran while one was open for 2% of the time, Pallas kernels for 2%

profile of v7, /device:TPU:6, one launch (start us, length us, event | category | flops | bytes accessed | tf_op | source)
XLA Modules:
  0.0 131.9 jit_solution(4145889950422876310)
XLA Ops:
  6.5 1.0 broadcast_in_dim.4
  7.5 15.6 %all_to_all.15 = f32[16,16,384]{2,1,0:T(8,128)S(1)} all-to-all(f32[16,16,384]{2,1,0:T(8,128)S(1)} %bitcast.16), channel_id=1, replica_groups=mesh['xh'=2,'y'=8,'core'=2,'zq'=4,'z0'=2,'xl'=2] {'xh','core','z0','xl'}, dimensions={0} | all-to-all | bytes 786432 | tf_op jit(solution)/shard_map/all_to_all | solution.py:121
  23.1 4.5 %all-to-all-start.1 = ((f32[8,256,384]{2,1,0:T(8,128)}), f32[8,256,384]{2,1,0:T(8,128)S(1)}, u32[]{:S(2)}, u32[]{:S(2)}) async-start(f32[8,256,384]{2,1,0:T(8,128)} %param.5), calls=%async_computation.1 | async-start | bytes 6291456 | tf_op jit(solution)/shard_map/all_to_all | solution.py:122
  27.6 0.8 fusion.1
  28.4 0.0 all-gather.3.cloned.1.call-update
  28.4 4.2 %collective-permute-start.3 = (f32[8,16,384]{2,1,0:T(8,128)}, f32[8,16,384]{2,1,0:T(8,128)S(1)}, u32[]{:S(2)}, u32[]{:S(2)}) collective-permute-start(f32[8,16,384]{2,1,0:T(8,128)} %get-tuple-element.9), channel_id=1, source_target_pairs={{0,192},{32,224},{64,0},{96,32},{128,64},{160,96},{192,128},{224,1... | collective-permute-start | bytes 589832 | tf_op jit(solution)/shard_map/ppermute | solution.py:104
  32.6 2.5 %collective-permute-start.2 = (f32[8,16,384]{2,1,0:T(8,128)}, f32[8,16,384]{2,1,0:T(8,128)}, u32[]{:S(2)}, u32[]{:S(2)}) collective-permute-start(f32[8,16,384]{2,1,0:T(8,128)} %get-tuple-element.9), channel_id=1, source_target_pairs={{0,64},{32,96},{64,128},{96,160},{128,192},{160,224},{192,0},{224,... | collective-permute-start | bytes 589832 | tf_op jit(solution)/shard_map/ppermute | solution.py:104
  35.2 4.6 %collective-permute-start.1 = (f32[8,16,384]{2,1,0:T(8,128)}, f32[8,16,384]{2,1,0:T(8,128)}, u32[]{:S(2)}, u32[]{:S(2)}) collective-permute-start(f32[8,16,384]{2,1,0:T(8,128)} %get-tuple-element.9), channel_id=1, source_target_pairs={{0,224},{32,0},{64,32},{96,64},{128,96},{160,128},{192,160},{224,1... | collective-permute-start | bytes 589832 | tf_op jit(solution)/shard_map/ppermute | solution.py:104
  39.8 1.9 %collective-permute-start = (f32[8,16,384]{2,1,0:T(8,128)}, f32[8,16,384]{2,1,0:T(8,128)}, u32[]{:S(2)}, u32[]{:S(2)}) collective-permute-start(f32[8,16,384]{2,1,0:T(8,128)} %get-tuple-element.9), channel_id=1, source_target_pairs={{0,32},{32,64},{64,96},{96,128},{128,160},{160,192},{192,224},{224... | collective-permute-start | bytes 589832 | tf_op jit(solution)/shard_map/ppermute | solution.py:104
  41.8 0.1 collective-permute-done.3
  41.8 5.5 %collective-permute-start.7 = (f32[4,16,384]{2,1,0:T(8,128)S(1)}, f32[4,16,384]{2,1,0:T(8,128)}, u32[]{:S(2)}, u32[]{:S(2)}) collective-permute-start(f32[4,16,384]{2,1,0:T(8,128)S(1)} %slice.19), channel_id=1, source_target_pairs={{0,192},{32,224},{64,0},{96,32},{128,64},{160,96},{192,128},{224,1... | collective-permute-start | bytes 294920 | tf_op jit(solution)/shard_map/ppermute | solution.py:104
  47.4 0.5 collective-permute-done.2
  47.8 0.9 slice.18
  48.7 1.9 %collective-permute-start.6 = (f32[4,16,384]{2,1,0:T(8,128)S(1)}, f32[4,16,384]{2,1,0:T(8,128)}, u32[]{:S(2)}, u32[]{:S(2)}) collective-permute-start(f32[4,16,384]{2,1,0:T(8,128)S(1)} %slice.18), channel_id=1, source_target_pairs={{0,64},{32,96},{64,128},{96,160},{128,192},{160,224},{192,0},{224,... | collective-permute-start | bytes 294920 | tf_op jit(solution)/shard_map/ppermute | solution.py:104
  50.7 6.3 %collective-permute-start.5 = (f32[8,16,384]{2,1,0:T(8,128)S(1)}, f32[8,16,384]{2,1,0:T(8,128)}, u32[]{:S(2)}, u32[]{:S(2)}) collective-permute-start(f32[8,16,384]{2,1,0:T(8,128)S(1)} %collective-permute-done.3), channel_id=1, source_target_pairs={{0,224},{32,0},{64,32},{96,64},{128,96},{160,128},{192,160},{224,1... | collective-permute-start | bytes 589832 | tf_op jit(solution)/shard_map/ppermute | solution.py:104
  57.0 0.0 collective-permute-done.1
  57.0 1.9 %collective-permute-start.4 = (f32[8,16,384]{2,1,0:T(8,128)}, f32[8,16,384]{2,1,0:T(8,128)}, u32[]{:S(2)}, u32[]{:S(2)}) collective-permute-start(f32[8,16,384]{2,1,0:T(8,128)} %collective-permute-done.2), channel_id=1, source_target_pairs={{0,32},{32,64},{64,96},{96,128},{128,160},{160,192},{192,224},{224... | collective-permute-start | bytes 589832 | tf_op jit(solution)/shard_map/ppermute | solution.py:104
  59.0 0.5 and_select_fusion.ys
  59.5 0.6 dynamic_slice.3
  60.8 2.1 %all-to-all-done.1.t_ref = f32[8,256,384]{2,1,0:T(8,128)S(1)} async-done(((f32[8,256,384]{2,1,0:T(8,128)}), f32[8,256,384]{2,1,0:T(8,128)S(1)}, u32[]{:S(2)}, u32[]{:S(2)}) %all-to-all-start.1) | async-done | bytes 3145760 | tf_op jit(solution)/shard_map/all_to_all | solution.py:122
  62.9 2.5 %shard_map.55 = (bf16[512,1536]{1,0:T(8,128)(2,1)}, bf16[512,1536]{1,0:T(8,128)(2,1)}) custom-call(s32[1]{0:T(128)} %bitcast.12.live, f32[8,256,384]{2,1,0:T(8,128)S(1)} %all-to-all-done.1.t_ref), custom_call_target="tpu_custom_call" | custom-call | flops 2359296 | bytes 6291456 | tf_op jit(solution)/shard_map/pallas_call | solution.py:34
  65.4 0.0 copy-done.1
  65.4 0.0 collective-permute-done
  65.4 0.0 collective-permute-done.7
  65.4 0.0 collective-permute-done.6
  65.4 0.0 collective-permute-done.5
  65.4 4.8 %collective-permute-done.4 = f32[8,16,384]{2,1,0:T(8,128)} collective-permute-done((f32[8,16,384]{2,1,0:T(8,128)}, f32[8,16,384]{2,1,0:T(8,128)}, u32[]{:S(2)}, u32[]{:S(2)}) %collective-permute-start.4) | collective-permute-done | bytes 196640 | tf_op jit(solution)/shard_map/ppermute | solution.py:104
  70.2 8.0 %all-gather.3.cloned.1.call-done = f32[64,16,384]{2,1,0:T(8,128)} async-done(((f32[8,16,384]{2,1,0:T(8,128)}), f32[64,16,384]{2,1,0:T(8,128)}) %all-gather.3.cloned.1.call-update) | async-done | bytes 1572880 | tf_op jit(solution)/shard_map/all_gather | solution.py:124
  78.2 6.9 %shard_map.56 = f32[512,512]{1,0:T(8,128)} custom-call(s32[9]{0:T(128)} %and_select_fusion.ys, f32[8,2,4,16,384]{4,3,2,1,0:T(8,128)} %bitcast.20, f32[2,4,16,384]{3,2,1,0:T(8,128)} %bitcast.18, f32[2,4,16,384]{3,2,1,0:T(8,128)} %bitcast.3.rest_1_, f32[2,4,16,384]{3,2,1,0:T(8,128)} %bitcast.4.rest_2_, f32[2,4,16,384]{3,2,1,0:T(8,128)} %bitcast.5.rest_3_, ...), custom_call_target="tpu_custom_call" | custom-call | flops 2415919104 | bytes 8388608 | tf_op jit(solution)/shard_map/pallas_call | solution.py:86
  85.1 39.1 %all_to_all.16 = f32[32,16,512]{2,1,0:T(8,128)S(1)} all-to-all(f32[32,16,512]{2,1,0:T(8,128)} %bitcast.17), channel_id=1, replica_groups=mesh['xh'=2,'y'=8,'core'=2,'zq'=4,'z0'=2,'xl'=2] {'zq','core','z0','xl'}, dimensions={0} | all-to-all | bytes 2097152 | tf_op jit(solution)/shard_map/all_to_all | solution.py:130
  124.2 0.1 reduce_sum.9
  124.4 0.7 add.34
  (9 shorter events, 0.0 us)
Async XLA Ops:
  23.1 35.8 %copy-start.3 = (s32[9]{0:T(128)S(1)}, s32[9]{0:T(128)}, u32[]{:S(2)}) copy-start(s32[9]{0:T(128)} %constant.47.clone) | copy-start | bytes 112
  23.1 36.4 %copy-start.2 = (s32[8]{0:T(128)S(1)}, s32[8]{0:T(128)}, u32[]{:S(2)}) copy-start(s32[8]{0:T(128)} %param.8) | copy-start | bytes 100
  23.1 39.8 %all-to-all-start.1 = ((f32[8,256,384]{2,1,0:T(8,128)}), f32[8,256,384]{2,1,0:T(8,128)S(1)}, u32[]{:S(2)}, u32[]{:S(2)}) async-start(f32[8,256,384]{2,1,0:T(8,128)} %param.5), calls=%async_computation.1 | async-start | bytes 6291456 | tf_op jit(solution)/shard_map/all_to_all | solution.py:122
  27.6 50.6 %all-gather.3.cloned.1.call-start = ((), (), s32[]{:S(2)}) async-start(), calls=%async_computation.3 | async-start | bytes 1769472 | tf_op jit(solution)/shard_map/all_gather | solution.py:124
  28.4 13.4 %collective-permute-start.3 = (f32[8,16,384]{2,1,0:T(8,128)}, f32[8,16,384]{2,1,0:T(8,128)S(1)}, u32[]{:S(2)}, u32[]{:S(2)}) collective-permute-start(f32[8,16,384]{2,1,0:T(8,128)} %get-tuple-element.9), channel_id=1, source_target_pairs={{0,192},{32,224},{64,0},{96,32},{128,64},{160,96},{192,128},{224,1... | collective-permute-start | bytes 589832 | tf_op jit(solution)/shard_map/ppermute | solution.py:104
  32.6 15.2 %collective-permute-start.2 = (f32[8,16,384]{2,1,0:T(8,128)}, f32[8,16,384]{2,1,0:T(8,128)}, u32[]{:S(2)}, u32[]{:S(2)}) collective-permute-start(f32[8,16,384]{2,1,0:T(8,128)} %get-tuple-element.9), channel_id=1, source_target_pairs={{0,64},{32,96},{64,128},{96,160},{128,192},{160,224},{192,0},{224,... | collective-permute-start | bytes 589832 | tf_op jit(solution)/shard_map/ppermute | solution.py:104
  35.2 21.8 %collective-permute-start.1 = (f32[8,16,384]{2,1,0:T(8,128)}, f32[8,16,384]{2,1,0:T(8,128)}, u32[]{:S(2)}, u32[]{:S(2)}) collective-permute-start(f32[8,16,384]{2,1,0:T(8,128)} %get-tuple-element.9), channel_id=1, source_target_pairs={{0,224},{32,0},{64,32},{96,64},{128,96},{160,128},{192,160},{224,1... | collective-permute-start | bytes 589832 | tf_op jit(solution)/shard_map/ppermute | solution.py:104
  39.8 25.6 %collective-permute-start = (f32[8,16,384]{2,1,0:T(8,128)}, f32[8,16,384]{2,1,0:T(8,128)}, u32[]{:S(2)}, u32[]{:S(2)}) collective-permute-start(f32[8,16,384]{2,1,0:T(8,128)} %get-tuple-element.9), channel_id=1, source_target_pairs={{0,32},{32,64},{64,96},{96,128},{128,160},{160,192},{192,224},{224... | collective-permute-start | bytes 589832 | tf_op jit(solution)/shard_map/ppermute | solution.py:104
  41.8 23.6 %copy-start.1 = (f32[8,16,384]{2,1,0:T(8,128)}, f32[8,16,384]{2,1,0:T(8,128)S(1)}, u32[]{:S(2)}) copy-start(f32[8,16,384]{2,1,0:T(8,128)S(1)} %collective-permute-done.3) | copy-start | bytes 589828
  41.8 23.6 %collective-permute-start.7 = (f32[4,16,384]{2,1,0:T(8,128)S(1)}, f32[4,16,384]{2,1,0:T(8,128)}, u32[]{:S(2)}, u32[]{:S(2)}) collective-permute-start(f32[4,16,384]{2,1,0:T(8,128)S(1)} %slice.19), channel_id=1, source_target_pairs={{0,192},{32,224},{64,0},{96,32},{128,64},{160,96},{192,128},{224,1... | collective-permute-start | bytes 294920 | tf_op jit(solution)/shard_map/ppermute | solution.py:104
  48.7 16.7 %collective-permute-start.6 = (f32[4,16,384]{2,1,0:T(8,128)S(1)}, f32[4,16,384]{2,1,0:T(8,128)}, u32[]{:S(2)}, u32[]{:S(2)}) collective-permute-start(f32[4,16,384]{2,1,0:T(8,128)S(1)} %slice.18), channel_id=1, source_target_pairs={{0,64},{32,96},{64,128},{96,160},{128,192},{160,224},{192,0},{224,... | collective-permute-start | bytes 294920 | tf_op jit(solution)/shard_map/ppermute | solution.py:104
  50.7 14.8 %collective-permute-start.5 = (f32[8,16,384]{2,1,0:T(8,128)S(1)}, f32[8,16,384]{2,1,0:T(8,128)}, u32[]{:S(2)}, u32[]{:S(2)}) collective-permute-start(f32[8,16,384]{2,1,0:T(8,128)S(1)} %collective-permute-done.3), channel_id=1, source_target_pairs={{0,224},{32,0},{64,32},{96,64},{128,96},{160,128},{192,160},{224,1... | collective-permute-start | bytes 589832 | tf_op jit(solution)/shard_map/ppermute | solution.py:104
  57.0 13.2 %collective-permute-start.4 = (f32[8,16,384]{2,1,0:T(8,128)}, f32[8,16,384]{2,1,0:T(8,128)}, u32[]{:S(2)}, u32[]{:S(2)}) collective-permute-start(f32[8,16,384]{2,1,0:T(8,128)} %collective-permute-done.2), channel_id=1, source_target_pairs={{0,32},{32,64},{64,96},{96,128},{128,160},{160,192},{192,224},{224... | collective-permute-start | bytes 589832 | tf_op jit(solution)/shard_map/ppermute | solution.py:104
  85.1 39.2 %copy-start = (f32[8,16,512]{2,1,0:T(8,128)S(1)}, f32[8,16,512]{2,1,0:T(8,128)}, u32[]{:S(2)}) copy-start(f32[8,16,512]{2,1,0:T(8,128)} %param.7) | copy-start | bytes 786436
Sparse Core Ops, SparseCore 0:
  30.5 47.6 all-gather.2

commit v8 on v7

v8 whole, which is shorter than its diff:
```python
import functools

import jax
import jax.numpy as jnp
from jax import lax
from jax.experimental import pallas as pl
from jax.experimental.pallas import tpu as pltpu
from jax.sharding import Mesh, PartitionSpec as P

GROUP = ("xh", "z0", "xl")
N_Y, N_ZQ, N_GROUP = 8, 4, 8
ROWS = 16
OUTER = 512
HALF = OUTER // 2
STEPS = 2
VMEM_MB = 24

DOT = functools.partial(
    lax.dot_general, dimension_numbers=(((1,), (1,)), ((), ())), preferred_element_type=jnp.float32
)


def split(x):
    high = x.astype(jnp.bfloat16)
    return high, (x - high.astype(jnp.float32)).astype(jnp.bfloat16)


def pair_kernel(live, t_ref, th, tl):
    rows, width = t_ref.shape[1:]
    slots = lax.broadcasted_iota(jnp.int32, (rows, width), 1)
    for g in range(N_GROUP):
        xh, c = divmod(g, 4)
        at = (slice(xh * rows, (xh + 1) * rows), slice(c * width, (c + 1) * width))
        th[at], tl[at] = split(jnp.where(slots + c * width < live[0], t_ref[g], 0.0))


def pairs(live, t):
    rows, width = t.shape[1] // N_ZQ, t.shape[2]
    total = 2 * t.shape[1]
    return pl.pallas_call(
        pair_kernel,
        out_shape=[jax.ShapeDtypeStruct((total, 4 * width), jnp.bfloat16)] * 2,
        grid_spec=pltpu.PrefetchScalarGridSpec(
            num_scalar_prefetch=1,
            grid=(N_ZQ,),
            in_specs=[pl.BlockSpec((N_GROUP, rows, width), lambda zq, m: (0, zq, 0))],
            out_specs=[pl.BlockSpec((2 * rows, 4 * width), lambda zq, m: (zq, 0))] * 2,
        ),
        compiler_params=pltpu.CompilerParams(vmem_limit_bytes=16 << 20),
        cost_estimate=pl.CostEstimate(flops=3 * t.size, bytes_accessed=8 * t.size, transcendentals=0),
    )(live, t)


NEAR = (0, -1, 1, -2, 2, -3, 3, 4)


def sums_kernel(place, v_mine, v_other, th, tl, out, vh, vl):
    depth, width = v_mine.shape[2], v_mine.shape[4]
    for v_ref, core in ((v_mine, place[N_Y]), (v_other, 1 - place[N_Y])):
        for i in range(N_Y):
            for xh in range(2):
                start = pl.multiple_of(xh * HALF + place[i] * (2 * ROWS) + core * ROWS, ROWS)
                rows = pl.ds(start, ROWS)
                for c in range(depth):
                    columns = slice(c * width, (c + 1) * width)
                    vh[rows, columns], vl[rows, columns] = split(v_ref[i, xh, c])
    sums = DOT(th[...], vh[...]) + (DOT(tl[...], vh[...]) + DOT(th[...], vl[...]))

    @pl.when(pl.program_id(0) == 0)
    def _():
        out[...] = sums

    @pl.when(pl.program_id(0) > 0)
    def _():
        out[...] += sums


def partial_sums(place, mine, other, th, tl):
    width = mine.shape[2]
    depth = 4 // STEPS
    mine, other = (x.reshape(N_Y, 2, 4, ROWS, width) for x in (mine, other))
    total = th.shape[0]
    t_spec = pl.BlockSpec((total, depth * width), lambda k, m: (0, k))
    v_spec = pl.BlockSpec((N_Y, 2, depth, ROWS, width), lambda k, m: (0, 0, k, 0, 0))
    return pl.pallas_call(
        sums_kernel,
        out_shape=jax.ShapeDtypeStruct((total, OUTER), jnp.float32),
        grid_spec=pltpu.PrefetchScalarGridSpec(
            num_scalar_prefetch=1,
            grid=(STEPS,),
            in_specs=[v_spec, v_spec, t_spec, t_spec],
            out_specs=pl.BlockSpec((total, OUTER), lambda k, m: (0, 0)),
            scratch_shapes=[pltpu.VMEM((OUTER, depth * width), jnp.bfloat16)] * 2,
        ),
        compiler_params=pltpu.CompilerParams(vmem_limit_bytes=VMEM_MB << 20),
        cost_estimate=pl.CostEstimate(flops=6 * th.size * OUTER, bytes_accessed=8 << 20, transcendentals=0),
    )(place, mine, other, th, tl)


def along_y(x, by):
    return lax.ppermute(x, "y", [(i, (i + by) % N_Y) for i in range(N_Y)])


def gather(own):
    down2, up2 = along_y(own, 2), along_y(own, -2)
    down1, up1 = along_y(own, 1), along_y(own, -1)
    far = along_y(down2, 2)
    down3, up3 = along_y(down2, 1), along_y(up2, -1)
    return jnp.concatenate([own, down1, up1, down2, up2, down3, up3, far])


def body(amplitudes, integrals, residual_in, cd_count):
    width = amplitudes.shape[2]
    live = cd_count[lax.axis_index(GROUP)] - lax.axis_index("zq") * (4 * width)
    ys = (lax.axis_index("y").astype(jnp.int32) + N_Y + jnp.array(NEAR, jnp.int32)) % N_Y
    place = jnp.concatenate([ys, lax.axis_index("core").astype(jnp.int32)[None]])

    v = lax.all_to_all(integrals, GROUP, 0, 0, tiled=True)
    t = lax.all_to_all(amplitudes, GROUP, 0, 0, tiled=True)
    mine = gather(v)
    other = lax.ppermute(mine, "core", [(0, 1), (1, 0)])
    th, tl = pairs(live[None].astype(jnp.int32), t)

    sums = partial_sums(place, mine, other, th, tl)
    parts = lax.all_to_all(sums.reshape(N_ZQ * N_GROUP, ROWS, OUTER), ("zq",) + GROUP, 0, 0, tiled=True)
    return residual_in + jnp.sum(parts.reshape(N_ZQ, N_GROUP, ROWS, OUTER), axis=0)


def solution(mesh):
    mesh = Mesh(mesh.devices.reshape(2, 8, 2, 4, 2, 2), ("xh", "y", "core", "zq", "z0", "xl"))
    row, col = ("xh", "y", "core"), ("zq", "z0", "xl")
    in_specs = (P(None, row, col), P(None, row, col), P(None, row + col, None), P())
    return jax.shard_map(body, mesh=mesh, in_specs=in_specs, out_specs=P(None, row + col, None), check_vma=False)
```

time: 133 us -> 106 us (0.80)
  between operations: 14.2 us -> 0.8 us
  waiting for transfers between devices: 15.4 us -> 2.82 us
  Pallas kernels: 9.44 us -> 6.16 us
  local copies, waits for them, and re-layouts: 3.29 us -> 6.17 us
    all_gather x1 -> x0, waiting for transfers between devices: 7.98 us -> none  [body(): v = lax.all_gather(v[:N_GROUP], 'y', axis=0)]
    ppermute x8 -> x7, starting transfers between devices: 29 us -> 24.1 us  [along_y(): return lax.ppermute(x, 'y', [(i, (i + by) % N_Y) for i in range(N_Y)])]
    unnamed x8 -> x13, local copies, waits for them, and re-layouts: 0.01 us -> 4.82 us
    ppermute x8 -> x7, waiting for transfers between devices: 5.3 us -> 1.34 us  [along_y(): return lax.ppermute(x, 'y', [(i, (i + by) % N_Y) for i in range(N_Y)])]
    all_to_all x1, blocking collectives: 39.1 us -> 41.6 us  [body(): lax.all_to_all(sums.reshape(N_ZQ * N_GROUP, ROWS, OUTER), ('zq',) + GROUP...]
    ppermute x0 -> x1, starting transfers between devices: none -> 1.91 us  [body(): other = lax.ppermute(mine, 'core', [(0, 1), (1, 0)])]
    all_to_all x1, blocking collectives: 15.6 us -> 13.8 us  [body(): v = lax.all_to_all(integrals, GROUP, 0, 0, tiled=True)]
    slice x3 -> x0, local copies, waits for them, and re-layouts: 1.69 us -> none  [the longest x2 0.91 us: gather_by_steps(): down4, up4 = (along_y(down2[:half], 2), along_y(up2[half:], -2))]
  transfers between devices with their start and end apart: 10 -> 9, of which waited for: 5 -> 3; matrix products, arithmetic and copies ran while one was open for 2% -> 6% of each run, Pallas kernels for 2% -> 1%
where the time goes in v8:
time: 106 us; the launch traced here: 104 us
  blocking collectives  55.4 us (52%)
  starting transfers between devices  32.2 us (30%)
  local copies, waits for them, and re-layouts  6.17 us (6%)
  Pallas kernels  6.16 us (6%)
  waiting for transfers between devices  2.82 us (3%)
    all_to_all x1, blocking collectives, body(): lax.all_to_all(sums.reshape(N_ZQ * N_GROUP, ROWS, OUTER), ('zq',) + GROUP...  41.6 us
    ppermute x7, starting transfers between devices, along_y(): return lax.ppermute(x, 'y', [(i, (i + by) % N_Y) for i in range(N_Y)])  24.1 us
    all_to_all x1, blocking collectives, body(): v = lax.all_to_all(integrals, GROUP, 0, 0, tiled=True)  13.8 us
    all_to_all x1, starting transfers between devices, body(): t = lax.all_to_all(amplitudes, GROUP, 0, 0, tiled=True)  6.18 us
    pallas_call x1, Pallas kernels, partial_sums(): pl.pallas_call(sums_kernel, out_shape=jax.ShapeDtypeStruct((total, OUTER)...  5.35 us
    unnamed x13, local copies, waits for them, and re-layouts  4.82 us
  transfers between devices with their start and end apart: 9, of which 3 were waited for; matrix products, arithmetic and copies ran while one was open for 6% of the time, Pallas kernels for 1%

profile of v8, /device:TPU:6, one launch (start us, length us, event | category | flops | bytes accessed | tf_op | source)
XLA Modules:
  0.0 104.4 jit_solution(16422341630453843949)
XLA Ops:
  0.0 13.8 %all_to_all.15 = f32[8,16,384]{2,1,0:T(8,128)S(1)} all-to-all(f32[8,16,384]{2,1,0:T(8,128)} %param.6), channel_id=1, replica_groups=mesh['xh'=2,'y'=8,'core'=2,'zq'=4,'z0'=2,'xl'=2] {'xh','z0','xl'}, dimensions={0} | all-to-all | bytes 393216 | tf_op jit(solution)/shard_map/all_to_all | solution.py:118
  13.8 6.2 %all-to-all-start.1 = ((f32[8,256,384]{2,1,0:T(8,128)}), f32[8,256,384]{2,1,0:T(8,128)S(1)}, u32[]{:S(2)}, u32[]{:S(2)}) async-start(f32[8,256,384]{2,1,0:T(8,128)} %param.5), calls=%async_computation.1 | async-start | bytes 6291456 | tf_op jit(solution)/shard_map/all_to_all | solution.py:119
  20.0 2.1 %collective-permute-start.2 = (f32[8,16,384]{2,1,0:T(8,128)S(1)}, f32[8,16,384]{2,1,0:T(8,128)S(1)}, u32[]{:S(2)}, u32[]{:S(2)}) collective-permute-start(f32[8,16,384]{2,1,0:T(8,128)S(1)} %all_to_all.15), channel_id=1, source_target_pairs={{0,64},{32,96},{64,128},{96,160},{128,192},{160,224},{192,0},{224,... | collective-permute-start | bytes 589832 | tf_op jit(solution)/shard_map/ppermute | solution.py:101
  22.0 6.0 %collective-permute-start.3 = (f32[8,16,384]{2,1,0:T(8,128)S(1)}, f32[8,16,384]{2,1,0:T(8,128)S(1)}, u32[]{:S(2)}, u32[]{:S(2)}) collective-permute-start(f32[8,16,384]{2,1,0:T(8,128)S(1)} %all_to_all.15), channel_id=1, source_target_pairs={{0,192},{32,224},{64,0},{96,32},{128,64},{160,96},{192,128},{224,1... | collective-permute-start | bytes 589832 | tf_op jit(solution)/shard_map/ppermute | solution.py:101
  28.0 1.9 %collective-permute-start = (f32[8,16,384]{2,1,0:T(8,128)S(1)}, f32[8,16,384]{2,1,0:T(8,128)S(1)}, u32[]{:S(2)}, u32[]{:S(2)}) collective-permute-start(f32[8,16,384]{2,1,0:T(8,128)S(1)} %all_to_all.15), channel_id=1, source_target_pairs={{0,32},{32,64},{64,96},{96,128},{128,160},{160,192},{192,224},{224... | collective-permute-start | bytes 589832 | tf_op jit(solution)/shard_map/ppermute | solution.py:101
  30.0 5.1 %collective-permute-start.1 = (f32[8,16,384]{2,1,0:T(8,128)S(1)}, f32[8,16,384]{2,1,0:T(8,128)S(1)}, u32[]{:S(2)}, u32[]{:S(2)}) collective-permute-start(f32[8,16,384]{2,1,0:T(8,128)S(1)} %all_to_all.15), channel_id=1, source_target_pairs={{0,224},{32,0},{64,32},{96,64},{128,96},{160,128},{192,160},{224,1... | collective-permute-start | bytes 589832 | tf_op jit(solution)/shard_map/ppermute | solution.py:101
  35.1 0.7 constant_dynamic-update-slice_fusion.7
  35.8 0.0 collective-permute-done.2
  35.8 1.9 %collective-permute-start.4 = (f32[8,16,384]{2,1,0:T(8,128)S(1)}, f32[8,16,384]{2,1,0:T(8,128)S(1)}, u32[]{:S(2)}, u32[]{:S(2)}) collective-permute-start(f32[8,16,384]{2,1,0:T(8,128)S(1)} %collective-permute-done.2), channel_id=1, source_target_pairs={{0,32},{32,64},{64,96},{96,128},{128,160},{160,192},{192,224},{224... | collective-permute-start | bytes 589832 | tf_op jit(solution)/shard_map/ppermute | solution.py:101
  37.7 3.1 %collective-permute-start.6 = (f32[8,16,384]{2,1,0:T(8,128)S(1)}, f32[8,16,384]{2,1,0:T(8,128)S(1)}, u32[]{:S(2)}, u32[]{:S(2)}) collective-permute-start(f32[8,16,384]{2,1,0:T(8,128)S(1)} %collective-permute-done.2), channel_id=1, source_target_pairs={{0,64},{32,96},{64,128},{96,160},{128,192},{160,224},{192,0},{224,... | collective-permute-start | bytes 589832 | tf_op jit(solution)/shard_map/ppermute | solution.py:101
  40.8 0.0 collective-permute-done.3
  40.8 4.0 %collective-permute-start.5 = (f32[8,16,384]{2,1,0:T(8,128)S(1)}, f32[8,16,384]{2,1,0:T(8,128)S(1)}, u32[]{:S(2)}, u32[]{:S(2)}) collective-permute-start(f32[8,16,384]{2,1,0:T(8,128)S(1)} %collective-permute-done.3), channel_id=1, source_target_pairs={{0,224},{32,0},{64,32},{96,64},{128,96},{160,128},{192,160},{224,1... | collective-permute-start | bytes 589832 | tf_op jit(solution)/shard_map/ppermute | solution.py:101
  44.8 0.0 collective-permute-done
  44.8 0.7 constant_dynamic-update-slice_fusion.6
  45.5 0.7 constant_dynamic-update-slice_fusion.5
  46.2 0.7 constant_dynamic-update-slice_fusion.4
  46.9 0.7 constant_dynamic-update-slice_fusion.3
  47.6 0.7 constant_dynamic-update-slice_fusion.2
  48.2 1.3 %collective-permute-done.5 = f32[8,16,384]{2,1,0:T(8,128)S(1)} collective-permute-done((f32[8,16,384]{2,1,0:T(8,128)S(1)}, f32[8,16,384]{2,1,0:T(8,128)S(1)}, u32[]{:S(2)}, u32[]{:S(2)}) %collective-permute-start.5) | collective-permute-done | bytes 196640 | tf_op jit(solution)/shard_map/ppermute | solution.py:101
  49.6 0.7 constant_dynamic-update-slice_fusion.1
  50.3 0.7 constant_dynamic-update-slice_fusion
  51.0 1.9 %collective-permute-start.7 = (f32[64,16,384]{2,1,0:T(8,128)}, f32[64,16,384]{2,1,0:T(8,128)}, u32[]{:S(2)}, u32[]{:S(2)}) collective-permute-start(f32[64,16,384]{2,1,0:T(8,128)} %constant_dynamic-update-slice_fusion), channel_id=1, source_target_pairs={{0,16},{16,0},{1,17},{17,1},{2,18},{18,2},{3,19},{19,3},{4,20},{20... | collective-permute-start | bytes 4718600 | tf_op jit(solution)/shard_map/ppermute | solution.py:121
  52.9 0.7 dynamic_slice.3
  54.2 0.1 pad_add_fusion.place
  54.3 1.0 %all-to-all-done.1.t_ref = f32[8,256,384]{2,1,0:T(8,128)S(1)} async-done(((f32[8,256,384]{2,1,0:T(8,128)}), f32[8,256,384]{2,1,0:T(8,128)S(1)}, u32[]{:S(2)}, u32[]{:S(2)}) %all-to-all-start.1) | async-done | bytes 3145760 | tf_op jit(solution)/shard_map/all_to_all | solution.py:119
  55.3 0.8 shard_map.55
  56.2 0.4 collective-permute-done.7
  56.6 5.4 %shard_map.56 = f32[512,512]{1,0:T(8,128)S(1)} custom-call(s32[9]{0:T(128)S(1)} %pad_add_fusion.place, f32[8,2,4,16,384]{4,3,2,1,0:T(8,128)} %bitcast.1.v_mine, f32[8,2,4,16,384]{4,3,2,1,0:T(8,128)} %bitcast.2.v_other, bf16[512,1536]{1,0:T(8,128)(2,1)S(1)} %get-tuple-element.7.th, bf16[512,1536]{1,0:T(8,128)(2,1)S(1)} %get-tuple-element.8.tl), custom_call_target="tpu_custom_call" | custom-call | flops 2415919104 | bytes 8388608 | tf_op jit(solution)/shard_map/pallas_call | solution.py:85
  62.0 0.0 copy-start
  62.0 41.6 %all_to_all.16 = f32[32,16,512]{2,1,0:T(8,128)S(1)} all-to-all(f32[32,16,512]{2,1,0:T(8,128)S(1)} %bitcast.7), channel_id=1, replica_groups=mesh['xh'=2,'y'=8,'core'=2,'zq'=4,'z0'=2,'xl'=2] {'zq','xh','z0','xl'}, dimensions={0} | all-to-all | bytes 2097152 | tf_op jit(solution)/shard_map/all_to_all | solution.py:125
  103.6 0.1 reduce_sum.9
  103.7 0.7 add.34
  (9 shorter events, 0.0 us)
Async XLA Ops:
  13.8 41.6 %all-to-all-start.1 = ((f32[8,256,384]{2,1,0:T(8,128)}), f32[8,256,384]{2,1,0:T(8,128)S(1)}, u32[]{:S(2)}, u32[]{:S(2)}) async-start(f32[8,256,384]{2,1,0:T(8,128)} %param.5), calls=%async_computation.1 | async-start | bytes 6291456 | tf_op jit(solution)/shard_map/all_to_all | solution.py:119
  20.0 32.9 %copy-start.1 = (s32[8]{0:T(128)S(1)}, s32[8]{0:T(128)}, u32[]{:S(2)}) copy-start(s32[8]{0:T(128)} %param.8) | copy-start | bytes 100
  20.0 34.2 %copy-start.2 = (s32[8]{0:T(128)S(1)}, s32[8]{0:T(128)}, u32[]{:S(2)}) copy-start(s32[8]{0:T(128)} %constant.51.clone) | copy-start | bytes 100
  20.0 15.8 %collective-permute-start.2 = (f32[8,16,384]{2,1,0:T(8,128)S(1)}, f32[8,16,384]{2,1,0:T(8,128)S(1)}, u32[]{:S(2)}, u32[]{:S(2)}) collective-permute-start(f32[8,16,384]{2,1,0:T(8,128)S(1)} %all_to_all.15), channel_id=1, source_target_pairs={{0,64},{32,96},{64,128},{96,160},{128,192},{160,224},{192,0},{224,... | collective-permute-start | bytes 589832 | tf_op jit(solution)/shard_map/ppermute | solution.py:101
  22.0 18.8 %collective-permute-start.3 = (f32[8,16,384]{2,1,0:T(8,128)S(1)}, f32[8,16,384]{2,1,0:T(8,128)S(1)}, u32[]{:S(2)}, u32[]{:S(2)}) collective-permute-start(f32[8,16,384]{2,1,0:T(8,128)S(1)} %all_to_all.15), channel_id=1, source_target_pairs={{0,192},{32,224},{64,0},{96,32},{128,64},{160,96},{192,128},{224,1... | collective-permute-start | bytes 589832 | tf_op jit(solution)/shard_map/ppermute | solution.py:101
  28.0 16.8 %collective-permute-start = (f32[8,16,384]{2,1,0:T(8,128)S(1)}, f32[8,16,384]{2,1,0:T(8,128)S(1)}, u32[]{:S(2)}, u32[]{:S(2)}) collective-permute-start(f32[8,16,384]{2,1,0:T(8,128)S(1)} %all_to_all.15), channel_id=1, source_target_pairs={{0,32},{32,64},{64,96},{96,128},{128,160},{160,192},{192,224},{224... | collective-permute-start | bytes 589832 | tf_op jit(solution)/shard_map/ppermute | solution.py:101
  30.0 15.5 %collective-permute-start.1 = (f32[8,16,384]{2,1,0:T(8,128)S(1)}, f32[8,16,384]{2,1,0:T(8,128)S(1)}, u32[]{:S(2)}, u32[]{:S(2)}) collective-permute-start(f32[8,16,384]{2,1,0:T(8,128)S(1)} %all_to_all.15), channel_id=1, source_target_pairs={{0,224},{32,0},{64,32},{96,64},{128,96},{160,128},{192,160},{224,1... | collective-permute-start | bytes 589832 | tf_op jit(solution)/shard_map/ppermute | solution.py:101
  35.8 11.8 %collective-permute-start.4 = (f32[8,16,384]{2,1,0:T(8,128)S(1)}, f32[8,16,384]{2,1,0:T(8,128)S(1)}, u32[]{:S(2)}, u32[]{:S(2)}) collective-permute-start(f32[8,16,384]{2,1,0:T(8,128)S(1)} %collective-permute-done.2), channel_id=1, source_target_pairs={{0,32},{32,64},{64,96},{96,128},{128,160},{160,192},{192,224},{224... | collective-permute-start | bytes 589832 | tf_op jit(solution)/shard_map/ppermute | solution.py:101
  37.7 12.6 %collective-permute-start.6 = (f32[8,16,384]{2,1,0:T(8,128)S(1)}, f32[8,16,384]{2,1,0:T(8,128)S(1)}, u32[]{:S(2)}, u32[]{:S(2)}) collective-permute-start(f32[8,16,384]{2,1,0:T(8,128)S(1)} %collective-permute-done.2), channel_id=1, source_target_pairs={{0,64},{32,96},{64,128},{96,160},{128,192},{160,224},{192,0},{224,... | collective-permute-start | bytes 589832 | tf_op jit(solution)/shard_map/ppermute | solution.py:101
  40.8 8.8 %collective-permute-start.5 = (f32[8,16,384]{2,1,0:T(8,128)S(1)}, f32[8,16,384]{2,1,0:T(8,128)S(1)}, u32[]{:S(2)}, u32[]{:S(2)}) collective-permute-start(f32[8,16,384]{2,1,0:T(8,128)S(1)} %collective-permute-done.3), channel_id=1, source_target_pairs={{0,224},{32,0},{64,32},{96,64},{128,96},{160,128},{192,160},{224,1... | collective-permute-start | bytes 589832 | tf_op jit(solution)/shard_map/ppermute | solution.py:101
  51.0 5.6 %collective-permute-start.7 = (f32[64,16,384]{2,1,0:T(8,128)}, f32[64,16,384]{2,1,0:T(8,128)}, u32[]{:S(2)}, u32[]{:S(2)}) collective-permute-start(f32[64,16,384]{2,1,0:T(8,128)} %constant_dynamic-update-slice_fusion), channel_id=1, source_target_pairs={{0,16},{16,0},{1,17},{17,1},{2,18},{18,2},{3,19},{19,3},{4,20},{20... | collective-permute-start | bytes 4718600 | tf_op jit(solution)/shard_map/ppermute | solution.py:121
  62.0 41.7 %copy-start = (f32[8,16,512]{2,1,0:T(8,128)S(1)}, f32[8,16,512]{2,1,0:T(8,128)}, u32[]{:S(2)}) copy-start(f32[8,16,512]{2,1,0:T(8,128)} %param.7) | copy-start | bytes 786436

commit v9 on v8

v9 whole, which is shorter than its diff:
```python
import functools

import jax
import jax.numpy as jnp
from jax import lax
from jax.experimental import pallas as pl
from jax.experimental.pallas import tpu as pltpu
from jax.sharding import Mesh, PartitionSpec as P

GROUP = ("xh", "z0", "xl")
N_Y, N_ZQ, N_GROUP = 8, 4, 8
ROWS = 16
OUTER = 512
HALF = OUTER // 2
STEPS = 2

DOT = functools.partial(
    lax.dot_general, dimension_numbers=(((1,), (1,)), ((), ())), preferred_element_type=jnp.float32
)


def split(x):
    high = x.astype(jnp.bfloat16)
    return high, (x - high.astype(jnp.float32)).astype(jnp.bfloat16)


NEAR = (0, -1, 1, -2, 2, -3, 3, 4)


def order_kernel(place, v_mine, v_other, vh, vl):
    width = v_mine.shape[4]
    for v_ref, core in ((v_mine, place[N_Y]), (v_other, 1 - place[N_Y])):
        for i in range(N_Y):
            for xh in range(2):
                start = pl.multiple_of(xh * HALF + place[i] * (2 * ROWS) + core * ROWS, ROWS)
                rows = pl.ds(start, ROWS)
                for c in range(4):
                    columns = slice(c * width, (c + 1) * width)
                    vh[rows, columns], vl[rows, columns] = split(v_ref[i, xh, c])


def in_order(place, mine, other):
    width = mine.shape[2]
    mine, other = (x.reshape(N_Y, 2, 4, ROWS, width) for x in (mine, other))
    v_spec = pl.BlockSpec(mine.shape, lambda k, m: (0, 0, 0, 0, 0))
    return pl.pallas_call(
        order_kernel,
        out_shape=[pltpu.HBM((OUTER, 4 * width), jnp.bfloat16)] * 2,
        grid_spec=pltpu.PrefetchScalarGridSpec(
            num_scalar_prefetch=1,
            grid=(1,),
            in_specs=[v_spec, v_spec],
            out_specs=[pl.BlockSpec((OUTER, 4 * width), lambda k, m: (0, 0))] * 2,
        ),
        compiler_params=pltpu.CompilerParams(vmem_limit_bytes=24 << 20),
        cost_estimate=pl.CostEstimate(flops=6 * mine.size, bytes_accessed=16 * mine.size, transcendentals=0),
    )(place, mine, other)


def sums_kernel(live, t_ref, vh, vl, out, th, tl):
    depth, rows, width = t_ref.shape[1:]
    rows = rows // N_ZQ
    slots = lax.broadcasted_iota(jnp.int32, (rows, width), 1) + pl.program_id(0) * (depth * width)
    for c in range(depth):
        alive = slots + c * width < live[0]
        for zq in range(N_ZQ):
            for xh in range(2):
                at = (slice((2 * zq + xh) * rows, (2 * zq + xh + 1) * rows), slice(c * width, (c + 1) * width))
                th[at], tl[at] = split(jnp.where(alive, t_ref[xh, c, zq * rows : (zq + 1) * rows], 0.0))
    sums = DOT(th[...], vh[...]) + (DOT(tl[...], vh[...]) + DOT(th[...], vl[...]))

    @pl.when(pl.program_id(0) == 0)
    def _():
        out[...] = sums

    @pl.when(pl.program_id(0) > 0)
    def _():
        out[...] += sums


def partial_sums(live, t, vh, vl):
    rows, width = t.shape[1:]
    depth = 4 // STEPS
    t = t.reshape(2, 4, rows, width)
    v_spec = pl.BlockSpec((OUTER, depth * width), lambda k, m: (0, k))
    return pl.pallas_call(
        sums_kernel,
        out_shape=jax.ShapeDtypeStruct((2 * rows, OUTER), jnp.float32),
        grid_spec=pltpu.PrefetchScalarGridSpec(
            num_scalar_prefetch=1,
            grid=(STEPS,),
            in_specs=[pl.BlockSpec((2, depth, rows, width), lambda k, m: (0, k, 0, 0)), v_spec, v_spec],
            out_specs=pl.BlockSpec((2 * rows, OUTER), lambda k, m: (0, 0)),
            scratch_shapes=[pltpu.VMEM((2 * rows, depth * width), jnp.bfloat16)] * 2,
        ),
        compiler_params=pltpu.CompilerParams(vmem_limit_bytes=24 << 20),
        cost_estimate=pl.CostEstimate(flops=6 * t.size * OUTER, bytes_accessed=8 << 20, transcendentals=0),
    )(live, t, vh, vl)


def along_y(x, by):
    return lax.ppermute(x, "y", [(i, (i + by) % N_Y) for i in range(N_Y)])


def gather(own):
    down2, up2 = along_y(own, 2), along_y(own, -2)
    down1, up1 = along_y(own, 1), along_y(own, -1)
    far = along_y(down2, 2)
    down3, up3 = along_y(down2, 1), along_y(up2, -1)
    return jnp.concatenate([own, down1, up1, down2, up2, down3, up3, far])


def body(amplitudes, integrals, residual_in, cd_count):
    width = amplitudes.shape[2]
    live = cd_count[lax.axis_index(GROUP)] - lax.axis_index("zq") * (4 * width)
    ys = (lax.axis_index("y").astype(jnp.int32) + N_Y + jnp.array(NEAR, jnp.int32)) % N_Y
    place = jnp.concatenate([ys, lax.axis_index("core").astype(jnp.int32)[None]])

    v = lax.all_to_all(integrals, GROUP, 0, 0, tiled=True)
    t = lax.all_to_all(amplitudes, GROUP, 0, 0, tiled=True)
    mine = gather(v)
    other = lax.ppermute(mine, "core", [(0, 1), (1, 0)])
    vh, vl = in_order(place, mine, other)

    sums = partial_sums(live[None].astype(jnp.int32), t, vh, vl)
    parts = lax.all_to_all(sums.reshape(N_ZQ * N_GROUP, ROWS, OUTER), ("zq",) + GROUP, 0, 0, tiled=True)
    return residual_in + jnp.sum(parts.reshape(N_ZQ, N_GROUP, ROWS, OUTER), axis=0)


def solution(mesh):
    mesh = Mesh(mesh.devices.reshape(2, 8, 2, 4, 2, 2), ("xh", "y", "core", "zq", "z0", "xl"))
    row, col = ("xh", "y", "core"), ("zq", "z0", "xl")
    in_specs = (P(None, row, col), P(None, row, col), P(None, row + col, None), P())
    return jax.shard_map(body, mesh=mesh, in_specs=in_specs, out_specs=P(None, row + col, None), check_vma=False)
```

time: 106 us -> 110 us (1.038)
  local copies, waits for them, and re-layouts: 6.17 us -> 8.96 us
  Pallas kernels: 6.16 us -> 7.94 us
    unnamed x13 -> x17, local copies, waits for them, and re-layouts: 4.82 us -> 7.68 us
    ppermute x1, waiting for transfers between devices: 0.44 us -> 2.35 us  [body(): other = lax.ppermute(mine, 'core', [(0, 1), (1, 0)])]
    pallas_call x2, Pallas kernels: 6.16 us -> 7.94 us  [the longest x1 4.49 us: in_order(): pl.pallas_call(order_kernel, out_shape=[pltpu.HBM((OUTER, 4 * width), jnp...]
  transfers between devices with their start and end apart: 9 -> 9, of which waited for: 3 -> 2; matrix products, arithmetic and copies ran while one was open for 6% -> 6% of each run, Pallas kernels for 1% -> 4%
where the time goes in v9:
time: 110 us; the launch traced here: 109 us
  blocking collectives  54.6 us (50%)
  starting transfers between devices  32.2 us (29%)
  local copies, waits for them, and re-layouts  8.96 us (8%)
  Pallas kernels  7.94 us (7%)
  waiting for transfers between devices  3.65 us (3%)
    all_to_all x1, blocking collectives, body(): lax.all_to_all(sums.reshape(N_ZQ * N_GROUP, ROWS, OUTER), ('zq',) + GROUP...  40.8 us
    ppermute x7, starting transfers between devices, along_y(): return lax.ppermute(x, 'y', [(i, (i + by) % N_Y) for i in range(N_Y)])  24.1 us
    all_to_all x1, blocking collectives, body(): v = lax.all_to_all(integrals, GROUP, 0, 0, tiled=True)  13.8 us
    unnamed x17, local copies, waits for them, and re-layouts  7.68 us
    all_to_all x1, starting transfers between devices, body(): t = lax.all_to_all(amplitudes, GROUP, 0, 0, tiled=True)  6.18 us
    pallas_call x1, Pallas kernels, in_order(): pl.pallas_call(order_kernel, out_shape=[pltpu.HBM((OUTER, 4 * width), jnp...  4.49 us
    pallas_call x1, Pallas kernels, partial_sums(): pl.pallas_call(sums_kernel, out_shape=jax.ShapeDtypeStruct((2 * rows, OUT...  3.44 us
    ppermute x1, waiting for transfers between devices, body(): other = lax.ppermute(mine, 'core', [(0, 1), (1, 0)])  2.35 us
  transfers between devices with their start and end apart: 9, of which 2 were waited for; matrix products, arithmetic and copies ran while one was open for 6% of the time, Pallas kernels for 4%

profile of v9, /device:TPU:6, one launch (start us, length us, event | category | flops | bytes accessed | tf_op | source)
XLA Modules:
  0.0 109.1 jit_solution(8586025385275336677)
XLA Ops:
  0.0 13.8 %all_to_all.15 = f32[8,16,384]{2,1,0:T(8,128)S(1)} all-to-all(f32[8,16,384]{2,1,0:T(8,128)} %param.6), channel_id=1, replica_groups=mesh['xh'=2,'y'=8,'core'=2,'zq'=4,'z0'=2,'xl'=2] {'xh','z0','xl'}, dimensions={0} | all-to-all | bytes 393216 | tf_op jit(solution)/shard_map/all_to_all | solution.py:119
  13.8 6.2 %all-to-all-start = ((f32[8,256,384]{2,1,0:T(8,128)}), f32[8,256,384]{2,1,0:T(8,128)S(1)}, u32[]{:S(2)}, u32[]{:S(2)}) async-start(f32[8,256,384]{2,1,0:T(8,128)} %param.5), calls=%async_computation | async-start | bytes 6291456 | tf_op jit(solution)/shard_map/all_to_all | solution.py:120
  20.0 2.1 %collective-permute-start.2 = (f32[8,16,384]{2,1,0:T(8,128)S(1)}, f32[8,16,384]{2,1,0:T(8,128)S(1)}, u32[]{:S(2)}, u32[]{:S(2)}) collective-permute-start(f32[8,16,384]{2,1,0:T(8,128)S(1)} %all_to_all.15), channel_id=1, source_target_pairs={{0,64},{32,96},{64,128},{96,160},{128,192},{160,224},{192,0},{224,... | collective-permute-start | bytes 589832 | tf_op jit(solution)/shard_map/ppermute | solution.py:102
  22.0 6.0 %collective-permute-start.3 = (f32[8,16,384]{2,1,0:T(8,128)S(1)}, f32[8,16,384]{2,1,0:T(8,128)S(1)}, u32[]{:S(2)}, u32[]{:S(2)}) collective-permute-start(f32[8,16,384]{2,1,0:T(8,128)S(1)} %all_to_all.15), channel_id=1, source_target_pairs={{0,192},{32,224},{64,0},{96,32},{128,64},{160,96},{192,128},{224,1... | collective-permute-start | bytes 589832 | tf_op jit(solution)/shard_map/ppermute | solution.py:102
  28.0 1.9 %collective-permute-start = (f32[8,16,384]{2,1,0:T(8,128)S(1)}, f32[8,16,384]{2,1,0:T(8,128)S(1)}, u32[]{:S(2)}, u32[]{:S(2)}) collective-permute-start(f32[8,16,384]{2,1,0:T(8,128)S(1)} %all_to_all.15), channel_id=1, source_target_pairs={{0,32},{32,64},{64,96},{96,128},{128,160},{160,192},{192,224},{224... | collective-permute-start | bytes 589832 | tf_op jit(solution)/shard_map/ppermute | solution.py:102
  30.0 5.1 %collective-permute-start.1 = (f32[8,16,384]{2,1,0:T(8,128)S(1)}, f32[8,16,384]{2,1,0:T(8,128)S(1)}, u32[]{:S(2)}, u32[]{:S(2)}) collective-permute-start(f32[8,16,384]{2,1,0:T(8,128)S(1)} %all_to_all.15), channel_id=1, source_target_pairs={{0,224},{32,0},{64,32},{96,64},{128,96},{160,128},{192,160},{224,1... | collective-permute-start | bytes 589832 | tf_op jit(solution)/shard_map/ppermute | solution.py:102
  35.1 0.7 constant_dynamic-update-slice_fusion.7
  35.8 0.0 collective-permute-done.2
  35.8 1.9 %collective-permute-start.4 = (f32[8,16,384]{2,1,0:T(8,128)S(1)}, f32[8,16,384]{2,1,0:T(8,128)S(1)}, u32[]{:S(2)}, u32[]{:S(2)}) collective-permute-start(f32[8,16,384]{2,1,0:T(8,128)S(1)} %collective-permute-done.2), channel_id=1, source_target_pairs={{0,32},{32,64},{64,96},{96,128},{128,160},{160,192},{192,224},{224... | collective-permute-start | bytes 589832 | tf_op jit(solution)/shard_map/ppermute | solution.py:102
  37.7 3.1 %collective-permute-start.6 = (f32[8,16,384]{2,1,0:T(8,128)S(1)}, f32[8,16,384]{2,1,0:T(8,128)S(1)}, u32[]{:S(2)}, u32[]{:S(2)}) collective-permute-start(f32[8,16,384]{2,1,0:T(8,128)S(1)} %collective-permute-done.2), channel_id=1, source_target_pairs={{0,64},{32,96},{64,128},{96,160},{128,192},{160,224},{192,0},{224,... | collective-permute-start | bytes 589832 | tf_op jit(solution)/shard_map/ppermute | solution.py:102
  40.8 0.0 collective-permute-done.3
  40.8 4.0 %collective-permute-start.5 = (f32[8,16,384]{2,1,0:T(8,128)S(1)}, f32[8,16,384]{2,1,0:T(8,128)S(1)}, u32[]{:S(2)}, u32[]{:S(2)}) collective-permute-start(f32[8,16,384]{2,1,0:T(8,128)S(1)} %collective-permute-done.3), channel_id=1, source_target_pairs={{0,224},{32,0},{64,32},{96,64},{128,96},{160,128},{192,160},{224,1... | collective-permute-start | bytes 589832 | tf_op jit(solution)/shard_map/ppermute | solution.py:102
  44.8 0.7 constant_dynamic-update-slice_fusion.6
  45.5 0.7 constant_dynamic-update-slice_fusion.5
  46.2 0.7 constant_dynamic-update-slice_fusion.4
  46.9 0.7 constant_dynamic-update-slice_fusion.3
  47.6 0.7 constant_dynamic-update-slice_fusion.2
  48.3 1.3 %collective-permute-done.5 = f32[8,16,384]{2,1,0:T(8,128)S(1)} collective-permute-done((f32[8,16,384]{2,1,0:T(8,128)S(1)}, f32[8,16,384]{2,1,0:T(8,128)S(1)}, u32[]{:S(2)}, u32[]{:S(2)}) %collective-permute-start.5) | collective-permute-done | bytes 196640 | tf_op jit(solution)/shard_map/ppermute | solution.py:102
  49.6 0.7 constant_dynamic-update-slice_fusion.1
  50.3 0.7 constant_dynamic-update-slice_fusion
  51.0 1.9 %collective-permute-start.7 = (f32[64,16,384]{2,1,0:T(8,128)}, f32[64,16,384]{2,1,0:T(8,128)}, u32[]{:S(2)}, u32[]{:S(2)}) collective-permute-start(f32[64,16,384]{2,1,0:T(8,128)} %constant_dynamic-update-slice_fusion), channel_id=1, source_target_pairs={{0,16},{16,0},{1,17},{17,1},{2,18},{18,2},{3,19},{19,3},{4,20},{20... | collective-permute-start | bytes 4718600 | tf_op jit(solution)/shard_map/ppermute | solution.py:122
  52.9 0.6 dynamic_slice.3
  54.2 0.1 pad_add_fusion.place
  54.2 2.4 %collective-permute-done.7 = f32[64,16,384]{2,1,0:T(8,128)} collective-permute-done((f32[64,16,384]{2,1,0:T(8,128)}, f32[64,16,384]{2,1,0:T(8,128)}, u32[]{:S(2)}, u32[]{:S(2)}) %collective-permute-start.7) | collective-permute-done | bytes 1572896 | tf_op jit(solution)/shard_map/ppermute | solution.py:122
  56.6 4.5 %shard_map.55 = (bf16[512,1536]{1,0:T(8,128)(2,1)}, bf16[512,1536]{1,0:T(8,128)(2,1)}) custom-call(s32[9]{0:T(128)S(1)} %pad_add_fusion.place, f32[8,2,4,16,384]{4,3,2,1,0:T(8,128)} %bitcast.4.v_mine, f32[8,2,4,16,384]{4,3,2,1,0:T(8,128)} %bitcast.5.v_other), custom_call_target="tpu_custom_call" | custom-call | flops 2359296 | bytes 6291456 | tf_op jit(solution)/shard_map/pallas_call | solution.py:46
  61.1 1.4 %copy-done = bf16[512,1536]{1,0:T(8,128)(2,1)S(1)} copy-done((bf16[512,1536]{1,0:T(8,128)(2,1)S(1)}, bf16[512,1536]{1,0:T(8,128)(2,1)}, u32[]{:S(2)}) %copy-start) | copy-done | bytes 1572888
  62.5 1.4 %copy-done.1 = bf16[512,1536]{1,0:T(8,128)(2,1)S(1)} copy-done((bf16[512,1536]{1,0:T(8,128)(2,1)S(1)}, bf16[512,1536]{1,0:T(8,128)(2,1)}, u32[]{:S(2)}) %copy-start.1) | copy-done | bytes 1572888
  63.9 3.4 %shard_map.56 = f32[512,512]{1,0:T(8,128)S(1)} custom-call(s32[1]{0:T(128)} %bitcast.1.live, f32[2,4,256,384]{3,2,1,0:T(8,128)S(1)} %bitcast.8, bf16[512,1536]{1,0:T(8,128)(2,1)S(1)} %copy-done, bf16[512,1536]{1,0:T(8,128)(2,1)S(1)} %copy-done.1), custom_call_target="tpu_custom_call" | custom-call | flops 2415919104 | bytes 8388608 | tf_op jit(solution)/shard_map/pallas_call | solution.py:86
  67.4 0.0 copy-start.2
  67.4 40.8 %all_to_all.16 = f32[32,16,512]{2,1,0:T(8,128)S(1)} all-to-all(f32[32,16,512]{2,1,0:T(8,128)S(1)} %bitcast.9), channel_id=1, replica_groups=mesh['xh'=2,'y'=8,'core'=2,'zq'=4,'z0'=2,'xl'=2] {'zq','xh','z0','xl'}, dimensions={0} | all-to-all | bytes 2097152 | tf_op jit(solution)/shard_map/all_to_all | solution.py:126
  108.2 0.1 reduce_sum.9
  108.3 0.7 add.34
  (13 shorter events, 0.0 us)
Async XLA Ops:
  13.8 47.3 %all-to-all-start = ((f32[8,256,384]{2,1,0:T(8,128)}), f32[8,256,384]{2,1,0:T(8,128)S(1)}, u32[]{:S(2)}, u32[]{:S(2)}) async-start(f32[8,256,384]{2,1,0:T(8,128)} %param.5), calls=%async_computation | async-start | bytes 6291456 | tf_op jit(solution)/shard_map/all_to_all | solution.py:120
  20.0 32.9 %copy-start.3 = (s32[8]{0:T(128)S(1)}, s32[8]{0:T(128)}, u32[]{:S(2)}) copy-start(s32[8]{0:T(128)} %param.8) | copy-start | bytes 100
  20.0 34.2 %copy-start.4 = (s32[8]{0:T(128)S(1)}, s32[8]{0:T(128)}, u32[]{:S(2)}) copy-start(s32[8]{0:T(128)} %constant.51.clone) | copy-start | bytes 100
  20.0 15.8 %collective-permute-start.2 = (f32[8,16,384]{2,1,0:T(8,128)S(1)}, f32[8,16,384]{2,1,0:T(8,128)S(1)}, u32[]{:S(2)}, u32[]{:S(2)}) collective-permute-start(f32[8,16,384]{2,1,0:T(8,128)S(1)} %all_to_all.15), channel_id=1, source_target_pairs={{0,64},{32,96},{64,128},{96,160},{128,192},{160,224},{192,0},{224,... | collective-permute-start | bytes 589832 | tf_op jit(solution)/shard_map/ppermute | solution.py:102
  22.0 18.8 %collective-permute-start.3 = (f32[8,16,384]{2,1,0:T(8,128)S(1)}, f32[8,16,384]{2,1,0:T(8,128)S(1)}, u32[]{:S(2)}, u32[]{:S(2)}) collective-permute-start(f32[8,16,384]{2,1,0:T(8,128)S(1)} %all_to_all.15), channel_id=1, source_target_pairs={{0,192},{32,224},{64,0},{96,32},{128,64},{160,96},{192,128},{224,1... | collective-permute-start | bytes 589832 | tf_op jit(solution)/shard_map/ppermute | solution.py:102
  28.0 16.8 %collective-permute-start = (f32[8,16,384]{2,1,0:T(8,128)S(1)}, f32[8,16,384]{2,1,0:T(8,128)S(1)}, u32[]{:S(2)}, u32[]{:S(2)}) collective-permute-start(f32[8,16,384]{2,1,0:T(8,128)S(1)} %all_to_all.15), channel_id=1, source_target_pairs={{0,32},{32,64},{64,96},{96,128},{128,160},{160,192},{192,224},{224... | collective-permute-start | bytes 589832 | tf_op jit(solution)/shard_map/ppermute | solution.py:102
  30.0 15.5 %collective-permute-start.1 = (f32[8,16,384]{2,1,0:T(8,128)S(1)}, f32[8,16,384]{2,1,0:T(8,128)S(1)}, u32[]{:S(2)}, u32[]{:S(2)}) collective-permute-start(f32[8,16,384]{2,1,0:T(8,128)S(1)} %all_to_all.15), channel_id=1, source_target_pairs={{0,224},{32,0},{64,32},{96,64},{128,96},{160,128},{192,160},{224,1... | collective-permute-start | bytes 589832 | tf_op jit(solution)/shard_map/ppermute | solution.py:102
  35.8 11.8 %collective-permute-start.4 = (f32[8,16,384]{2,1,0:T(8,128)S(1)}, f32[8,16,384]{2,1,0:T(8,128)S(1)}, u32[]{:S(2)}, u32[]{:S(2)}) collective-permute-start(f32[8,16,384]{2,1,0:T(8,128)S(1)} %collective-permute-done.2), channel_id=1, source_target_pairs={{0,32},{32,64},{64,96},{96,128},{128,160},{160,192},{192,224},{224... | collective-permute-start | bytes 589832 | tf_op jit(solution)/shard_map/ppermute | solution.py:102
  37.7 12.5 %collective-permute-start.6 = (f32[8,16,384]{2,1,0:T(8,128)S(1)}, f32[8,16,384]{2,1,0:T(8,128)S(1)}, u32[]{:S(2)}, u32[]{:S(2)}) collective-permute-start(f32[8,16,384]{2,1,0:T(8,128)S(1)} %collective-permute-done.2), channel_id=1, source_target_pairs={{0,64},{32,96},{64,128},{96,160},{128,192},{160,224},{192,0},{224,... | collective-permute-start | bytes 589832 | tf_op jit(solution)/shard_map/ppermute | solution.py:102
  40.8 8.8 %collective-permute-start.5 = (f32[8,16,384]{2,1,0:T(8,128)S(1)}, f32[8,16,384]{2,1,0:T(8,128)S(1)}, u32[]{:S(2)}, u32[]{:S(2)}) collective-permute-start(f32[8,16,384]{2,1,0:T(8,128)S(1)} %collective-permute-done.3), channel_id=1, source_target_pairs={{0,224},{32,0},{64,32},{96,64},{128,96},{160,128},{192,160},{224,1... | collective-permute-start | bytes 589832 | tf_op jit(solution)/shard_map/ppermute | solution.py:102
  51.0 5.6 %collective-permute-start.7 = (f32[64,16,384]{2,1,0:T(8,128)}, f32[64,16,384]{2,1,0:T(8,128)}, u32[]{:S(2)}, u32[]{:S(2)}) collective-permute-start(f32[64,16,384]{2,1,0:T(8,128)} %constant_dynamic-update-slice_fusion), channel_id=1, source_target_pairs={{0,16},{16,0},{1,17},{17,1},{2,18},{18,2},{3,19},{19,3},{4,20},{20... | collective-permute-start | bytes 4718600 | tf_op jit(solution)/shard_map/ppermute | solution.py:122
  61.1 1.4 %copy-start = (bf16[512,1536]{1,0:T(8,128)(2,1)S(1)}, bf16[512,1536]{1,0:T(8,128)(2,1)}, u32[]{:S(2)}) copy-start(bf16[512,1536]{1,0:T(8,128)(2,1)} %get-tuple-element.7.vh) | copy-start | bytes 4718596
  62.5 1.4 %copy-start.1 = (bf16[512,1536]{1,0:T(8,128)(2,1)S(1)}, bf16[512,1536]{1,0:T(8,128)(2,1)}, u32[]{:S(2)}) copy-start(bf16[512,1536]{1,0:T(8,128)(2,1)} %get-tuple-element.8.vl) | copy-start | bytes 4718596
  67.4 41.0 %copy-start.2 = (f32[8,16,512]{2,1,0:T(8,128)S(1)}, f32[8,16,512]{2,1,0:T(8,128)}, u32[]{:S(2)}) copy-start(f32[8,16,512]{2,1,0:T(8,128)} %param.7) | copy-start | bytes 786436

commit v10 on v9

v10 whole, which is shorter than its diff:
```python
import functools

import jax
import jax.numpy as jnp
from jax import lax
from jax.experimental import pallas as pl
from jax.experimental.pallas import tpu as pltpu
from jax.sharding import Mesh, PartitionSpec as P

GROUP = ("xh", "z0", "xl")
N_Y, N_ZQ, N_GROUP = 8, 4, 8
ROWS = 16
OUTER = 512
HALF = OUTER // 2
STEPS = 2

DOT = functools.partial(
    lax.dot_general, dimension_numbers=(((1,), (1,)), ((), ())), preferred_element_type=jnp.float32
)


def split(x):
    high = x.astype(jnp.bfloat16)
    return high, (x - high.astype(jnp.float32)).astype(jnp.bfloat16)


NEAR = (0, -1, 1, -2, 2, -3, 3, 4)


def sums_kernel(place, t_ref, v_mine, v_other, out, th, tl, vh, vl):
    depth, rows, width = t_ref.shape[1:]
    rows = rows // N_ZQ
    slots = lax.broadcasted_iota(jnp.int32, (rows, width), 1) + pl.program_id(0) * (depth * width)
    for c in range(depth):
        columns = slice(c * width, (c + 1) * width)
        alive = slots + c * width < place[N_Y + 1]
        for zq in range(N_ZQ):
            for xh in range(2):
                at = (slice((2 * zq + xh) * rows, (2 * zq + xh + 1) * rows), columns)
                th[at], tl[at] = split(jnp.where(alive, t_ref[xh, c, zq * rows : (zq + 1) * rows], 0.0))
    for v_ref, core in ((v_mine, place[N_Y]), (v_other, 1 - place[N_Y])):
        for i in range(N_Y):
            for xh in range(2):
                start = pl.multiple_of(xh * HALF + place[i] * (2 * ROWS) + core * ROWS, ROWS)
                for c in range(depth):
                    at = (pl.ds(start, ROWS), slice(c * width, (c + 1) * width))
                    vh[at], vl[at] = split(v_ref[i, xh, c])
    sums = DOT(th[...], vh[...]) + (DOT(tl[...], vh[...]) + DOT(th[...], vl[...]))

    @pl.when(pl.program_id(0) == 0)
    def _():
        out[...] = sums

    @pl.when(pl.program_id(0) > 0)
    def _():
        out[...] += sums


def partial_sums(place, t, mine, other):
    rows, width = t.shape[1:]
    depth = 4 // STEPS
    t = t.reshape(2, 4, rows, width)
    mine, other = (x.reshape(N_Y, 2, 4, ROWS, width) for x in (mine, other))
    v_spec = pl.BlockSpec((N_Y, 2, depth, ROWS, width), lambda k, m: (0, 0, k, 0, 0))
    return pl.pallas_call(
        sums_kernel,
        out_shape=jax.ShapeDtypeStruct((2 * rows, OUTER), jnp.float32),
        grid_spec=pltpu.PrefetchScalarGridSpec(
            num_scalar_prefetch=1,
            grid=(STEPS,),
            in_specs=[pl.BlockSpec((2, depth, rows, width), lambda k, m: (0, k, 0, 0)), v_spec, v_spec],
            out_specs=pl.BlockSpec((2 * rows, OUTER), lambda k, m: (0, 0)),
            scratch_shapes=[pltpu.VMEM((2 * rows, depth * width), jnp.bfloat16)] * 2
            + [pltpu.VMEM((OUTER, depth * width), jnp.bfloat16)] * 2,
        ),
        compiler_params=pltpu.CompilerParams(vmem_limit_bytes=24 << 20),
        cost_estimate=pl.CostEstimate(flops=6 * t.size * OUTER, bytes_accessed=8 << 20, transcendentals=0),
    )(place, t, mine, other)


def along_y(x, by):
    return lax.ppermute(x, "y", [(i, (i + by) % N_Y) for i in range(N_Y)])


def gather(own):
    down2, up2 = along_y(own, 2), along_y(own, -2)
    down1, up1 = along_y(own, 1), along_y(own, -1)
    far = along_y(down2, 2)
    down3, up3 = along_y(down2, 1), along_y(up2, -1)
    return jnp.concatenate([own, down1, up1, down2, up2, down3, up3, far])


def body(amplitudes, integrals, residual_in, cd_count):
    width = amplitudes.shape[2]
    live = cd_count[lax.axis_index(GROUP)] - lax.axis_index("zq") * (4 * width)
    ys = (lax.axis_index("y").astype(jnp.int32) + N_Y + jnp.array(NEAR, jnp.int32)) % N_Y
    place = jnp.concatenate([ys, jnp.stack([lax.axis_index("core"), live]).astype(jnp.int32)])

    v = lax.all_to_all(integrals, GROUP, 0, 0, tiled=True)
    t = lax.all_to_all(amplitudes, GROUP, 0, 0, tiled=True)
    mine = gather(v)
    other = lax.ppermute(mine, "core", [(0, 1), (1, 0)])

    sums = partial_sums(place, t, mine, other)
    parts = lax.all_to_all(sums.reshape(N_ZQ * N_GROUP, ROWS, OUTER), ("zq",) + GROUP, 0, 0, tiled=True)
    return residual_in + jnp.sum(parts.reshape(N_ZQ, N_GROUP, ROWS, OUTER), axis=0)


def solution(mesh):
    mesh = Mesh(mesh.devices.reshape(2, 8, 2, 4, 2, 2), ("xh", "y", "core", "zq", "z0", "xl"))
    row, col = ("xh", "y", "core"), ("zq", "z0", "xl")
    in_specs = (P(None, row, col), P(None, row, col), P(None, row + col, None), P())
    return jax.shard_map(body, mesh=mesh, in_specs=in_specs, out_specs=P(None, row + col, None), check_vma=False)
```

time: 110 us -> 105 us (0.955)
  local copies, waits for them, and re-layouts: 8.96 us -> 6.14 us
  Pallas kernels: 7.94 us -> 5.53 us
    pallas_call x1 -> x0, Pallas kernels: 4.49 us -> none  [in_order(): pl.pallas_call(order_kernel, out_shape=[pltpu.HBM((OUTER, 4 * width), jnp...]
    unnamed x17 -> x13, local copies, waits for them, and re-layouts: 7.68 us -> 4.86 us
    pallas_call x1, Pallas kernels: 3.44 us -> 5.53 us  [partial_sums(): pl.pallas_call(sums_kernel, out_shape=jax.ShapeDtypeStruct((2 * rows, OUT...]
  transfers between devices with their start and end apart: 9 -> 9, of which waited for: 2 -> 2; matrix products, arithmetic and copies ran while one was open for 6% -> 6% of each run, Pallas kernels for 4% -> 0%
where the time goes in v10:
time: 105 us; the launch traced here: 104 us
  blocking collectives  54.6 us (52%)
  starting transfers between devices  32.2 us (31%)
  local copies, waits for them, and re-layouts  6.14 us (6%)
  Pallas kernels  5.53 us (5%)
  waiting for transfers between devices  3.65 us (3%)
    all_to_all x1, blocking collectives, body(): lax.all_to_all(sums.reshape(N_ZQ * N_GROUP, ROWS, OUTER), ('zq',) + GROUP...  40.8 us
    ppermute x7, starting transfers between devices, along_y(): return lax.ppermute(x, 'y', [(i, (i + by) % N_Y) for i in range(N_Y)])  24.1 us
    all_to_all x1, blocking collectives, body(): v = lax.all_to_all(integrals, GROUP, 0, 0, tiled=True)  13.8 us
    all_to_all x1, starting transfers between devices, body(): t = lax.all_to_all(amplitudes, GROUP, 0, 0, tiled=True)  6.18 us
    pallas_call x1, Pallas kernels, partial_sums(): pl.pallas_call(sums_kernel, out_shape=jax.ShapeDtypeStruct((2 * rows, OUT...  5.53 us
    unnamed x13, local copies, waits for them, and re-layouts  4.86 us
    ppermute x1, waiting for transfers between devices, body(): other = lax.ppermute(mine, 'core', [(0, 1), (1, 0)])  2.35 us
  transfers between devices with their start and end apart: 9, of which 2 were waited for; matrix products, arithmetic and copies ran while one was open for 6% of the time, Pallas kernels for 0%

profile of v10, /device:TPU:6, one launch (start us, length us, event | category | flops | bytes accessed | tf_op | source)
XLA Modules:
  0.0 103.8 jit_solution(17235120987201682742)
XLA Ops:
  0.0 13.8 %all_to_all.15 = f32[8,16,384]{2,1,0:T(8,128)S(1)} all-to-all(f32[8,16,384]{2,1,0:T(8,128)} %param.6), channel_id=1, replica_groups=mesh['xh'=2,'y'=8,'core'=2,'zq'=4,'z0'=2,'xl'=2] {'xh','z0','xl'}, dimensions={0} | all-to-all | bytes 393216 | tf_op jit(solution)/shard_map/all_to_all | solution.py:99
  13.8 6.2 %all-to-all-start = ((f32[8,256,384]{2,1,0:T(8,128)}), f32[8,256,384]{2,1,0:T(8,128)S(1)}, u32[]{:S(2)}, u32[]{:S(2)}) async-start(f32[8,256,384]{2,1,0:T(8,128)} %param.5), calls=%async_computation | async-start | bytes 6291456 | tf_op jit(solution)/shard_map/all_to_all | solution.py:100
  20.0 2.1 %collective-permute-start.2 = (f32[8,16,384]{2,1,0:T(8,128)S(1)}, f32[8,16,384]{2,1,0:T(8,128)S(1)}, u32[]{:S(2)}, u32[]{:S(2)}) collective-permute-start(f32[8,16,384]{2,1,0:T(8,128)S(1)} %all_to_all.15), channel_id=1, source_target_pairs={{0,64},{32,96},{64,128},{96,160},{128,192},{160,224},{192,0},{224,... | collective-permute-start | bytes 589832 | tf_op jit(solution)/shard_map/ppermute | solution.py:82
  22.0 6.0 %collective-permute-start.3 = (f32[8,16,384]{2,1,0:T(8,128)S(1)}, f32[8,16,384]{2,1,0:T(8,128)S(1)}, u32[]{:S(2)}, u32[]{:S(2)}) collective-permute-start(f32[8,16,384]{2,1,0:T(8,128)S(1)} %all_to_all.15), channel_id=1, source_target_pairs={{0,192},{32,224},{64,0},{96,32},{128,64},{160,96},{192,128},{224,1... | collective-permute-start | bytes 589832 | tf_op jit(solution)/shard_map/ppermute | solution.py:82
  28.0 1.9 %collective-permute-start = (f32[8,16,384]{2,1,0:T(8,128)S(1)}, f32[8,16,384]{2,1,0:T(8,128)S(1)}, u32[]{:S(2)}, u32[]{:S(2)}) collective-permute-start(f32[8,16,384]{2,1,0:T(8,128)S(1)} %all_to_all.15), channel_id=1, source_target_pairs={{0,32},{32,64},{64,96},{96,128},{128,160},{160,192},{192,224},{224... | collective-permute-start | bytes 589832 | tf_op jit(solution)/shard_map/ppermute | solution.py:82
  30.0 5.1 %collective-permute-start.1 = (f32[8,16,384]{2,1,0:T(8,128)S(1)}, f32[8,16,384]{2,1,0:T(8,128)S(1)}, u32[]{:S(2)}, u32[]{:S(2)}) collective-permute-start(f32[8,16,384]{2,1,0:T(8,128)S(1)} %all_to_all.15), channel_id=1, source_target_pairs={{0,224},{32,0},{64,32},{96,64},{128,96},{160,128},{192,160},{224,1... | collective-permute-start | bytes 589832 | tf_op jit(solution)/shard_map/ppermute | solution.py:82
  35.1 0.7 constant_dynamic-update-slice_fusion.7
  35.8 0.0 collective-permute-done.2
  35.8 1.9 %collective-permute-start.4 = (f32[8,16,384]{2,1,0:T(8,128)S(1)}, f32[8,16,384]{2,1,0:T(8,128)S(1)}, u32[]{:S(2)}, u32[]{:S(2)}) collective-permute-start(f32[8,16,384]{2,1,0:T(8,128)S(1)} %collective-permute-done.2), channel_id=1, source_target_pairs={{0,32},{32,64},{64,96},{96,128},{128,160},{160,192},{192,224},{224... | collective-permute-start | bytes 589832 | tf_op jit(solution)/shard_map/ppermute | solution.py:82
  37.7 3.1 %collective-permute-start.6 = (f32[8,16,384]{2,1,0:T(8,128)S(1)}, f32[8,16,384]{2,1,0:T(8,128)S(1)}, u32[]{:S(2)}, u32[]{:S(2)}) collective-permute-start(f32[8,16,384]{2,1,0:T(8,128)S(1)} %collective-permute-done.2), channel_id=1, source_target_pairs={{0,64},{32,96},{64,128},{96,160},{128,192},{160,224},{192,0},{224,... | collective-permute-start | bytes 589832 | tf_op jit(solution)/shard_map/ppermute | solution.py:82
  40.8 0.0 collective-permute-done.3
  40.8 4.0 %collective-permute-start.5 = (f32[8,16,384]{2,1,0:T(8,128)S(1)}, f32[8,16,384]{2,1,0:T(8,128)S(1)}, u32[]{:S(2)}, u32[]{:S(2)}) collective-permute-start(f32[8,16,384]{2,1,0:T(8,128)S(1)} %collective-permute-done.3), channel_id=1, source_target_pairs={{0,224},{32,0},{64,32},{96,64},{128,96},{160,128},{192,160},{224,1... | collective-permute-start | bytes 589832 | tf_op jit(solution)/shard_map/ppermute | solution.py:82
  44.8 0.0 collective-permute-done
  44.8 0.7 constant_dynamic-update-slice_fusion.6
  45.5 0.0 collective-permute-done.1
  45.5 0.7 constant_dynamic-update-slice_fusion.5
  46.2 0.7 constant_dynamic-update-slice_fusion.4
  46.9 0.7 constant_dynamic-update-slice_fusion.3
  47.6 0.7 constant_dynamic-update-slice_fusion.2
  48.3 1.3 %collective-permute-done.5 = f32[8,16,384]{2,1,0:T(8,128)S(1)} collective-permute-done((f32[8,16,384]{2,1,0:T(8,128)S(1)}, f32[8,16,384]{2,1,0:T(8,128)S(1)}, u32[]{:S(2)}, u32[]{:S(2)}) %collective-permute-start.5) | collective-permute-done | bytes 196640 | tf_op jit(solution)/shard_map/ppermute | solution.py:82
  49.6 0.7 constant_dynamic-update-slice_fusion.1
  50.3 0.0 collective-permute-done.6
  50.3 0.7 constant_dynamic-update-slice_fusion
  51.0 1.9 %collective-permute-start.7 = (f32[64,16,384]{2,1,0:T(8,128)}, f32[64,16,384]{2,1,0:T(8,128)}, u32[]{:S(2)}, u32[]{:S(2)}) collective-permute-start(f32[64,16,384]{2,1,0:T(8,128)} %constant_dynamic-update-slice_fusion), channel_id=1, source_target_pairs={{0,16},{16,0},{1,17},{17,1},{2,18},{18,2},{3,19},{19,3},{4,20},{20... | collective-permute-start | bytes 4718600 | tf_op jit(solution)/shard_map/ppermute | solution.py:102
  52.9 0.6 dynamic_slice.3
  54.2 0.1 pad_add_fusion.place
  54.2 2.4 %collective-permute-done.7 = f32[64,16,384]{2,1,0:T(8,128)} collective-permute-done((f32[64,16,384]{2,1,0:T(8,128)}, f32[64,16,384]{2,1,0:T(8,128)}, u32[]{:S(2)}, u32[]{:S(2)}) %collective-permute-start.7) | collective-permute-done | bytes 1572896 | tf_op jit(solution)/shard_map/ppermute | solution.py:102
  56.6 5.5 %shard_map.55 = f32[512,512]{1,0:T(8,128)S(1)} custom-call(s32[10]{0:T(128)S(1)} %pad_add_fusion.place, f32[2,4,256,384]{3,2,1,0:T(8,128)S(1)} %bitcast.8, f32[8,2,4,16,384]{4,3,2,1,0:T(8,128)} %bitcast.4.v_mine, f32[8,2,4,16,384]{4,3,2,1,0:T(8,128)} %bitcast.5.v_other), custom_call_target="tpu_custom_call" | custom-call | flops 2415919104 | bytes 8388608 | tf_op jit(solution)/shard_map/pallas_call | solution.py:65
  62.1 0.0 copy-start
  62.2 40.8 %all_to_all.16 = f32[32,16,512]{2,1,0:T(8,128)S(1)} all-to-all(f32[32,16,512]{2,1,0:T(8,128)S(1)} %bitcast.9), channel_id=1, replica_groups=mesh['xh'=2,'y'=8,'core'=2,'zq'=4,'z0'=2,'xl'=2] {'zq','xh','z0','xl'}, dimensions={0} | all-to-all | bytes 2097152 | tf_op jit(solution)/shard_map/all_to_all | solution.py:105
  102.9 0.1 reduce_sum.9
  103.0 0.7 add.34
  (8 shorter events, 0.0 us)
Async XLA Ops:
  13.8 42.8 %all-to-all-start = ((f32[8,256,384]{2,1,0:T(8,128)}), f32[8,256,384]{2,1,0:T(8,128)S(1)}, u32[]{:S(2)}, u32[]{:S(2)}) async-start(f32[8,256,384]{2,1,0:T(8,128)} %param.5), calls=%async_computation | async-start | bytes 6291456 | tf_op jit(solution)/shard_map/all_to_all | solution.py:100
  20.0 32.9 %copy-start.1 = (s32[8]{0:T(128)S(1)}, s32[8]{0:T(128)}, u32[]{:S(2)}) copy-start(s32[8]{0:T(128)} %param.8) | copy-start | bytes 100
  20.0 34.2 %copy-start.2 = (s32[8]{0:T(128)S(1)}, s32[8]{0:T(128)}, u32[]{:S(2)}) copy-start(s32[8]{0:T(128)} %constant.51.clone) | copy-start | bytes 100
  20.0 15.8 %collective-permute-start.2 = (f32[8,16,384]{2,1,0:T(8,128)S(1)}, f32[8,16,384]{2,1,0:T(8,128)S(1)}, u32[]{:S(2)}, u32[]{:S(2)}) collective-permute-start(f32[8,16,384]{2,1,0:T(8,128)S(1)} %all_to_all.15), channel_id=1, source_target_pairs={{0,64},{32,96},{64,128},{96,160},{128,192},{160,224},{192,0},{224,... | collective-permute-start | bytes 589832 | tf_op jit(solution)/shard_map/ppermute | solution.py:82
  22.0 18.8 %collective-permute-start.3 = (f32[8,16,384]{2,1,0:T(8,128)S(1)}, f32[8,16,384]{2,1,0:T(8,128)S(1)}, u32[]{:S(2)}, u32[]{:S(2)}) collective-permute-start(f32[8,16,384]{2,1,0:T(8,128)S(1)} %all_to_all.15), channel_id=1, source_target_pairs={{0,192},{32,224},{64,0},{96,32},{128,64},{160,96},{192,128},{224,1... | collective-permute-start | bytes 589832 | tf_op jit(solution)/shard_map/ppermute | solution.py:82
  28.0 16.8 %collective-permute-start = (f32[8,16,384]{2,1,0:T(8,128)S(1)}, f32[8,16,384]{2,1,0:T(8,128)S(1)}, u32[]{:S(2)}, u32[]{:S(2)}) collective-permute-start(f32[8,16,384]{2,1,0:T(8,128)S(1)} %all_to_all.15), channel_id=1, source_target_pairs={{0,32},{32,64},{64,96},{96,128},{128,160},{160,192},{192,224},{224... | collective-permute-start | bytes 589832 | tf_op jit(solution)/shard_map/ppermute | solution.py:82
  30.0 15.5 %collective-permute-start.1 = (f32[8,16,384]{2,1,0:T(8,128)S(1)}, f32[8,16,384]{2,1,0:T(8,128)S(1)}, u32[]{:S(2)}, u32[]{:S(2)}) collective-permute-start(f32[8,16,384]{2,1,0:T(8,128)S(1)} %all_to_all.15), channel_id=1, source_target_pairs={{0,224},{32,0},{64,32},{96,64},{128,96},{160,128},{192,160},{224,1... | collective-permute-start | bytes 589832 | tf_op jit(solution)/shard_map/ppermute | solution.py:82
  35.8 11.8 %collective-permute-start.4 = (f32[8,16,384]{2,1,0:T(8,128)S(1)}, f32[8,16,384]{2,1,0:T(8,128)S(1)}, u32[]{:S(2)}, u32[]{:S(2)}) collective-permute-start(f32[8,16,384]{2,1,0:T(8,128)S(1)} %collective-permute-done.2), channel_id=1, source_target_pairs={{0,32},{32,64},{64,96},{96,128},{128,160},{160,192},{192,224},{224... | collective-permute-start | bytes 589832 | tf_op jit(solution)/shard_map/ppermute | solution.py:82
  37.7 12.6 %collective-permute-start.6 = (f32[8,16,384]{2,1,0:T(8,128)S(1)}, f32[8,16,384]{2,1,0:T(8,128)S(1)}, u32[]{:S(2)}, u32[]{:S(2)}) collective-permute-start(f32[8,16,384]{2,1,0:T(8,128)S(1)} %collective-permute-done.2), channel_id=1, source_target_pairs={{0,64},{32,96},{64,128},{96,160},{128,192},{160,224},{192,0},{224,... | collective-permute-start | bytes 589832 | tf_op jit(solution)/shard_map/ppermute | solution.py:82
  40.8 8.8 %collective-permute-start.5 = (f32[8,16,384]{2,1,0:T(8,128)S(1)}, f32[8,16,384]{2,1,0:T(8,128)S(1)}, u32[]{:S(2)}, u32[]{:S(2)}) collective-permute-start(f32[8,16,384]{2,1,0:T(8,128)S(1)} %collective-permute-done.3), channel_id=1, source_target_pairs={{0,224},{32,0},{64,32},{96,64},{128,96},{160,128},{192,160},{224,1... | collective-permute-start | bytes 589832 | tf_op jit(solution)/shard_map/ppermute | solution.py:82
  51.0 5.6 %collective-permute-start.7 = (f32[64,16,384]{2,1,0:T(8,128)}, f32[64,16,384]{2,1,0:T(8,128)}, u32[]{:S(2)}, u32[]{:S(2)}) collective-permute-start(f32[64,16,384]{2,1,0:T(8,128)} %constant_dynamic-update-slice_fusion), channel_id=1, source_target_pairs={{0,16},{16,0},{1,17},{17,1},{2,18},{18,2},{3,19},{19,3},{4,20},{20... | collective-permute-start | bytes 4718600 | tf_op jit(solution)/shard_map/ppermute | solution.py:102
  62.1 40.9 %copy-start = (f32[8,16,512]{2,1,0:T(8,128)S(1)}, f32[8,16,512]{2,1,0:T(8,128)}, u32[]{:S(2)}) copy-start(f32[8,16,512]{2,1,0:T(8,128)} %param.7) | copy-start | bytes 786436

commit v11 on v10

--- a/solution.py
+++ b/solution.py
@@ -12,7 +12,6 @@
 ROWS = 16
 OUTER = 512
 HALF = OUTER // 2
-STEPS = 2
 
 DOT = functools.partial(
     lax.dot_general, dimension_numbers=(((1,), (1,)), ((), ())), preferred_element_type=jnp.float32
@@ -27,53 +26,64 @@
 NEAR = (0, -1, 1, -2, 2, -3, 3, 4)
 
 
-def sums_kernel(place, t_ref, v_mine, v_other, out, th, tl, vh, vl):
+def put(ref, rows, c, halves, which):
+    width = halves[0].shape[1]
+    depth = ref.shape[1] // (3 * width)
+    for i, half in enumerate(which):
+        start = (i * depth + c) * width
+        ref[rows, start : start + width] = halves[half]
+
+
+def sums_kernel(place, t_ref, mine_ref, other_ref, out, ts, vs, v_mine, v_other, sems):
+    copies = [
+        pltpu.make_async_copy(source, held, sems.at[i])
+        for i, (source, held) in enumerate(((mine_ref, v_mine), (other_ref, v_other)))
+    ]
+    for copy in copies:
+        copy.start()
     depth, rows, width = t_ref.shape[1:]
     rows = rows // N_ZQ
-    slots = lax.broadcasted_iota(jnp.int32, (rows, width), 1) + pl.program_id(0) * (depth * width)
+    slots = lax.broadcasted_iota(jnp.int32, (rows, width), 1)
     for c in range(depth):
         columns = slice(c * width, (c + 1) * width)
         alive = slots + c * width < place[N_Y + 1]
         for zq in range(N_ZQ):
             for xh in range(2):
                 at = (slice((2 * zq + xh) * rows, (2 * zq + xh + 1) * rows), columns)
-                th[at], tl[at] = split(jnp.where(alive, t_ref[xh, c, zq * rows : (zq + 1) * rows], 0.0))
-    for v_ref, core in ((v_mine, place[N_Y]), (v_other, 1 - place[N_Y])):
+                put(ts, at[0], c, split(jnp.where(alive, t_ref[xh, c, zq * rows : (zq + 1) * rows], 0.0)), (0, 1, 0))
+    for copy, v_ref, core in zip(copies, (v_mine, v_other), (place[N_Y], 1 - place[N_Y])):
+        copy.wait()
         for i in range(N_Y):
             for xh in range(2):
                 start = pl.multiple_of(xh * HALF + place[i] * (2 * ROWS) + core * ROWS, ROWS)
                 for c in range(depth):
-                    at = (pl.ds(start, ROWS), slice(c * width, (c + 1) * width))
-                    vh[at], vl[at] = split(v_ref[i, xh, c])
-    sums = DOT(th[...], vh[...]) + (DOT(tl[...], vh[...]) + DOT(th[...], vl[...]))
-
-    @pl.when(pl.program_id(0) == 0)
-    def _():
-        out[...] = sums
-
-    @pl.when(pl.program_id(0) > 0)
-    def _():
-        out[...] += sums
+                    put(vs, pl.ds(start, ROWS), c, split(v_ref[i, xh, c]), (0, 0, 1))
+    out[...] = DOT(ts[...], vs[...])
 
 
 def partial_sums(place, t, mine, other):
     rows, width = t.shape[1:]
-    depth = 4 // STEPS
     t = t.reshape(2, 4, rows, width)
     mine, other = (x.reshape(N_Y, 2, 4, ROWS, width) for x in (mine, other))
-    v_spec = pl.BlockSpec((N_Y, 2, depth, ROWS, width), lambda k, m: (0, 0, k, 0, 0))
+    deep = 12 * width
+    held = pltpu.VMEM(mine.shape, mine.dtype)
     return pl.pallas_call(
         sums_kernel,
         out_shape=jax.ShapeDtypeStruct((2 * rows, OUTER), jnp.float32),
         grid_spec=pltpu.PrefetchScalarGridSpec(
             num_scalar_prefetch=1,
-            grid=(STEPS,),
-            in_specs=[pl.BlockSpec((2, depth, rows, width), lambda k, m: (0, k, 0, 0)), v_spec, v_spec],
+            grid=(1,),
+            in_specs=[pl.BlockSpec(t.shape, lambda k, m: (0, 0, 0, 0))] + [pl.BlockSpec(memory_space=pl.ANY)] * 2,
             out_specs=pl.BlockSpec((2 * rows, OUTER), lambda k, m: (0, 0)),
-            scratch_shapes=[pltpu.VMEM((2 * rows, depth * width), jnp.bfloat16)] * 2
-            + [pltpu.VMEM((OUTER, depth * width), jnp.bfloat16)] * 2,
+            scratch_shapes=[
+                pltpu.VMEM((2 * rows, deep), jnp.bfloat16),
+                pltpu.VMEM((OUTER, deep), jnp.bfloat16),
+                held,
+                held,
+                pltpu.SemaphoreType.DMA((2,)),
+            ],
         ),
-        compiler_params=pltpu.CompilerParams(vmem_limit_bytes=24 << 20),
+        compiler_params=pltpu.CompilerParams(vmem_limit_bytes=32 << 20),
         cost_estimate=pl.CostEstimate(flops=6 * t.size * OUTER, bytes_accessed=8 << 20, transcendentals=0),
     )(place, t, mine, other)
 

time: 105 us -> 105 us (level)
  no operation moved by 1% of the time
where the time goes in v11:
time: 105 us; the launch traced here: 104 us
  blocking collectives  54.6 us (52%)
  starting transfers between devices  32.2 us (31%)
  local copies, waits for them, and re-layouts  6.14 us (6%)
  Pallas kernels  5.28 us (5%)
  waiting for transfers between devices  3.65 us (3%)
    all_to_all x1, blocking collectives, body(): lax.all_to_all(sums.reshape(N_ZQ * N_GROUP, ROWS, OUTER), ('zq',) + GROUP...  40.8 us
    ppermute x7, starting transfers between devices, along_y(): return lax.ppermute(x, 'y', [(i, (i + by) % N_Y) for i in range(N_Y)])  24.1 us
    all_to_all x1, blocking collectives, body(): v = lax.all_to_all(integrals, GROUP, 0, 0, tiled=True)  13.8 us
    all_to_all x1, starting transfers between devices, body(): t = lax.all_to_all(amplitudes, GROUP, 0, 0, tiled=True)  6.18 us
    pallas_call x1, Pallas kernels, partial_sums(): pl.pallas_call(sums_kernel, out_shape=jax.ShapeDtypeStruct((2 * rows, OUT...  5.28 us
    unnamed x13, local copies, waits for them, and re-layouts  4.86 us
    ppermute x1, waiting for transfers between devices, body(): other = lax.ppermute(mine, 'core', [(0, 1), (1, 0)])  2.35 us
  transfers between devices with their start and end apart: 9, of which 2 were waited for; matrix products, arithmetic and copies ran while one was open for 6% of the time, Pallas kernels for 0%

profile of v11, /device:TPU:6, one launch (start us, length us, event | category | flops | bytes accessed | tf_op | source)
XLA Modules:
  0.0 103.5 jit_solution(6199030914848366989)
XLA Ops:
  0.0 13.8 %all_to_all.15 = f32[8,16,384]{2,1,0:T(8,128)S(1)} all-to-all(f32[8,16,384]{2,1,0:T(8,128)} %param.6), channel_id=1, replica_groups=mesh['xh'=2,'y'=8,'core'=2,'zq'=4,'z0'=2,'xl'=2] {'xh','z0','xl'}, dimensions={0} | all-to-all | bytes 393216 | tf_op jit(solution)/shard_map/all_to_all | solution.py:109
  13.8 6.2 %all-to-all-start = ((f32[8,256,384]{2,1,0:T(8,128)}), f32[8,256,384]{2,1,0:T(8,128)S(1)}, u32[]{:S(2)}, u32[]{:S(2)}) async-start(f32[8,256,384]{2,1,0:T(8,128)} %param.5), calls=%async_computation | async-start | bytes 6291456 | tf_op jit(solution)/shard_map/all_to_all | solution.py:110
  20.0 2.1 %collective-permute-start.2 = (f32[8,16,384]{2,1,0:T(8,128)S(1)}, f32[8,16,384]{2,1,0:T(8,128)S(1)}, u32[]{:S(2)}, u32[]{:S(2)}) collective-permute-start(f32[8,16,384]{2,1,0:T(8,128)S(1)} %all_to_all.15), channel_id=1, source_target_pairs={{0,64},{32,96},{64,128},{96,160},{128,192},{160,224},{192,0},{224,... | collective-permute-start | bytes 589832 | tf_op jit(solution)/shard_map/ppermute | solution.py:92
  22.0 6.0 %collective-permute-start.3 = (f32[8,16,384]{2,1,0:T(8,128)S(1)}, f32[8,16,384]{2,1,0:T(8,128)S(1)}, u32[]{:S(2)}, u32[]{:S(2)}) collective-permute-start(f32[8,16,384]{2,1,0:T(8,128)S(1)} %all_to_all.15), channel_id=1, source_target_pairs={{0,192},{32,224},{64,0},{96,32},{128,64},{160,96},{192,128},{224,1... | collective-permute-start | bytes 589832 | tf_op jit(solution)/shard_map/ppermute | solution.py:92
  28.0 1.9 %collective-permute-start = (f32[8,16,384]{2,1,0:T(8,128)S(1)}, f32[8,16,384]{2,1,0:T(8,128)S(1)}, u32[]{:S(2)}, u32[]{:S(2)}) collective-permute-start(f32[8,16,384]{2,1,0:T(8,128)S(1)} %all_to_all.15), channel_id=1, source_target_pairs={{0,32},{32,64},{64,96},{96,128},{128,160},{160,192},{192,224},{224... | collective-permute-start | bytes 589832 | tf_op jit(solution)/shard_map/ppermute | solution.py:92
  30.0 5.1 %collective-permute-start.1 = (f32[8,16,384]{2,1,0:T(8,128)S(1)}, f32[8,16,384]{2,1,0:T(8,128)S(1)}, u32[]{:S(2)}, u32[]{:S(2)}) collective-permute-start(f32[8,16,384]{2,1,0:T(8,128)S(1)} %all_to_all.15), channel_id=1, source_target_pairs={{0,224},{32,0},{64,32},{96,64},{128,96},{160,128},{192,160},{224,1... | collective-permute-start | bytes 589832 | tf_op jit(solution)/shard_map/ppermute | solution.py:92
  35.1 0.7 constant_dynamic-update-slice_fusion.7
  35.8 0.0 collective-permute-done.2
  35.8 1.9 %collective-permute-start.4 = (f32[8,16,384]{2,1,0:T(8,128)S(1)}, f32[8,16,384]{2,1,0:T(8,128)S(1)}, u32[]{:S(2)}, u32[]{:S(2)}) collective-permute-start(f32[8,16,384]{2,1,0:T(8,128)S(1)} %collective-permute-done.2), channel_id=1, source_target_pairs={{0,32},{32,64},{64,96},{96,128},{128,160},{160,192},{192,224},{224... | collective-permute-start | bytes 589832 | tf_op jit(solution)/shard_map/ppermute | solution.py:92
  37.7 3.1 %collective-permute-start.6 = (f32[8,16,384]{2,1,0:T(8,128)S(1)}, f32[8,16,384]{2,1,0:T(8,128)S(1)}, u32[]{:S(2)}, u32[]{:S(2)}) collective-permute-start(f32[8,16,384]{2,1,0:T(8,128)S(1)} %collective-permute-done.2), channel_id=1, source_target_pairs={{0,64},{32,96},{64,128},{96,160},{128,192},{160,224},{192,0},{224,... | collective-permute-start | bytes 589832 | tf_op jit(solution)/shard_map/ppermute | solution.py:92
  40.8 0.0 collective-permute-done.3
  40.8 4.0 %collective-permute-start.5 = (f32[8,16,384]{2,1,0:T(8,128)S(1)}, f32[8,16,384]{2,1,0:T(8,128)S(1)}, u32[]{:S(2)}, u32[]{:S(2)}) collective-permute-start(f32[8,16,384]{2,1,0:T(8,128)S(1)} %collective-permute-done.3), channel_id=1, source_target_pairs={{0,224},{32,0},{64,32},{96,64},{128,96},{160,128},{192,160},{224,1... | collective-permute-start | bytes 589832 | tf_op jit(solution)/shard_map/ppermute | solution.py:92
  44.8 0.7 constant_dynamic-update-slice_fusion.6
  45.5 0.7 constant_dynamic-update-slice_fusion.5
  46.2 0.7 constant_dynamic-update-slice_fusion.4
  46.9 0.7 constant_dynamic-update-slice_fusion.3
  47.6 0.0 collective-permute-done.4
  47.6 0.7 constant_dynamic-update-slice_fusion.2
  48.3 1.3 %collective-permute-done.5 = f32[8,16,384]{2,1,0:T(8,128)S(1)} collective-permute-done((f32[8,16,384]{2,1,0:T(8,128)S(1)}, f32[8,16,384]{2,1,0:T(8,128)S(1)}, u32[]{:S(2)}, u32[]{:S(2)}) %collective-permute-start.5) | collective-permute-done | bytes 196640 | tf_op jit(solution)/shard_map/ppermute | solution.py:92
  49.6 0.7 constant_dynamic-update-slice_fusion.1
  50.3 0.0 collective-permute-done.6
  50.3 0.7 constant_dynamic-update-slice_fusion
  51.0 1.9 %collective-permute-start.7 = (f32[64,16,384]{2,1,0:T(8,128)}, f32[64,16,384]{2,1,0:T(8,128)}, u32[]{:S(2)}, u32[]{:S(2)}) collective-permute-start(f32[64,16,384]{2,1,0:T(8,128)} %constant_dynamic-update-slice_fusion), channel_id=1, source_target_pairs={{0,16},{16,0},{1,17},{17,1},{2,18},{18,2},{3,19},{19,3},{4,20},{20... | collective-permute-start | bytes 4718600 | tf_op jit(solution)/shard_map/ppermute | solution.py:112
  52.9 0.6 dynamic_slice.3
  54.2 0.1 pad_add_fusion.place
  54.2 2.4 %collective-permute-done.7 = f32[64,16,384]{2,1,0:T(8,128)} collective-permute-done((f32[64,16,384]{2,1,0:T(8,128)}, f32[64,16,384]{2,1,0:T(8,128)}, u32[]{:S(2)}, u32[]{:S(2)}) %collective-permute-start.7) | collective-permute-done | bytes 1572896 | tf_op jit(solution)/shard_map/ppermute | solution.py:112
  56.6 0.0 all-to-all-done
  56.6 5.3 %shard_map.55 = f32[512,512]{1,0:T(8,128)S(1)} custom-call(s32[10]{0:T(128)S(1)} %pad_add_fusion.place, f32[2,4,256,384]{3,2,1,0:T(8,128)S(1)} %bitcast.8, f32[8,2,4,16,384]{4,3,2,1,0:T(8,128)} %bitcast.4.mine_ref, f32[8,2,4,16,384]{4,3,2,1,0:T(8,128)} %bitcast.5.other_ref), custom_call_target="tpu_custom_call" | custom-call | flops 2415919104 | bytes 8388608 | tf_op jit(solution)/shard_map/pallas_call | solution.py:70
  61.9 0.0 copy-start
  61.9 40.8 %all_to_all.16 = f32[32,16,512]{2,1,0:T(8,128)S(1)} all-to-all(f32[32,16,512]{2,1,0:T(8,128)S(1)} %bitcast.9), channel_id=1, replica_groups=mesh['xh'=2,'y'=8,'core'=2,'zq'=4,'z0'=2,'xl'=2] {'zq','xh','z0','xl'}, dimensions={0} | all-to-all | bytes 2097152 | tf_op jit(solution)/shard_map/all_to_all | solution.py:115
  102.7 0.1 reduce_sum.9
  102.8 0.7 add.34
  (8 shorter events, 0.0 us)
Async XLA Ops:
  13.8 42.8 %all-to-all-start = ((f32[8,256,384]{2,1,0:T(8,128)}), f32[8,256,384]{2,1,0:T(8,128)S(1)}, u32[]{:S(2)}, u32[]{:S(2)}) async-start(f32[8,256,384]{2,1,0:T(8,128)} %param.5), calls=%async_computation | async-start | bytes 6291456 | tf_op jit(solution)/shard_map/all_to_all | solution.py:110
  20.0 32.9 %copy-start.1 = (s32[8]{0:T(128)S(1)}, s32[8]{0:T(128)}, u32[]{:S(2)}) copy-start(s32[8]{0:T(128)} %param.8) | copy-start | bytes 100
  20.0 34.2 %copy-start.2 = (s32[8]{0:T(128)S(1)}, s32[8]{0:T(128)}, u32[]{:S(2)}) copy-start(s32[8]{0:T(128)} %constant.51.clone) | copy-start | bytes 100
  20.0 15.8 %collective-permute-start.2 = (f32[8,16,384]{2,1,0:T(8,128)S(1)}, f32[8,16,384]{2,1,0:T(8,128)S(1)}, u32[]{:S(2)}, u32[]{:S(2)}) collective-permute-start(f32[8,16,384]{2,1,0:T(8,128)S(1)} %all_to_all.15), channel_id=1, source_target_pairs={{0,64},{32,96},{64,128},{96,160},{128,192},{160,224},{192,0},{224,... | collective-permute-start | bytes 589832 | tf_op jit(solution)/shard_map/ppermute | solution.py:92
  22.0 18.8 %collective-permute-start.3 = (f32[8,16,384]{2,1,0:T(8,128)S(1)}, f32[8,16,384]{2,1,0:T(8,128)S(1)}, u32[]{:S(2)}, u32[]{:S(2)}) collective-permute-start(f32[8,16,384]{2,1,0:T(8,128)S(1)} %all_to_all.15), channel_id=1, source_target_pairs={{0,192},{32,224},{64,0},{96,32},{128,64},{160,96},{192,128},{224,1... | collective-permute-start | bytes 589832 | tf_op jit(solution)/shard_map/ppermute | solution.py:92
  28.0 16.8 %collective-permute-start = (f32[8,16,384]{2,1,0:T(8,128)S(1)}, f32[8,16,384]{2,1,0:T(8,128)S(1)}, u32[]{:S(2)}, u32[]{:S(2)}) collective-permute-start(f32[8,16,384]{2,1,0:T(8,128)S(1)} %all_to_all.15), channel_id=1, source_target_pairs={{0,32},{32,64},{64,96},{96,128},{128,160},{160,192},{192,224},{224... | collective-permute-start | bytes 589832 | tf_op jit(solution)/shard_map/ppermute | solution.py:92
  30.0 15.5 %collective-permute-start.1 = (f32[8,16,384]{2,1,0:T(8,128)S(1)}, f32[8,16,384]{2,1,0:T(8,128)S(1)}, u32[]{:S(2)}, u32[]{:S(2)}) collective-permute-start(f32[8,16,384]{2,1,0:T(8,128)S(1)} %all_to_all.15), channel_id=1, source_target_pairs={{0,224},{32,0},{64,32},{96,64},{128,96},{160,128},{192,160},{224,1... | collective-permute-start | bytes 589832 | tf_op jit(solution)/shard_map/ppermute | solution.py:92
  35.8 11.8 %collective-permute-start.4 = (f32[8,16,384]{2,1,0:T(8,128)S(1)}, f32[8,16,384]{2,1,0:T(8,128)S(1)}, u32[]{:S(2)}, u32[]{:S(2)}) collective-permute-start(f32[8,16,384]{2,1,0:T(8,128)S(1)} %collective-permute-done.2), channel_id=1, source_target_pairs={{0,32},{32,64},{64,96},{96,128},{128,160},{160,192},{192,224},{224... | collective-permute-start | bytes 589832 | tf_op jit(solution)/shard_map/ppermute | solution.py:92
  37.7 12.6 %collective-permute-start.6 = (f32[8,16,384]{2,1,0:T(8,128)S(1)}, f32[8,16,384]{2,1,0:T(8,128)S(1)}, u32[]{:S(2)}, u32[]{:S(2)}) collective-permute-start(f32[8,16,384]{2,1,0:T(8,128)S(1)} %collective-permute-done.2), channel_id=1, source_target_pairs={{0,64},{32,96},{64,128},{96,160},{128,192},{160,224},{192,0},{224,... | collective-permute-start | bytes 589832 | tf_op jit(solution)/shard_map/ppermute | solution.py:92
  40.8 8.8 %collective-permute-start.5 = (f32[8,16,384]{2,1,0:T(8,128)S(1)}, f32[8,16,384]{2,1,0:T(8,128)S(1)}, u32[]{:S(2)}, u32[]{:S(2)}) collective-permute-start(f32[8,16,384]{2,1,0:T(8,128)S(1)} %collective-permute-done.3), channel_id=1, source_target_pairs={{0,224},{32,0},{64,32},{96,64},{128,96},{160,128},{192,160},{224,1... | collective-permute-start | bytes 589832 | tf_op jit(solution)/shard_map/ppermute | solution.py:92
  51.0 5.6 %collective-permute-start.7 = (f32[64,16,384]{2,1,0:T(8,128)}, f32[64,16,384]{2,1,0:T(8,128)}, u32[]{:S(2)}, u32[]{:S(2)}) collective-permute-start(f32[64,16,384]{2,1,0:T(8,128)} %constant_dynamic-update-slice_fusion), channel_id=1, source_target_pairs={{0,16},{16,0},{1,17},{17,1},{2,18},{18,2},{3,19},{19,3},{4,20},{20... | collective-permute-start | bytes 4718600 | tf_op jit(solution)/shard_map/ppermute | solution.py:112
  61.9 40.9 %copy-start = (f32[8,16,512]{2,1,0:T(8,128)S(1)}, f32[8,16,512]{2,1,0:T(8,128)}, u32[]{:S(2)}) copy-start(f32[8,16,512]{2,1,0:T(8,128)} %param.7) | copy-start | bytes 786436

commit v12 on v11

--- a/solution.py
+++ b/solution.py
@@ -72,9 +72,9 @@
         out_shape=jax.ShapeDtypeStruct((2 * rows, OUTER), jnp.float32),
         grid_spec=pltpu.PrefetchScalarGridSpec(
             num_scalar_prefetch=1,
-            grid=(1,),
-            in_specs=[pl.BlockSpec(t.shape, lambda k, m: (0, 0, 0, 0))] + [pl.BlockSpec(memory_space=pl.ANY)] * 2,
-            out_specs=pl.BlockSpec((2 * rows, OUTER), lambda k, m: (0, 0)),
+            grid=(),
+            in_specs=[pl.BlockSpec(memory_space=pltpu.VMEM)] + [pl.BlockSpec(memory_space=pl.ANY)] * 2,
+            out_specs=pl.BlockSpec(memory_space=pltpu.VMEM),
             scratch_shapes=[
                 pltpu.VMEM((2 * rows, deep), jnp.bfloat16),
                 pltpu.VMEM((OUTER, deep), jnp.bfloat16),

time: 105 us -> 105 us (level)
  no operation moved by 1% of the time
where the time goes in v12:
time: 105 us; the launch traced here: 104 us
  blocking collectives  54.6 us (52%)
  starting transfers between devices  32.2 us (31%)
  local copies, waits for them, and re-layouts  6.14 us (6%)
  Pallas kernels  5.28 us (5%)
  waiting for transfers between devices  3.65 us (3%)
    all_to_all x1, blocking collectives, body(): lax.all_to_all(sums.reshape(N_ZQ * N_GROUP, ROWS, OUTER), ('zq',) + GROUP...  40.8 us
    ppermute x7, starting transfers between devices, along_y(): return lax.ppermute(x, 'y', [(i, (i + by) % N_Y) for i in range(N_Y)])  24.1 us
    all_to_all x1, blocking collectives, body(): v = lax.all_to_all(integrals, GROUP, 0, 0, tiled=True)  13.8 us
    all_to_all x1, starting transfers between devices, body(): t = lax.all_to_all(amplitudes, GROUP, 0, 0, tiled=True)  6.18 us
    pallas_call x1, Pallas kernels, partial_sums(): pl.pallas_call(sums_kernel, out_shape=jax.ShapeDtypeStruct((2 * rows, OUT...  5.28 us
    unnamed x13, local copies, waits for them, and re-layouts  4.86 us
    ppermute x1, waiting for transfers between devices, body(): other = lax.ppermute(mine, 'core', [(0, 1), (1, 0)])  2.35 us
  transfers between devices with their start and end apart: 9, of which 2 were waited for; matrix products, arithmetic and copies ran while one was open for 6% of the time, Pallas kernels for 0%

profile of v12, /device:TPU:6, one launch (start us, length us, event | category | flops | bytes accessed | tf_op | source)
XLA Modules:
  0.0 103.5 jit_solution(6199030914848366989)
XLA Ops:
  0.0 13.8 %all_to_all.15 = f32[8,16,384]{2,1,0:T(8,128)S(1)} all-to-all(f32[8,16,384]{2,1,0:T(8,128)} %param.6), channel_id=1, replica_groups=mesh['xh'=2,'y'=8,'core'=2,'zq'=4,'z0'=2,'xl'=2] {'xh','z0','xl'}, dimensions={0} | all-to-all | bytes 393216 | tf_op jit(solution)/shard_map/all_to_all | solution.py:109
  13.8 6.2 %all-to-all-start = ((f32[8,256,384]{2,1,0:T(8,128)}), f32[8,256,384]{2,1,0:T(8,128)S(1)}, u32[]{:S(2)}, u32[]{:S(2)}) async-start(f32[8,256,384]{2,1,0:T(8,128)} %param.5), calls=%async_computation | async-start | bytes 6291456 | tf_op jit(solution)/shard_map/all_to_all | solution.py:110
  20.0 2.1 %collective-permute-start.2 = (f32[8,16,384]{2,1,0:T(8,128)S(1)}, f32[8,16,384]{2,1,0:T(8,128)S(1)}, u32[]{:S(2)}, u32[]{:S(2)}) collective-permute-start(f32[8,16,384]{2,1,0:T(8,128)S(1)} %all_to_all.15), channel_id=1, source_target_pairs={{0,64},{32,96},{64,128},{96,160},{128,192},{160,224},{192,0},{224,... | collective-permute-start | bytes 589832 | tf_op jit(solution)/shard_map/ppermute | solution.py:92
  22.0 6.0 %collective-permute-start.3 = (f32[8,16,384]{2,1,0:T(8,128)S(1)}, f32[8,16,384]{2,1,0:T(8,128)S(1)}, u32[]{:S(2)}, u32[]{:S(2)}) collective-permute-start(f32[8,16,384]{2,1,0:T(8,128)S(1)} %all_to_all.15), channel_id=1, source_target_pairs={{0,192},{32,224},{64,0},{96,32},{128,64},{160,96},{192,128},{224,1... | collective-permute-start | bytes 589832 | tf_op jit(solution)/shard_map/ppermute | solution.py:92
  28.0 1.9 %collective-permute-start = (f32[8,16,384]{2,1,0:T(8,128)S(1)}, f32[8,16,384]{2,1,0:T(8,128)S(1)}, u32[]{:S(2)}, u32[]{:S(2)}) collective-permute-start(f32[8,16,384]{2,1,0:T(8,128)S(1)} %all_to_all.15), channel_id=1, source_target_pairs={{0,32},{32,64},{64,96},{96,128},{128,160},{160,192},{192,224},{224... | collective-permute-start | bytes 589832 | tf_op jit(solution)/shard_map/ppermute | solution.py:92
  30.0 5.1 %collective-permute-start.1 = (f32[8,16,384]{2,1,0:T(8,128)S(1)}, f32[8,16,384]{2,1,0:T(8,128)S(1)}, u32[]{:S(2)}, u32[]{:S(2)}) collective-permute-start(f32[8,16,384]{2,1,0:T(8,128)S(1)} %all_to_all.15), channel_id=1, source_target_pairs={{0,224},{32,0},{64,32},{96,64},{128,96},{160,128},{192,160},{224,1... | collective-permute-start | bytes 589832 | tf_op jit(solution)/shard_map/ppermute | solution.py:92
  35.1 0.7 constant_dynamic-update-slice_fusion.7
  35.8 0.0 collective-permute-done.2
  35.8 1.9 %collective-permute-start.4 = (f32[8,16,384]{2,1,0:T(8,128)S(1)}, f32[8,16,384]{2,1,0:T(8,128)S(1)}, u32[]{:S(2)}, u32[]{:S(2)}) collective-permute-start(f32[8,16,384]{2,1,0:T(8,128)S(1)} %collective-permute-done.2), channel_id=1, source_target_pairs={{0,32},{32,64},{64,96},{96,128},{128,160},{160,192},{192,224},{224... | collective-permute-start | bytes 589832 | tf_op jit(solution)/shard_map/ppermute | solution.py:92
  37.7 3.1 %collective-permute-start.6 = (f32[8,16,384]{2,1,0:T(8,128)S(1)}, f32[8,16,384]{2,1,0:T(8,128)S(1)}, u32[]{:S(2)}, u32[]{:S(2)}) collective-permute-start(f32[8,16,384]{2,1,0:T(8,128)S(1)} %collective-permute-done.2), channel_id=1, source_target_pairs={{0,64},{32,96},{64,128},{96,160},{128,192},{160,224},{192,0},{224,... | collective-permute-start | bytes 589832 | tf_op jit(solution)/shard_map/ppermute | solution.py:92
  40.8 0.0 collective-permute-done.3
  40.8 4.0 %collective-permute-start.5 = (f32[8,16,384]{2,1,0:T(8,128)S(1)}, f32[8,16,384]{2,1,0:T(8,128)S(1)}, u32[]{:S(2)}, u32[]{:S(2)}) collective-permute-start(f32[8,16,384]{2,1,0:T(8,128)S(1)} %collective-permute-done.3), channel_id=1, source_target_pairs={{0,224},{32,0},{64,32},{96,64},{128,96},{160,128},{192,160},{224,1... | collective-permute-start | bytes 589832 | tf_op jit(solution)/shard_map/ppermute | solution.py:92
  44.8 0.7 constant_dynamic-update-slice_fusion.6
  45.5 0.7 constant_dynamic-update-slice_fusion.5
  46.2 0.7 constant_dynamic-update-slice_fusion.4
  46.9 0.7 constant_dynamic-update-slice_fusion.3
  47.6 0.0 collective-permute-done.4
  47.6 0.7 constant_dynamic-update-slice_fusion.2
  48.3 1.3 %collective-permute-done.5 = f32[8,16,384]{2,1,0:T(8,128)S(1)} collective-permute-done((f32[8,16,384]{2,1,0:T(8,128)S(1)}, f32[8,16,384]{2,1,0:T(8,128)S(1)}, u32[]{:S(2)}, u32[]{:S(2)}) %collective-permute-start.5) | collective-permute-done | bytes 196640 | tf_op jit(solution)/shard_map/ppermute | solution.py:92
  49.6 0.7 constant_dynamic-update-slice_fusion.1
  50.3 0.0 collective-permute-done.6
  50.3 0.7 constant_dynamic-update-slice_fusion
  51.0 1.9 %collective-permute-start.7 = (f32[64,16,384]{2,1,0:T(8,128)}, f32[64,16,384]{2,1,0:T(8,128)}, u32[]{:S(2)}, u32[]{:S(2)}) collective-permute-start(f32[64,16,384]{2,1,0:T(8,128)} %constant_dynamic-update-slice_fusion), channel_id=1, source_target_pairs={{0,16},{16,0},{1,17},{17,1},{2,18},{18,2},{3,19},{19,3},{4,20},{20... | collective-permute-start | bytes 4718600 | tf_op jit(solution)/shard_map/ppermute | solution.py:112
  52.9 0.6 dynamic_slice.3
  54.2 0.1 pad_add_fusion.place
  54.2 2.4 %collective-permute-done.7 = f32[64,16,384]{2,1,0:T(8,128)} collective-permute-done((f32[64,16,384]{2,1,0:T(8,128)}, f32[64,16,384]{2,1,0:T(8,128)}, u32[]{:S(2)}, u32[]{:S(2)}) %collective-permute-start.7) | collective-permute-done | bytes 1572896 | tf_op jit(solution)/shard_map/ppermute | solution.py:112
  56.6 0.0 all-to-all-done
  56.6 5.3 %shard_map.55 = f32[512,512]{1,0:T(8,128)S(1)} custom-call(s32[10]{0:T(128)S(1)} %pad_add_fusion.place, f32[2,4,256,384]{3,2,1,0:T(8,128)S(1)} %bitcast.8, f32[8,2,4,16,384]{4,3,2,1,0:T(8,128)} %bitcast.4.mine_ref, f32[8,2,4,16,384]{4,3,2,1,0:T(8,128)} %bitcast.5.other_ref), custom_call_target="tpu_custom_call" | custom-call | flops 2415919104 | bytes 8388608 | tf_op jit(solution)/shard_map/pallas_call | solution.py:70
  61.9 0.0 copy-start
  61.9 40.8 %all_to_all.16 = f32[32,16,512]{2,1,0:T(8,128)S(1)} all-to-all(f32[32,16,512]{2,1,0:T(8,128)S(1)} %bitcast.9), channel_id=1, replica_groups=mesh['xh'=2,'y'=8,'core'=2,'zq'=4,'z0'=2,'xl'=2] {'zq','xh','z0','xl'}, dimensions={0} | all-to-all | bytes 2097152 | tf_op jit(solution)/shard_map/all_to_all | solution.py:115
  102.7 0.1 reduce_sum.9
  102.8 0.7 add.34
  (8 shorter events, 0.0 us)
Async XLA Ops:
  13.8 42.8 %all-to-all-start = ((f32[8,256,384]{2,1,0:T(8,128)}), f32[8,256,384]{2,1,0:T(8,128)S(1)}, u32[]{:S(2)}, u32[]{:S(2)}) async-start(f32[8,256,384]{2,1,0:T(8,128)} %param.5), calls=%async_computation | async-start | bytes 6291456 | tf_op jit(solution)/shard_map/all_to_all | solution.py:110
  20.0 32.9 %copy-start.1 = (s32[8]{0:T(128)S(1)}, s32[8]{0:T(128)}, u32[]{:S(2)}) copy-start(s32[8]{0:T(128)} %param.8) | copy-start | bytes 100
  20.0 34.2 %copy-start.2 = (s32[8]{0:T(128)S(1)}, s32[8]{0:T(128)}, u32[]{:S(2)}) copy-start(s32[8]{0:T(128)} %constant.51.clone) | copy-start | bytes 100
  20.0 15.8 %collective-permute-start.2 = (f32[8,16,384]{2,1,0:T(8,128)S(1)}, f32[8,16,384]{2,1,0:T(8,128)S(1)}, u32[]{:S(2)}, u32[]{:S(2)}) collective-permute-start(f32[8,16,384]{2,1,0:T(8,128)S(1)} %all_to_all.15), channel_id=1, source_target_pairs={{0,64},{32,96},{64,128},{96,160},{128,192},{160,224},{192,0},{224,... | collective-permute-start | bytes 589832 | tf_op jit(solution)/shard_map/ppermute | solution.py:92
  22.0 18.8 %collective-permute-start.3 = (f32[8,16,384]{2,1,0:T(8,128)S(1)}, f32[8,16,384]{2,1,0:T(8,128)S(1)}, u32[]{:S(2)}, u32[]{:S(2)}) collective-permute-start(f32[8,16,384]{2,1,0:T(8,128)S(1)} %all_to_all.15), channel_id=1, source_target_pairs={{0,192},{32,224},{64,0},{96,32},{128,64},{160,96},{192,128},{224,1... | collective-permute-start | bytes 589832 | tf_op jit(solution)/shard_map/ppermute | solution.py:92
  28.0 16.8 %collective-permute-start = (f32[8,16,384]{2,1,0:T(8,128)S(1)}, f32[8,16,384]{2,1,0:T(8,128)S(1)}, u32[]{:S(2)}, u32[]{:S(2)}) collective-permute-start(f32[8,16,384]{2,1,0:T(8,128)S(1)} %all_to_all.15), channel_id=1, source_target_pairs={{0,32},{32,64},{64,96},{96,128},{128,160},{160,192},{192,224},{224... | collective-permute-start | bytes 589832 | tf_op jit(solution)/shard_map/ppermute | solution.py:92
  30.0 15.5 %collective-permute-start.1 = (f32[8,16,384]{2,1,0:T(8,128)S(1)}, f32[8,16,384]{2,1,0:T(8,128)S(1)}, u32[]{:S(2)}, u32[]{:S(2)}) collective-permute-start(f32[8,16,384]{2,1,0:T(8,128)S(1)} %all_to_all.15), channel_id=1, source_target_pairs={{0,224},{32,0},{64,32},{96,64},{128,96},{160,128},{192,160},{224,1... | collective-permute-start | bytes 589832 | tf_op jit(solution)/shard_map/ppermute | solution.py:92
  35.8 11.8 %collective-permute-start.4 = (f32[8,16,384]{2,1,0:T(8,128)S(1)}, f32[8,16,384]{2,1,0:T(8,128)S(1)}, u32[]{:S(2)}, u32[]{:S(2)}) collective-permute-start(f32[8,16,384]{2,1,0:T(8,128)S(1)} %collective-permute-done.2), channel_id=1, source_target_pairs={{0,32},{32,64},{64,96},{96,128},{128,160},{160,192},{192,224},{224... | collective-permute-start | bytes 589832 | tf_op jit(solution)/shard_map/ppermute | solution.py:92
  37.7 12.6 %collective-permute-start.6 = (f32[8,16,384]{2,1,0:T(8,128)S(1)}, f32[8,16,384]{2,1,0:T(8,128)S(1)}, u32[]{:S(2)}, u32[]{:S(2)}) collective-permute-start(f32[8,16,384]{2,1,0:T(8,128)S(1)} %collective-permute-done.2), channel_id=1, source_target_pairs={{0,64},{32,96},{64,128},{96,160},{128,192},{160,224},{192,0},{224,... | collective-permute-start | bytes 589832 | tf_op jit(solution)/shard_map/ppermute | solution.py:92
  40.8 8.8 %collective-permute-start.5 = (f32[8,16,384]{2,1,0:T(8,128)S(1)}, f32[8,16,384]{2,1,0:T(8,128)S(1)}, u32[]{:S(2)}, u32[]{:S(2)}) collective-permute-start(f32[8,16,384]{2,1,0:T(8,128)S(1)} %collective-permute-done.3), channel_id=1, source_target_pairs={{0,224},{32,0},{64,32},{96,64},{128,96},{160,128},{192,160},{224,1... | collective-permute-start | bytes 589832 | tf_op jit(solution)/shard_map/ppermute | solution.py:92
  51.0 5.6 %collective-permute-start.7 = (f32[64,16,384]{2,1,0:T(8,128)}, f32[64,16,384]{2,1,0:T(8,128)}, u32[]{:S(2)}, u32[]{:S(2)}) collective-permute-start(f32[64,16,384]{2,1,0:T(8,128)} %constant_dynamic-update-slice_fusion), channel_id=1, source_target_pairs={{0,16},{16,0},{1,17},{17,1},{2,18},{18,2},{3,19},{19,3},{4,20},{20... | collective-permute-start | bytes 4718600 | tf_op jit(solution)/shard_map/ppermute | solution.py:112
  61.9 40.9 %copy-start = (f32[8,16,512]{2,1,0:T(8,128)S(1)}, f32[8,16,512]{2,1,0:T(8,128)}, u32[]{:S(2)}) copy-start(f32[8,16,512]{2,1,0:T(8,128)} %param.7) | copy-start | bytes 786436

commit v13 on v12

--- a/solution.py
+++ b/solution.py
@@ -34,7 +34,7 @@
         ref[rows, start : start + width] = halves[half]
 
 
-def sums_kernel(place, t_ref, mine_ref, other_ref, out, ts, vs, v_mine, v_other, sems):
+def sums_kernel(place, t_ref, mine_ref, other_ref, out, ts, ts_late, vs, v_mine, v_other, sems):
     copies = [
         pltpu.make_async_copy(source, held, sems.at[i])
         for i, (source, held) in enumerate(((mine_ref, v_mine), (other_ref, v_other)))
@@ -44,13 +44,17 @@
     depth, rows, width = t_ref.shape[1:]
     rows = rows // N_ZQ
     slots = lax.broadcasted_iota(jnp.int32, (rows, width), 1)
-    for c in range(depth):
-        columns = slice(c * width, (c + 1) * width)
-        alive = slots + c * width < place[N_Y + 1]
-        for zq in range(N_ZQ):
-            for xh in range(2):
-                at = (slice((2 * zq + xh) * rows, (2 * zq + xh + 1) * rows), columns)
-                put(ts, at[0], c, split(jnp.where(alive, t_ref[xh, c, zq * rows : (zq + 1) * rows], 0.0)), (0, 1, 0))
+
+    def fill(ref, first):
+        for c in range(depth):
+            alive = slots + c * width < place[N_Y + 1]
+            for i in range(N_ZQ // 2):
+                for xh in range(2):
+                    block = t_ref[xh, c, (first + i) * rows : (first + i + 1) * rows]
+                    at = slice((2 * i + xh) * rows, (2 * i + xh + 1) * rows)
+                    put(ref, at, c, split(jnp.where(alive, block, 0.0)), (0, 1, 0))
+
+    fill(ts, 0)
     for copy, v_ref, core in zip(copies, (v_mine, v_other), (place[N_Y], 1 - place[N_Y])):
         copy.wait()
         for i in range(N_Y):
@@ -58,7 +62,10 @@
                 start = pl.multiple_of(xh * HALF + place[i] * (2 * ROWS) + core * ROWS, ROWS)
                 for c in range(depth):
                     put(vs, pl.ds(start, ROWS), c, split(v_ref[i, xh, c]), (0, 0, 1))
-    out[...] = DOT(ts[...], vs[...])
+    half = out.shape[0] // 2
+    out[:half] = DOT(ts[...], vs[...])
+    fill(ts_late, N_ZQ // 2)
+    out[half:] = DOT(ts_late[...], vs[...])
 
 
 def partial_sums(place, t, mine, other):
@@ -76,7 +83,8 @@
             in_specs=[pl.BlockSpec(memory_space=pltpu.VMEM)] + [pl.BlockSpec(memory_space=pl.ANY)] * 2,
             out_specs=pl.BlockSpec(memory_space=pltpu.VMEM),
             scratch_shapes=[
-                pltpu.VMEM((2 * rows, deep), jnp.bfloat16),
+                pltpu.VMEM((rows, deep), jnp.bfloat16),
+                pltpu.VMEM((rows, deep), jnp.bfloat16),
                 pltpu.VMEM((OUTER, deep), jnp.bfloat16),
                 held,
                 held,

time: 105 us -> 105 us (level)
  no operation moved by 1% of the time
where the time goes in v13:
time: 105 us; the launch traced here: 104 us
  blocking collectives  54.6 us (52%)
  starting transfers between devices  32.2 us (31%)
  local copies, waits for them, and re-layouts  6.14 us (6%)
  Pallas kernels  5.3 us (5%)
  waiting for transfers between devices  3.65 us (3%)
    all_to_all x1, blocking collectives, body(): lax.all_to_all(sums.reshape(N_ZQ * N_GROUP, ROWS, OUTER), ('zq',) + GROUP...  40.8 us
    ppermute x7, starting transfers between devices, along_y(): return lax.ppermute(x, 'y', [(i, (i + by) % N_Y) for i in range(N_Y)])  24.1 us
    all_to_all x1, blocking collectives, body(): v = lax.all_to_all(integrals, GROUP, 0, 0, tiled=True)  13.8 us
    all_to_all x1, starting transfers between devices, body(): t = lax.all_to_all(amplitudes, GROUP, 0, 0, tiled=True)  6.18 us
    pallas_call x1, Pallas kernels, partial_sums(): pl.pallas_call(sums_kernel, out_shape=jax.ShapeDtypeStruct((2 * rows, OUT...  5.3 us
    unnamed x13, local copies, waits for them, and re-layouts  4.86 us
    ppermute x1, waiting for transfers between devices, body(): other = lax.ppermute(mine, 'core', [(0, 1), (1, 0)])  2.35 us
  transfers between devices with their start and end apart: 9, of which 2 were waited for; matrix products, arithmetic and copies ran while one was open for 6% of the time, Pallas kernels for 0%

profile of v13, /device:TPU:6, one launch (start us, length us, event | category | flops | bytes accessed | tf_op | source)
XLA Modules:
  0.0 103.6 jit_solution(972501279332503052)
XLA Ops:
  0.0 13.8 %all_to_all.15 = f32[8,16,384]{2,1,0:T(8,128)S(1)} all-to-all(f32[8,16,384]{2,1,0:T(8,128)} %param.6), channel_id=1, replica_groups=mesh['xh'=2,'y'=8,'core'=2,'zq'=4,'z0'=2,'xl'=2] {'xh','z0','xl'}, dimensions={0} | all-to-all | bytes 393216 | tf_op jit(solution)/shard_map/all_to_all | solution.py:117
  13.8 6.2 %all-to-all-start = ((f32[8,256,384]{2,1,0:T(8,128)}), f32[8,256,384]{2,1,0:T(8,128)S(1)}, u32[]{:S(2)}, u32[]{:S(2)}) async-start(f32[8,256,384]{2,1,0:T(8,128)} %param.5), calls=%async_computation | async-start | bytes 6291456 | tf_op jit(solution)/shard_map/all_to_all | solution.py:118
  20.0 2.1 %collective-permute-start.2 = (f32[8,16,384]{2,1,0:T(8,128)S(1)}, f32[8,16,384]{2,1,0:T(8,128)S(1)}, u32[]{:S(2)}, u32[]{:S(2)}) collective-permute-start(f32[8,16,384]{2,1,0:T(8,128)S(1)} %all_to_all.15), channel_id=1, source_target_pairs={{0,64},{32,96},{64,128},{96,160},{128,192},{160,224},{192,0},{224,... | collective-permute-start | bytes 589832 | tf_op jit(solution)/shard_map/ppermute | solution.py:100
  22.0 6.0 %collective-permute-start.3 = (f32[8,16,384]{2,1,0:T(8,128)S(1)}, f32[8,16,384]{2,1,0:T(8,128)S(1)}, u32[]{:S(2)}, u32[]{:S(2)}) collective-permute-start(f32[8,16,384]{2,1,0:T(8,128)S(1)} %all_to_all.15), channel_id=1, source_target_pairs={{0,192},{32,224},{64,0},{96,32},{128,64},{160,96},{192,128},{224,1... | collective-permute-start | bytes 589832 | tf_op jit(solution)/shard_map/ppermute | solution.py:100
  28.0 1.9 %collective-permute-start = (f32[8,16,384]{2,1,0:T(8,128)S(1)}, f32[8,16,384]{2,1,0:T(8,128)S(1)}, u32[]{:S(2)}, u32[]{:S(2)}) collective-permute-start(f32[8,16,384]{2,1,0:T(8,128)S(1)} %all_to_all.15), channel_id=1, source_target_pairs={{0,32},{32,64},{64,96},{96,128},{128,160},{160,192},{192,224},{224... | collective-permute-start | bytes 589832 | tf_op jit(solution)/shard_map/ppermute | solution.py:100
  30.0 5.1 %collective-permute-start.1 = (f32[8,16,384]{2,1,0:T(8,128)S(1)}, f32[8,16,384]{2,1,0:T(8,128)S(1)}, u32[]{:S(2)}, u32[]{:S(2)}) collective-permute-start(f32[8,16,384]{2,1,0:T(8,128)S(1)} %all_to_all.15), channel_id=1, source_target_pairs={{0,224},{32,0},{64,32},{96,64},{128,96},{160,128},{192,160},{224,1... | collective-permute-start | bytes 589832 | tf_op jit(solution)/shard_map/ppermute | solution.py:100
  35.1 0.7 constant_dynamic-update-slice_fusion.7
  35.8 0.0 collective-permute-done.2
  35.8 1.9 %collective-permute-start.4 = (f32[8,16,384]{2,1,0:T(8,128)S(1)}, f32[8,16,384]{2,1,0:T(8,128)S(1)}, u32[]{:S(2)}, u32[]{:S(2)}) collective-permute-start(f32[8,16,384]{2,1,0:T(8,128)S(1)} %collective-permute-done.2), channel_id=1, source_target_pairs={{0,32},{32,64},{64,96},{96,128},{128,160},{160,192},{192,224},{224... | collective-permute-start | bytes 589832 | tf_op jit(solution)/shard_map/ppermute | solution.py:100
  37.7 3.1 %collective-permute-start.6 = (f32[8,16,384]{2,1,0:T(8,128)S(1)}, f32[8,16,384]{2,1,0:T(8,128)S(1)}, u32[]{:S(2)}, u32[]{:S(2)}) collective-permute-start(f32[8,16,384]{2,1,0:T(8,128)S(1)} %collective-permute-done.2), channel_id=1, source_target_pairs={{0,64},{32,96},{64,128},{96,160},{128,192},{160,224},{192,0},{224,... | collective-permute-start | bytes 589832 | tf_op jit(solution)/shard_map/ppermute | solution.py:100
  40.8 0.0 collective-permute-done.3
  40.8 4.0 %collective-permute-start.5 = (f32[8,16,384]{2,1,0:T(8,128)S(1)}, f32[8,16,384]{2,1,0:T(8,128)S(1)}, u32[]{:S(2)}, u32[]{:S(2)}) collective-permute-start(f32[8,16,384]{2,1,0:T(8,128)S(1)} %collective-permute-done.3), channel_id=1, source_target_pairs={{0,224},{32,0},{64,32},{96,64},{128,96},{160,128},{192,160},{224,1... | collective-permute-start | bytes 589832 | tf_op jit(solution)/shard_map/ppermute | solution.py:100
  44.8 0.0 collective-permute-done
  44.8 0.7 constant_dynamic-update-slice_fusion.6
  45.5 0.0 collective-permute-done.1
  45.5 0.7 constant_dynamic-update-slice_fusion.5
  46.2 0.7 constant_dynamic-update-slice_fusion.4
  46.9 0.7 constant_dynamic-update-slice_fusion.3
  47.6 0.7 constant_dynamic-update-slice_fusion.2
  48.3 1.3 %collective-permute-done.5 = f32[8,16,384]{2,1,0:T(8,128)S(1)} collective-permute-done((f32[8,16,384]{2,1,0:T(8,128)S(1)}, f32[8,16,384]{2,1,0:T(8,128)S(1)}, u32[]{:S(2)}, u32[]{:S(2)}) %collective-permute-start.5) | collective-permute-done | bytes 196640 | tf_op jit(solution)/shard_map/ppermute | solution.py:100
  49.6 0.7 constant_dynamic-update-slice_fusion.1
  50.3 0.0 collective-permute-done.6
  50.3 0.7 constant_dynamic-update-slice_fusion
  51.0 1.9 %collective-permute-start.7 = (f32[64,16,384]{2,1,0:T(8,128)}, f32[64,16,384]{2,1,0:T(8,128)}, u32[]{:S(2)}, u32[]{:S(2)}) collective-permute-start(f32[64,16,384]{2,1,0:T(8,128)} %constant_dynamic-update-slice_fusion), channel_id=1, source_target_pairs={{0,16},{16,0},{1,17},{17,1},{2,18},{18,2},{3,19},{19,3},{4,20},{20... | collective-permute-start | bytes 4718600 | tf_op jit(solution)/shard_map/ppermute | solution.py:120
  52.9 0.6 dynamic_slice.3
  54.2 0.1 pad_add_fusion.place
  54.2 2.4 %collective-permute-done.7 = f32[64,16,384]{2,1,0:T(8,128)} collective-permute-done((f32[64,16,384]{2,1,0:T(8,128)}, f32[64,16,384]{2,1,0:T(8,128)}, u32[]{:S(2)}, u32[]{:S(2)}) %collective-permute-start.7) | collective-permute-done | bytes 1572896 | tf_op jit(solution)/shard_map/ppermute | solution.py:120
  56.6 5.3 %shard_map.55 = f32[512,512]{1,0:T(8,128)S(1)} custom-call(s32[10]{0:T(128)S(1)} %pad_add_fusion.place, f32[2,4,256,384]{3,2,1,0:T(8,128)S(1)} %bitcast.8, f32[8,2,4,16,384]{4,3,2,1,0:T(8,128)} %bitcast.4.mine_ref, f32[8,2,4,16,384]{4,3,2,1,0:T(8,128)} %bitcast.5.other_ref), custom_call_target="tpu_custom_call" | custom-call | flops 2415919104 | bytes 8388608 | tf_op jit(solution)/shard_map/pallas_call | solution.py:77
  61.9 0.0 copy-start
  61.9 40.8 %all_to_all.16 = f32[32,16,512]{2,1,0:T(8,128)S(1)} all-to-all(f32[32,16,512]{2,1,0:T(8,128)S(1)} %bitcast.9), channel_id=1, replica_groups=mesh['xh'=2,'y'=8,'core'=2,'zq'=4,'z0'=2,'xl'=2] {'zq','xh','z0','xl'}, dimensions={0} | all-to-all | bytes 2097152 | tf_op jit(solution)/shard_map/all_to_all | solution.py:123
  102.7 0.1 reduce_sum.9
  102.8 0.7 add.34
  (8 shorter events, 0.0 us)
Async XLA Ops:
  13.8 42.8 %all-to-all-start = ((f32[8,256,384]{2,1,0:T(8,128)}), f32[8,256,384]{2,1,0:T(8,128)S(1)}, u32[]{:S(2)}, u32[]{:S(2)}) async-start(f32[8,256,384]{2,1,0:T(8,128)} %param.5), calls=%async_computation | async-start | bytes 6291456 | tf_op jit(solution)/shard_map/all_to_all | solution.py:118
  20.0 32.9 %copy-start.1 = (s32[8]{0:T(128)S(1)}, s32[8]{0:T(128)}, u32[]{:S(2)}) copy-start(s32[8]{0:T(128)} %param.8) | copy-start | bytes 100
  20.0 34.2 %copy-start.2 = (s32[8]{0:T(128)S(1)}, s32[8]{0:T(128)}, u32[]{:S(2)}) copy-start(s32[8]{0:T(128)} %constant.51.clone) | copy-start | bytes 100
  20.0 15.8 %collective-permute-start.2 = (f32[8,16,384]{2,1,0:T(8,128)S(1)}, f32[8,16,384]{2,1,0:T(8,128)S(1)}, u32[]{:S(2)}, u32[]{:S(2)}) collective-permute-start(f32[8,16,384]{2,1,0:T(8,128)S(1)} %all_to_all.15), channel_id=1, source_target_pairs={{0,64},{32,96},{64,128},{96,160},{128,192},{160,224},{192,0},{224,... | collective-permute-start | bytes 589832 | tf_op jit(solution)/shard_map/ppermute | solution.py:100
  22.0 18.8 %collective-permute-start.3 = (f32[8,16,384]{2,1,0:T(8,128)S(1)}, f32[8,16,384]{2,1,0:T(8,128)S(1)}, u32[]{:S(2)}, u32[]{:S(2)}) collective-permute-start(f32[8,16,384]{2,1,0:T(8,128)S(1)} %all_to_all.15), channel_id=1, source_target_pairs={{0,192},{32,224},{64,0},{96,32},{128,64},{160,96},{192,128},{224,1... | collective-permute-start | bytes 589832 | tf_op jit(solution)/shard_map/ppermute | solution.py:100
  28.0 16.8 %collective-permute-start = (f32[8,16,384]{2,1,0:T(8,128)S(1)}, f32[8,16,384]{2,1,0:T(8,128)S(1)}, u32[]{:S(2)}, u32[]{:S(2)}) collective-permute-start(f32[8,16,384]{2,1,0:T(8,128)S(1)} %all_to_all.15), channel_id=1, source_target_pairs={{0,32},{32,64},{64,96},{96,128},{128,160},{160,192},{192,224},{224... | collective-permute-start | bytes 589832 | tf_op jit(solution)/shard_map/ppermute | solution.py:100
  30.0 15.5 %collective-permute-start.1 = (f32[8,16,384]{2,1,0:T(8,128)S(1)}, f32[8,16,384]{2,1,0:T(8,128)S(1)}, u32[]{:S(2)}, u32[]{:S(2)}) collective-permute-start(f32[8,16,384]{2,1,0:T(8,128)S(1)} %all_to_all.15), channel_id=1, source_target_pairs={{0,224},{32,0},{64,32},{96,64},{128,96},{160,128},{192,160},{224,1... | collective-permute-start | bytes 589832 | tf_op jit(solution)/shard_map/ppermute | solution.py:100
  35.8 11.8 %collective-permute-start.4 = (f32[8,16,384]{2,1,0:T(8,128)S(1)}, f32[8,16,384]{2,1,0:T(8,128)S(1)}, u32[]{:S(2)}, u32[]{:S(2)}) collective-permute-start(f32[8,16,384]{2,1,0:T(8,128)S(1)} %collective-permute-done.2), channel_id=1, source_target_pairs={{0,32},{32,64},{64,96},{96,128},{128,160},{160,192},{192,224},{224... | collective-permute-start | bytes 589832 | tf_op jit(solution)/shard_map/ppermute | solution.py:100
  37.7 12.6 %collective-permute-start.6 = (f32[8,16,384]{2,1,0:T(8,128)S(1)}, f32[8,16,384]{2,1,0:T(8,128)S(1)}, u32[]{:S(2)}, u32[]{:S(2)}) collective-permute-start(f32[8,16,384]{2,1,0:T(8,128)S(1)} %collective-permute-done.2), channel_id=1, source_target_pairs={{0,64},{32,96},{64,128},{96,160},{128,192},{160,224},{192,0},{224,... | collective-permute-start | bytes 589832 | tf_op jit(solution)/shard_map/ppermute | solution.py:100
  40.8 8.8 %collective-permute-start.5 = (f32[8,16,384]{2,1,0:T(8,128)S(1)}, f32[8,16,384]{2,1,0:T(8,128)S(1)}, u32[]{:S(2)}, u32[]{:S(2)}) collective-permute-start(f32[8,16,384]{2,1,0:T(8,128)S(1)} %collective-permute-done.3), channel_id=1, source_target_pairs={{0,224},{32,0},{64,32},{96,64},{128,96},{160,128},{192,160},{224,1... | collective-permute-start | bytes 589832 | tf_op jit(solution)/shard_map/ppermute | solution.py:100
  51.0 5.6 %collective-permute-start.7 = (f32[64,16,384]{2,1,0:T(8,128)}, f32[64,16,384]{2,1,0:T(8,128)}, u32[]{:S(2)}, u32[]{:S(2)}) collective-permute-start(f32[64,16,384]{2,1,0:T(8,128)} %constant_dynamic-update-slice_fusion), channel_id=1, source_target_pairs={{0,16},{16,0},{1,17},{17,1},{2,18},{18,2},{3,19},{19,3},{4,20},{20... | collective-permute-start | bytes 4718600 | tf_op jit(solution)/shard_map/ppermute | solution.py:120
  61.9 40.9 %copy-start = (f32[8,16,512]{2,1,0:T(8,128)S(1)}, f32[8,16,512]{2,1,0:T(8,128)}, u32[]{:S(2)}) copy-start(f32[8,16,512]{2,1,0:T(8,128)} %param.7) | copy-start | bytes 786436
